TPU v7x, 256 devices: a whole 4x4x8 slice. The times are simulated.
256 devices in a mesh: band: 8 (over y, x_hi), pw: 32 (over x_lo, z, core).
Axes of the slice: x: 4 (x_hi: 2, x_lo: 2; x = x_hi * 2 + x_lo), y: 4, z: 8, core: 2. Of those that a mesh axis runs over, the one named last changes fastest.
Arguments:
- orbitals: bfloat16 [256, 96, 96, 96], P('band', 'pw'), may hold values from -6 to 6
- owners: int32 [4], replicated, may hold values from 0 to 7, as said below
- chosen: int32 [4, 2], replicated, may hold values from 0 to 31
- shell_index: int32 [96, 96, 96], P(None, 'pw'), may hold values from 0 to 127
- shell_kernel: float32 [128], replicated, may hold values from 0.1 to 1
Outputs:
- applied: bfloat16 [256, 96, 96, 96], P('band', 'pw')
Inputs may be any that keep to these rules, and one draw needn't show every extreme that they name: The owners of different rounds are different band groups.
All inputs are finite; a program needn't handle non-finite values.
Results may differ from a plain program's by a relative error of at most 0.012.
Values may be sent and summed in bfloat16 or wider, within the bound.
No kernel may reach another device: no remote copies, remote signals or barrier semaphores. Data moves between devices by JAX's collectives and lax.ppermute only.
A program may use at most 192 MiB of HBM per device.

v0:
```python
import math

import jax
import jax.numpy as jnp
from jax import lax
from jax.sharding import PartitionSpec as P

EXCHANGE_FRACTION = 0.25
FORM_FIRST = "bxyz,kz->bxyk"
FORM_SECOND = "bxyz,ky->bxkz"
FORM_THIRD = "bxyz,kx->bkyz"


def from_root(value, axis, root):
    mine = lax.axis_index(axis) == root
    return lax.psum(jnp.where(mine, value, jnp.zeros_like(value)), axis)


def cas_table(length):
    counter = lax.iota(jnp.int32, length)
    product = counter[:, None] * counter[None, :] % length
    angles = product.astype(jnp.float32) * (2.0 * math.pi / length)
    return ((jnp.cos(angles) + jnp.sin(angles)) / math.sqrt(length)).astype(jnp.bfloat16)


def apply_axis(values, transform, form):
    return jnp.einsum(form, values, transform, preferred_element_type=jnp.float32)


def level_field(shell_index, shell_kernel):
    levels = lax.iota(jnp.int32, shell_kernel.shape[0])

    def one_plane(plane):
        return jnp.sum(jnp.where(plane[..., None] == levels, shell_kernel, 0.0), axis=-1)

    return lax.map(one_plane, shell_index)


def forward_local(pair_data, transform):
    section = apply_axis(pair_data, transform, FORM_FIRST).astype(jnp.bfloat16)
    return apply_axis(section, transform, FORM_SECOND).astype(jnp.bfloat16)


def middle_sections(values, transform, kernel):
    section = (kernel * apply_axis(values, transform, FORM_THIRD)).astype(jnp.bfloat16)
    section = apply_axis(section, transform, FORM_THIRD).astype(jnp.bfloat16)
    return apply_axis(section, transform, FORM_FIRST).astype(jnp.bfloat16)


def broadcast_round(orbitals, owners, chosen, round_number):
    picked_rows = jnp.take(orbitals, chosen[round_number], axis=0)
    return from_root(picked_rows, "band", owners[round_number])


def gather_sources(orbitals, owners, chosen):
    rounds, sources = chosen.shape
    return [
        broadcast_round(orbitals, owners, chosen, round_number) for round_number in range(rounds)
    ]


def on_device(orbitals, owners, chosen, shell_index, shell_kernel):
    length = orbitals.shape[2]
    transform = cas_table(length)
    kernel = level_field(shell_index, shell_kernel)
    round_sources = gather_sources(orbitals, owners, chosen)
    count, planes, width_y, width_z = orbitals.shape
    summed = jnp.zeros(orbitals.shape, jnp.float32)
    for source in round_sources:
        sources = source.shape[0]
        pair_data = (
            source.astype(jnp.float32)[:, None] * orbitals.astype(jnp.float32)[None]
        ).astype(jnp.bfloat16)
        pair_data = pair_data.reshape(sources * count, planes, width_y, width_z)
        forward = forward_local(pair_data, transform)
        finished = middle_sections(
            lax.all_to_all(forward, "pw", split_axis=2, concat_axis=1, tiled=True),
            transform,
            kernel,
        )
        returned = lax.all_to_all(finished, "pw", split_axis=1, concat_axis=2, tiled=True)
        returned = returned.reshape(sources, count, planes, width_y, width_z)
        for source_number in range(sources):
            potential = apply_axis(returned[source_number], transform, FORM_SECOND)
            summed = summed + source[source_number].astype(jnp.float32)[None] * potential
    return (-EXCHANGE_FRACTION * summed).astype(jnp.bfloat16)


def solution(mesh):
    return jax.shard_map(
        on_device,
        mesh=mesh,
        in_specs=(P("band", "pw", None, None), P(), P(), P(None, "pw", None), P()),
        out_specs=P("band", "pw", None, None),
        check_vma=False,
    )
```

profile of v0, /device:TPU:4, one launch (start us, length us, event | category | flops | bytes accessed | tf_op | source)
XLA Modules:
  0.0 1109.2 jit_solution(5976830774765233007)
XLA Ops:
  6.5 1.0 slice_reduce_fusion.3
  7.6 1.5 fusion.367
  11.6 2.2 gather_fusion
  13.9 2.2 gather_fusion.2
  16.1 2.2 gather_fusion.1
  18.4 2.2 gather_fusion.3
  23.6 4.6 convert_element_type.278
  28.2 87.2 %all-reduce.3.cloned.1.call-done = (bf16[2,3,96,96]{3,2,1,0:T(8,128)(2,1)}, bf16[2,3,96,96]{3,2,1,0:T(8,128)(2,1)}, bf16[2,3,96,96]{3,2,1,0:T(8,128)(2,1)}, bf16[2,3,96,96]{3,2,1,0:T(8,128)(2,1)}) async-done(((bf16[2,3,96,96]{3,2,1,0:T(8,128)(2,1)}, bf16[2,3,96,96]{3,2,1,0:T(8,128)(2,1)}, bf16[2,3,96,96]{3,2,1,0:T(8,128)(2,1)}, bf16[2,3,96,96]{3,2,1,0:T(8,128)(2,1)}), (bf16[2,3,96,96]{3,2,1,0:T(8,128)(2,1)}, ...) | async-done | bytes 442384 | tf_op jit(solution)/shard_map/psum | solution.py:16
  116.3 0.9 convert_element_type.300
  117.2 0.9 convert_element_type.289
  118.2 0.9 convert_element_type.277
  119.1 9.3 multiply_convert_fusion.7
  128.4 7.5 convert_bitcast_fusion.2
  135.9 6.3 copy.134
  142.2 9.0 all-to-all-start.2
  151.2 7.4 convert_bitcast_fusion.3
  158.6 6.4 copy.125
  165.0 92.9 %all-to-all-done.2 = bf16[64,3,96,96]{3,0,1,2:T(8,128)(2,1)} async-done(((bf16[64,3,96,96]{3,0,1,2:T(8,128)(2,1)}), bf16[64,3,96,96]{3,0,1,2:T(8,128)(2,1)}, u32[]{:S(2)}, u32[]{:S(2)}) %all-to-all-start.2) | async-done | bytes 3538976 | tf_op jit(solution)/shard_map/all_to_all | solution.py:77
  257.8 6.9 all-to-all-start
  264.7 7.5 convert_bitcast_fusion.1
  272.2 6.3 copy.143
  278.5 92.8 %all-to-all-done = bf16[64,3,96,96]{3,0,1,2:T(8,128)(2,1)} async-done(((bf16[64,3,96,96]{3,0,1,2:T(8,128)(2,1)}), bf16[64,3,96,96]{3,0,1,2:T(8,128)(2,1)}, u32[]{:S(2)}, u32[]{:S(2)}) %all-to-all-start) | async-done | bytes 3538976 | tf_op jit(solution)/shard_map/all_to_all | solution.py:77
  371.3 7.3 all-to-all-start.4
  378.6 7.4 convert_bitcast_fusion
  386.0 6.4 copy.152
  392.4 92.8 %all-to-all-done.4 = bf16[64,3,96,96]{3,0,1,2:T(8,128)(2,1)} async-done(((bf16[64,3,96,96]{3,0,1,2:T(8,128)(2,1)}), bf16[64,3,96,96]{3,0,1,2:T(8,128)(2,1)}, u32[]{:S(2)}, u32[]{:S(2)}) %all-to-all-start.4) | async-done | bytes 3538976 | tf_op jit(solution)/shard_map/all_to_all | solution.py:77
  485.2 6.8 all-to-all-start.6
  492.1 98.6 %while.11 = (s32[]{:T(128)}, f32[96,3,96]{2,0,1:T(8,128)S(1)}, s32[96,3,96]{2,0,1:T(8,128)}, f32[128]{0:T(128)S(1)}, s32[]{:T(128)}, /*index=5*/s32[]{:T(128)}) while((s32[]{:T(128)}, f32[96,3,96]{2,0,1:T(8,128)S(1)}, s32[96,3,96]{2,0,1:T(8,128)}, f32[128]{0:T(128)S(1)}, s32[]{:T(128)}, /*index=5*/s32[]{:T(128)}) %tuple.53), condition=%wide.region_3.5_spmd.clone, body=%wide.region_1.4_spmd.clone.sunk | while | flops 110306 | bytes 12117 | solution.py:36
  590.7 3.4 copy.127
  594.1 10.9 fusion.37
  605.0 8.8 fusion.87
  613.7 6.4 copy.129
  620.2 8.4 all-to-all-start.1
  628.5 3.4 copy.136
  632.0 10.9 fusion.35
  642.9 8.7 fusion.92
  651.5 6.8 copy.138
  658.3 76.9 %all-to-all-done.1 = bf16[64,96,3,96]{3,0,2,1:T(8,128)(2,1)} async-done(((bf16[64,96,3,96]{3,0,2,1:T(8,128)(2,1)}), bf16[64,96,3,96]{3,0,2,1:T(8,128)(2,1)}, u32[]{:S(2)}, u32[]{:S(2)}) %all-to-all-start.1) | async-done | bytes 3538976 | tf_op jit(solution)/shard_map/all_to_all | solution.py:81
  735.2 6.9 all-to-all-start.3
  742.0 3.4 copy.145
  745.5 10.9 fusion.33
  756.4 8.7 fusion.97
  765.1 6.4 copy.147
  771.5 77.2 %all-to-all-done.3 = bf16[64,96,3,96]{3,0,2,1:T(8,128)(2,1)} async-done(((bf16[64,96,3,96]{3,0,2,1:T(8,128)(2,1)}), bf16[64,96,3,96]{3,0,2,1:T(8,128)(2,1)}, u32[]{:S(2)}, u32[]{:S(2)}) %all-to-all-start.3) | async-done | bytes 3538976 | tf_op jit(solution)/shard_map/all_to_all | solution.py:81
  848.7 6.9 all-to-all-start.5
  855.5 3.4 copy.154
  859.0 10.9 fusion.31
  869.9 8.7 fusion.102
  878.6 6.7 copy.156
  885.3 76.9 %all-to-all-done.5 = bf16[64,96,3,96]{3,0,2,1:T(8,128)(2,1)} async-done(((bf16[64,96,3,96]{3,0,2,1:T(8,128)(2,1)}), bf16[64,96,3,96]{3,0,2,1:T(8,128)(2,1)}, u32[]{:S(2)}, u32[]{:S(2)}) %all-to-all-start.5) | async-done | bytes 3538976 | tf_op jit(solution)/shard_map/all_to_all | solution.py:81
  962.2 6.9 all-to-all-start.7
  969.2 3.2 fusion.363
  973.4 3.2 fusion.364
  977.7 3.2 fusion.365
  981.8 4.0 fusion.119
  985.8 4.1 fusion.117
  989.8 4.1 fusion.115
  993.9 4.0 fusion.113
  998.0 4.3 fusion.111
  1002.3 73.4 %all-to-all-done.7 = bf16[64,96,3,96]{3,0,2,1:T(8,128)(2,1)} async-done(((bf16[64,96,3,96]{3,0,2,1:T(8,128)(2,1)}), bf16[64,96,3,96]{3,0,2,1:T(8,128)(2,1)}, u32[]{:S(2)}, u32[]{:S(2)}) %all-to-all-start.7) | async-done | bytes 3538976 | tf_op jit(solution)/shard_map/all_to_all | solution.py:81
  1075.7 3.2 fusion.366
  1079.4 4.1 fusion.109
  1083.9 4.0 fusion.107
  1088.0 14.2 %fusion.16 = bf16[32,3,96,96]{3,2,1,0:T(8,128)(2,1)} fusion(f32[96,32,3,96]{3,0,2,1:T(8,128)} %fusion.107, f32[96,32,3,96]{3,0,2,1:T(8,128)} %fusion.109, f32[96,32,3,96]{3,0,2,1:T(8,128)} %fusion.111, f32[96,32,3,96]{3,0,2,1:T(8,128)} %fusion.113, f32[96,32,3,96]{3,0,2,1:T(8,128)} %fusion.115, f32[96,32,3,96]{3,0,2,1:T(8,128)S(1)} %bitcast.243, ...), kind=kOutput, calls=%fused_computation.28 | convolution fusion | flops 185020416 | bytes 29196288 | tf_op jit(solution)/shard_map/bxyz,ky->bxkz/dot_general | solution.py:27
  (529 shorter events, 103.6 us)
Async XLA Ops:
  6.5 108.8 %all-reduce.3.cloned.1.call-start = ((), (), s32[]{:S(2)}) async-start(), calls=%async_computation.8 | async-start | bytes 1179648 | tf_op jit(solution)/shard_map/psum | solution.py:16
  142.2 115.6 %all-to-all-start.2 = ((bf16[64,3,96,96]{3,0,1,2:T(8,128)(2,1)}), bf16[64,3,96,96]{3,0,1,2:T(8,128)(2,1)}, u32[]{:S(2)}, u32[]{:S(2)}) async-start(bf16[64,3,96,96]{3,0,1,2:T(8,128)(2,1)} %copy.134), calls=%async_computation.2 | async-start | bytes 9437184 | tf_op jit(solution)/shard_map/all_to_all | solution.py:77
  257.8 113.5 %all-to-all-start = ((bf16[64,3,96,96]{3,0,1,2:T(8,128)(2,1)}), bf16[64,3,96,96]{3,0,1,2:T(8,128)(2,1)}, u32[]{:S(2)}, u32[]{:S(2)}) async-start(bf16[64,3,96,96]{3,0,1,2:T(8,128)(2,1)} %copy.125), calls=%async_computation | async-start | bytes 9437184 | tf_op jit(solution)/shard_map/all_to_all | solution.py:77
  371.3 113.9 %all-to-all-start.4 = ((bf16[64,3,96,96]{3,0,1,2:T(8,128)(2,1)}), bf16[64,3,96,96]{3,0,1,2:T(8,128)(2,1)}, u32[]{:S(2)}, u32[]{:S(2)}) async-start(bf16[64,3,96,96]{3,0,1,2:T(8,128)(2,1)} %copy.143), calls=%async_computation.4 | async-start | bytes 9437184 | tf_op jit(solution)/shard_map/all_to_all | solution.py:77
  392.4 99.7 %copy-start.4 = (f32[128]{0:T(128)S(1)}, f32[128]{0:T(128)}, u32[]{:S(2)}) copy-start(f32[128]{0:T(128)} %param.13) | copy-start | bytes 1540
  485.2 135.0 %all-to-all-start.6 = ((bf16[64,3,96,96]{3,0,1,2:T(8,128)(2,1)}), bf16[64,3,96,96]{3,0,1,2:T(8,128)(2,1)}, u32[]{:S(2)}, u32[]{:S(2)}) async-start(bf16[64,3,96,96]{3,0,1,2:T(8,128)(2,1)} %copy.152), calls=%async_computation.6 | async-start | bytes 9437184 | tf_op jit(solution)/shard_map/all_to_all | solution.py:77
  620.2 115.0 %all-to-all-start.1 = ((bf16[64,96,3,96]{3,0,2,1:T(8,128)(2,1)}), bf16[64,96,3,96]{3,0,2,1:T(8,128)(2,1)}, u32[]{:S(2)}, u32[]{:S(2)}) async-start(bf16[64,96,3,96]{3,0,2,1:T(8,128)(2,1)} %copy.129), calls=%async_computation.1 | async-start | bytes 9437184 | tf_op jit(solution)/shard_map/all_to_all | solution.py:81
  735.2 113.5 %all-to-all-start.3 = ((bf16[64,96,3,96]{3,0,2,1:T(8,128)(2,1)}), bf16[64,96,3,96]{3,0,2,1:T(8,128)(2,1)}, u32[]{:S(2)}, u32[]{:S(2)}) async-start(bf16[64,96,3,96]{3,0,2,1:T(8,128)(2,1)} %copy.138), calls=%async_computation.3 | async-start | bytes 9437184 | tf_op jit(solution)/shard_map/all_to_all | solution.py:81
  848.7 113.5 %all-to-all-start.5 = ((bf16[64,96,3,96]{3,0,2,1:T(8,128)(2,1)}), bf16[64,96,3,96]{3,0,2,1:T(8,128)(2,1)}, u32[]{:S(2)}, u32[]{:S(2)}) async-start(bf16[64,96,3,96]{3,0,2,1:T(8,128)(2,1)} %copy.147), calls=%async_computation.5 | async-start | bytes 9437184 | tf_op jit(solution)/shard_map/all_to_all | solution.py:81
  885.3 83.8 %copy-start.3 = (bf16[2,3,96,96]{3,2,1,0:T(8,128)(2,1)S(1)}, bf16[2,3,96,96]{3,2,1,0:T(8,128)(2,1)}, u32[]{:S(2)}) copy-start(bf16[2,3,96,96]{3,2,1,0:T(8,128)(2,1)} %get-tuple-element.72) | copy-start | bytes 331780
  885.3 83.8 %copy-start.2 = (bf16[2,3,96,96]{3,2,1,0:T(8,128)(2,1)S(1)}, bf16[2,3,96,96]{3,2,1,0:T(8,128)(2,1)}, u32[]{:S(2)}) copy-start(bf16[2,3,96,96]{3,2,1,0:T(8,128)(2,1)} %get-tuple-element.73) | copy-start | bytes 331780
  885.3 83.8 %copy-start.1 = (bf16[2,3,96,96]{3,2,1,0:T(8,128)(2,1)S(1)}, bf16[2,3,96,96]{3,2,1,0:T(8,128)(2,1)}, u32[]{:S(2)}) copy-start(bf16[2,3,96,96]{3,2,1,0:T(8,128)(2,1)} %get-tuple-element.74) | copy-start | bytes 331780
  885.3 83.9 %copy-start = (bf16[2,3,96,96]{3,2,1,0:T(8,128)(2,1)S(1)}, bf16[2,3,96,96]{3,2,1,0:T(8,128)(2,1)}, u32[]{:S(2)}) copy-start(bf16[2,3,96,96]{3,2,1,0:T(8,128)(2,1)} %get-tuple-element.75) | copy-start | bytes 331780
  962.2 113.5 %all-to-all-start.7 = ((bf16[64,96,3,96]{3,0,2,1:T(8,128)(2,1)}), bf16[64,96,3,96]{3,0,2,1:T(8,128)(2,1)}, u32[]{:S(2)}, u32[]{:S(2)}) async-start(bf16[64,96,3,96]{3,0,2,1:T(8,128)(2,1)} %copy.156), calls=%async_computation.7 | async-start | bytes 9437184 | tf_op jit(solution)/shard_map/all_to_all | solution.py:81
  1079.3 8.6 slice-start
  1079.3 8.6 slice-start.2
  1083.5 4.5 slice-start.1
  1083.5 4.5 slice-start.3
Sparse Core Ops, SparseCore 0:
  23.8 91.5 all-reduce.2
where the time goes:
time: 1120 us; the launch traced here: 1110 us
  waiting for transfers between devices  670 us (60%)
  local copies, waits for them, and re-layouts  168 us (15%)
  matrix products  151 us (13%)
  starting transfers between devices  58.8 us (5%)
  other arithmetic  42 us (4%)
  between operations  16.5 us (1%)
    all_to_all x4, waiting for transfers between devices, on_device(): lax.all_to_all(finished, 'pw', split_axis=1, concat_axis=2, tiled=True)  304 us
    all_to_all x4, waiting for transfers between devices, on_device(): lax.all_to_all(forward, 'pw', split_axis=2, concat_axis=1, tiled=True)  279 us
    dot_general x20, matrix products, apply_axis(): jnp.einsum(form, values, transform, preferred_element_type=jnp.float32)  151 us
    psum x1, waiting for transfers between devices, from_root(): return lax.psum(jnp.where(mine, value, jnp.zeros_like(value)), axis)  87.2 us
    dynamic_slice x192, local copies, waits for them, and re-layouts, level_field(): return lax.map(one_plane, shell_index)  69.6 us
    all_to_all x4, starting transfers between devices, on_device(): lax.all_to_all(forward, 'pw', split_axis=2, concat_axis=1, tiled=True)  29.9 us
    all_to_all x4, starting transfers between devices, on_device(): lax.all_to_all(finished, 'pw', split_axis=1, concat_axis=2, tiled=True)  28.9 us
    convert_element_type x4, local copies, waits for them, and re-layouts, middle_sections(): return apply_axis(section, transform, FORM_FIRST).astype(jnp.bfloat16)  26.3 us
  transfers between devices with their start and end apart: 9, of which 8 were waited for; matrix products, arithmetic and copies ran while one was open for 26% of the time, Pallas kernels for 0%

commit v1 on v0

v1 whole, which is shorter than its diff:
```python
import math

import jax
import jax.numpy as jnp
from jax import lax
from jax.experimental import pallas as pl
from jax.experimental.pallas import tpu as pltpu
from jax.sharding import PartitionSpec as P

F32 = jnp.float32
BF16 = jnp.bfloat16
EXCHANGE_FRACTION = 0.25
LANES = 128
VMEM_LIMIT = 60 * 2**20
PITCH = 104


def cas_table(length):
    counter = lax.iota(jnp.int32, length)
    product = counter[:, None] * counter[None, :] % length
    angles = product.astype(F32) * (2.0 * math.pi / length)
    return ((jnp.cos(angles) + jnp.sin(angles)) / math.sqrt(length)).astype(BF16)


def double_table(table):
    length = table.shape[0]
    wide = jnp.zeros((2 * LANES, 2 * LANES), table.dtype)
    wide = wide.at[:length, :length].set(table)
    return wide.at[LANES : LANES + length, LANES : LANES + length].set(table)


def dot(a, b):
    return jnp.dot(a, b, preferred_element_type=F32)


def lookup_kernel(level_ref, values_ref, field_ref):
    parts, _, planes, length, width = level_ref.shape

    @pl.loop(0, parts)
    def _(part):
        for plane in range(planes):
            levels = level_ref[part, 0, plane].astype(F32).astype(jnp.int32)
            levels = jnp.concatenate([levels, jnp.zeros((length, LANES - width), jnp.int32)], axis=1)
            values = jnp.broadcast_to(values_ref[...], (length, LANES))
            field_ref[part * planes + plane] = jnp.take_along_axis(values, levels, axis=1)


def kernel_field(gathered, shell_kernel):
    parts, count, planes, length, width = gathered.shape
    return pl.pallas_call(
        lookup_kernel,
        grid=(1,),
        in_specs=[
            pl.BlockSpec((parts, 1, planes, length, width), lambda i: (0, count - 1, 0, 0, 0)),
            pl.BlockSpec((1, LANES), lambda i: (0, 0)),
        ],
        out_specs=pl.BlockSpec((parts * planes, length, LANES), lambda i: (0, 0, 0)),
        out_shape=jax.ShapeDtypeStruct((parts * planes, length, LANES), F32),
        compiler_params=pltpu.CompilerParams(vmem_limit_bytes=VMEM_LIMIT),
        name="kernel_field",
    )(gathered, shell_kernel.reshape(1, LANES))


def solve_kernel(orbital_ref, source_ref, field_ref, table_ref, double_ref, out_ref, first, second, total):
    parts, planes, length, width = orbital_ref.shape
    grid_step = pl.program_id(0)
    group = 8 * planes
    middle_group = 24
    table = table_ref[...]
    halves = (slice(0, LANES), slice(LANES, 2 * LANES))
    blank = jnp.zeros((length, LANES - width), BF16)

    @pl.when(grid_step == 0)
    def _():
        total[...] = jnp.zeros_like(total)

    @pl.loop(0, parts * planes // group)
    def _(step):
        pairs = []
        for k in range(group):
            part, plane = step * (group // planes) + k // planes, k % planes
            orbital = orbital_ref[part, plane].astype(F32)
            for s in range(2):
                pair = source_ref[part, s, plane].astype(F32) * orbital
                pairs += [pair.astype(BF16), blank]
        rows = [jnp.concatenate(pairs[4 * k : 4 * k + 4], axis=1) for k in range(group)]
        along_z = dot(jnp.concatenate(rows, axis=0), double_ref[...]).astype(BF16)
        for k in range(group):
            section = dot(table, along_z[k * length : (k + 1) * length])
            at = pl.multiple_of((step * group + k) * PITCH, 8)
            for s in range(2):
                first[s, pl.ds(at, length), :] = section[:, halves[s]]

    @pl.loop(0, length // middle_group)
    def _(step):
        for k in range(middle_group):
            row = step * middle_group + k
            values = [first[s, pl.ds(row, length, stride=PITCH), :].astype(BF16) for s in range(2)]
            section = dot(table, jnp.concatenate(values, axis=1))
            field = field_ref[row]
            values = [(section[:, halves[s]] * field).astype(BF16) for s in range(2)]
            section = dot(table, jnp.concatenate(values, axis=1))
            at = pl.multiple_of(row * PITCH, 8)
            for s in range(2):
                second[s, pl.ds(at, length), :] = section[:, halves[s]]

    @pl.loop(0, parts * planes // group)
    def _(step):
        sections = []
        for k in range(group):
            row = step * group + k
            values = [second[s, pl.ds(row, length, stride=PITCH), :].astype(BF16) for s in range(2)]
            sections.append(dot(table, jnp.concatenate(values, axis=1)).astype(BF16))
        potential = dot(jnp.concatenate(sections, axis=0), double_ref[...])
        for k in range(group):
            part, plane = step * (group // planes) + k // planes, k % planes
            here = potential[k * length : (k + 1) * length]
            terms = [source_ref[part, s, plane].astype(F32) * here[:, halves[s]][:, :width] for s in range(2)]
            total[step * group + k] += terms[0] + terms[1]

    @pl.when(grid_step == pl.num_programs(0) - 1)
    def _():
        @pl.loop(0, parts)
        def _(part):
            for plane in range(planes):
                out_ref[part, plane] = (-EXCHANGE_FRACTION * total[part * planes + plane]).astype(BF16)


def solve(orbital, gathered, field, table, rounds):
    parts, planes, length, width = orbital.shape
    once = pl.Buffered(1)
    return pl.pallas_call(
        solve_kernel,
        grid=(rounds,),
        in_specs=[
            pl.BlockSpec(orbital.shape, lambda r: (0, 0, 0, 0), pipeline_mode=once),
            pl.BlockSpec((parts, 2, planes, length, width), lambda r: (0, r, 0, 0, 0)),
            pl.BlockSpec(field.shape, lambda r: (0, 0, 0), pipeline_mode=once),
            pl.BlockSpec((length, length), lambda r: (0, 0)),
            pl.BlockSpec((2 * LANES, 2 * LANES), lambda r: (0, 0)),
        ],
        out_specs=pl.BlockSpec(orbital.shape, lambda r: (0, 0, 0, 0)),
        out_shape=jax.ShapeDtypeStruct(orbital.shape, BF16),
        scratch_shapes=[
            pltpu.VMEM((2, length * PITCH, LANES), F32),
            pltpu.VMEM((2, length * PITCH, LANES), F32),
            pltpu.VMEM((length, length, width), F32),
        ],
        compiler_params=pltpu.CompilerParams(vmem_limit_bytes=VMEM_LIMIT),
        name="solve",
    )(orbital, gathered, field, table, double_table(table))


def band_sources(orbitals, owners, chosen):
    bands = lax.axis_size("band")
    me = lax.axis_index("band")
    own_round = jnp.argmax(owners == me)
    own = jnp.take(orbitals, chosen[own_round], axis=0)
    shifted = [own]
    for shift in range(1, bands):
        shifted.append(lax.ppermute(own, "band", [(b, (b + shift) % bands) for b in range(bands)]))
    shifted = jnp.stack(shifted)
    return jnp.take(shifted, (me - owners) % bands, axis=0)


def on_device(orbitals, owners, chosen, shell_index, shell_kernel):
    rounds, sources = chosen.shape
    count, planes, length, width = orbitals.shape
    table = cas_table(length)
    slabs = band_sources(orbitals, owners, chosen).reshape(rounds * sources, planes, length, width)
    levels = jnp.swapaxes(shell_index, 0, 1).astype(BF16)
    slabs = jnp.concatenate([slabs, levels[None]], axis=0)
    gathered = lax.all_gather(slabs, "pw")
    orbital = lax.all_to_all(orbitals, "pw", 0, 0, tiled=True)
    field = kernel_field(gathered, shell_kernel)
    applied = solve(orbital, gathered, field, table, rounds)
    return lax.all_to_all(applied, "pw", 0, 0, tiled=True)


def solution(mesh):
    return jax.shard_map(
        on_device,
        mesh=mesh,
        in_specs=(P("band", "pw", None, None), P(), P(), P(None, "pw", None), P()),
        out_specs=P("band", "pw", None, None),
        check_vma=False,
    )
```

time: 1120 us -> 355 us (0.32)
  waiting for transfers between devices: 670 us -> 179 us
  local copies, waits for them, and re-layouts: 168 us -> 6.77 us
  matrix products: 151 us -> 0 us
  blocking collectives: 0 us -> 65.2 us
  Pallas kernels: 0 us -> 60.4 us
  other arithmetic: 42 us -> 4.47 us
  starting transfers between devices: 58.8 us -> 21.6 us
    all_to_all x8 -> x1, waiting for transfers between devices: 583 us -> 0.01 us  [on_device(): orbital = lax.all_to_all(orbitals, 'pw', 0, 0, tiled=True)]
    all_gather x0 -> x1, waiting for transfers between devices: none -> 161 us  [on_device(): gathered = lax.all_gather(slabs, 'pw')]
    dot_general x20 -> x0, matrix products: 151 us -> none  [apply_axis(): jnp.einsum(form, values, transform, preferred_element_type=jnp.float32)]
    psum x1 -> x0, waiting for transfers between devices: 87.2 us -> none  [from_root(): return lax.psum(jnp.where(mine, value, jnp.zeros_like(value)), axis)]
    dynamic_slice x192 -> x1, local copies, waits for them, and re-layouts: 69.6 us -> 0.19 us  [band_sources(): own = jnp.take(orbitals, chosen[own_round], axis=0)]
    all_to_all x0 -> x1, blocking collectives: none -> 65.2 us  [on_device(): return lax.all_to_all(applied, 'pw', 0, 0, tiled=True)]
    pallas_call x0 -> x2, Pallas kernels: none -> 60.4 us  [the longest x1 51.1 us: solve(): pl.pallas_call(solve_kernel, grid=(rounds,), in_specs=[pl.BlockSpec(orbit...]
    convert_element_type x8 -> x0, local copies, waits for them, and re-layouts: 51.8 us -> none  [the longest x4 26.3 us: middle_sections(): return apply_axis(section, transform, FORM_FIRST).astype(jnp.bfloat16)]
  transfers between devices with their start and end apart: 9 -> 9, of which waited for: 8 -> 4; matrix products, arithmetic and copies ran while one was open for 26% -> 1% of each run, Pallas kernels for 0% -> 3%
where the time goes in v1:
time: 355 us; the launch traced here: 352 us
  waiting for transfers between devices  179 us (50%)
  blocking collectives  65.2 us (18%)
  Pallas kernels  60.4 us (17%)
  starting transfers between devices  21.6 us (6%)
  between operations  15.4 us (4%)
  local copies, waits for them, and re-layouts  6.77 us (2%)
  other arithmetic  4.47 us (1%)
    all_gather x1, waiting for transfers between devices, on_device(): gathered = lax.all_gather(slabs, 'pw')  161 us
    all_to_all x1, blocking collectives, on_device(): return lax.all_to_all(applied, 'pw', 0, 0, tiled=True)  65.2 us
    pallas_call x1, Pallas kernels, solve(): pl.pallas_call(solve_kernel, grid=(rounds,), in_specs=[pl.BlockSpec(orbit...  51.1 us
    ppermute x7, waiting for transfers between devices, band_sources(): lax.ppermute(own, 'band', [(b, (b + shift) % bands) for b in range(bands)])  17.4 us
    ppermute x7, starting transfers between devices, band_sources(): lax.ppermute(own, 'band', [(b, (b + shift) % bands) for b in range(bands)])  12.1 us
    all_to_all x1, starting transfers between devices, on_device(): orbital = lax.all_to_all(orbitals, 'pw', 0, 0, tiled=True)  9.5 us
    pallas_call x1, Pallas kernels, kernel_field(): pl.pallas_call(lookup_kernel, grid=(1,), in_specs=[pl.BlockSpec((parts, 1...  9.24 us
  transfers between devices with their start and end apart: 9, of which 4 were waited for; matrix products, arithmetic and copies ran while one was open for 1% of the time, Pallas kernels for 3%

profile of v1, /device:TPU:4, one launch (start us, length us, event | category | flops | bytes accessed | tf_op | source)
XLA Modules:
  0.0 352.3 jit_solution(17458318642907937228)
XLA Ops:
  6.5 0.0 copy-start
  6.5 0.0 all-gather.3.cloned.1.call-start
  6.5 1.3 compare_reduce_fusion
  9.7 0.0 copy-done
  9.7 0.2 dynamic-slice_reduce_fusion
  9.9 2.2 gather_fusion
  12.2 0.1 broadcast_select_fusion
  12.3 2.3 collective-permute-start.6
  14.6 1.3 collective-permute-start.5
  15.9 3.1 collective-permute-start.4
  19.0 2.9 collective-permute-start.3
  21.9 0.7 collective-permute-start
  22.6 0.7 compare_and_fusion.1
  23.2 0.1 fusion
  23.3 0.1 broadcast_in_dim.36
  23.4 0.1 broadcast_in_dim.37
  23.5 0.9 convert_bitcast_fusion
  24.4 4.1 %collective-permute-done = bf16[2,3,96,96]{3,2,1,0:T(8,128)(2,1)S(1)} collective-permute-done((bf16[2,3,96,96]{3,2,1,0:T(8,128)(2,1)S(1)}, bf16[2,3,96,96]{3,2,1,0:T(8,128)(2,1)S(1)}, u32[]{:S(2)}, u32[]{:S(2)}) %collective-permute-start) | collective-permute-done | bytes 110624 | tf_op jit(solution)/shard_map/ppermute | solution.py:161
  28.5 0.0 collective-permute-start.1
  28.5 6.3 %collective-permute-done.1 = bf16[2,3,96,96]{3,2,1,0:T(8,128)(2,1)S(1)} collective-permute-done((bf16[2,3,96,96]{3,2,1,0:T(8,128)(2,1)S(1)}, bf16[2,3,96,96]{3,2,1,0:T(8,128)(2,1)S(1)}, u32[]{:S(2)}, u32[]{:S(2)}) %collective-permute-start.1) | collective-permute-done | bytes 110624 | tf_op jit(solution)/shard_map/ppermute | solution.py:161
  34.9 1.8 collective-permute-start.2
  36.7 7.0 %collective-permute-done.2 = bf16[2,3,96,96]{3,2,1,0:T(8,128)(2,1)S(1)} collective-permute-done((bf16[2,3,96,96]{3,2,1,0:T(8,128)(2,1)S(1)}, bf16[2,3,96,96]{3,2,1,0:T(8,128)(2,1)S(1)}, u32[]{:S(2)}, u32[]{:S(2)}) %collective-permute-start.2) | collective-permute-done | bytes 110624 | tf_op jit(solution)/shard_map/ppermute | solution.py:161
  43.7 0.0 collective-permute-done.3
  43.7 0.0 collective-permute-done.4
  43.7 0.0 collective-permute-done.5
  43.8 0.0 collective-permute-done.6
  43.8 0.7 gather_fusion.1
  44.5 0.1 bitcast_select_fusion
  44.6 1.0 pad_maximum_fusion
  45.6 0.0 all-gather.3.cloned.1.call-update
  45.6 9.5 %all-to-all-start = ((bf16[32,3,96,96]{3,2,1,0:T(8,128)(2,1)}), bf16[32,3,96,96]{3,2,1,0:T(8,128)(2,1)S(1)}, u32[]{:S(2)}, u32[]{:S(2)}) async-start(bf16[32,3,96,96]{3,2,1,0:T(8,128)(2,1)} %param.9), calls=%async_computation | async-start | bytes 4718592 | tf_op jit(solution)/shard_map/all_to_all | solution.py:174
  55.1 0.2 multiply_convert_fusion.table_ref
  55.3 0.0 copy-start.3
  55.4 0.5 scatter.9.double_ref
  55.9 0.0 copy-start.2
  55.9 161.1 %all-gather.3.cloned.1.call-done = bf16[288,3,96,96]{3,2,1,0:T(8,128)(2,1)} async-done(((bf16[9,3,96,96]{3,2,1,0:T(8,128)(2,1)}), bf16[288,3,96,96]{3,2,1,0:T(8,128)(2,1)}) %all-gather.3.cloned.1.call-update) | async-done | bytes 15925264 | tf_op jit(solution)/shard_map/all_gather | solution.py:173
  217.1 9.2 %kernel_field.1.field_ref = f32[96,96,128]{2,1,0:T(8,128)} custom-call(bf16[32,9,3,96,96]{4,3,2,1,0:T(8,128)(2,1)} %bitcast.30, f32[1,128]{1,0:T(1,128)} %bitcast.32), custom_call_target="tpu_custom_call" | custom-call | tf_op jit(solution)/shard_map/kernel_field/pallas_call | solution.py:50
  226.3 0.0 copy-done.3
  226.3 0.0 copy-done.2
  226.3 0.0 all-to-all-done.orbital_ref
  226.3 0.0 copy-start.1
  226.3 1.4 copy-done.1
  227.7 51.1 %solve.1 = bf16[32,3,96,96]{3,2,1,0:T(8,128)(2,1)} custom-call(bf16[32,3,96,96]{3,2,1,0:T(8,128)(2,1)} %copy-done.1, bf16[32,9,3,96,96]{4,3,2,1,0:T(8,128)(2,1)} %bitcast.31, f32[96,96,128]{2,1,0:T(8,128)} %kernel_field.1.field_ref, bf16[96,96]{1,0:T(8,128)(2,1)} %copy-done.3, bf16[256,256]{1,0:T(8,128)(2,1)} %copy-done.2), custom_call_target="tpu_custom_call" | custom-call | tf_op jit(solution)/shard_map/solve/pallas_call | solution.py:132
  278.8 65.2 %all_to_all.10 = bf16[32,3,96,96]{3,2,1,0:T(8,128)(2,1)S(1)} all-to-all(bf16[32,3,96,96]{3,2,1,0:T(8,128)(2,1)} %solve.1), channel_id=1, replica_groups=mesh['band'=8,'pw'=32] {'pw'}, dimensions={0} | all-to-all | bytes 3538944 | tf_op jit(solution)/shard_map/all_to_all | solution.py:177
  344.1 1.4 copy.15
  (12 shorter events, 0.2 us)
Async XLA Ops:
  6.5 3.2 copy-start
  6.5 210.5 %all-gather.3.cloned.1.call-start = ((), (), s32[]{:S(2)}) async-start(), calls=%async_computation.2 | async-start | bytes 21897216 | tf_op jit(solution)/shard_map/all_gather | solution.py:173
  12.3 31.5 %collective-permute-start.6 = (bf16[2,3,96,96]{3,2,1,0:T(8,128)(2,1)S(1)}, bf16[2,3,96,96]{3,2,1,0:T(8,128)(2,1)S(1)}, u32[]{:S(2)}, u32[]{:S(2)}) collective-permute-start(bf16[2,3,96,96]{3,2,1,0:T(8,128)(2,1)S(1)} %broadcast_select_fusion), channel_id=1, source_target_pairs={{0,224},{32,0},{64,32},{96,64},{128,96},{160,128},{192,160},{224,1... | collective-permute-start | bytes 331784 | tf_op jit(solution)/shard_map/ppermute | solution.py:161
  14.6 29.1 %collective-permute-start.5 = (bf16[2,3,96,96]{3,2,1,0:T(8,128)(2,1)S(1)}, bf16[2,3,96,96]{3,2,1,0:T(8,128)(2,1)S(1)}, u32[]{:S(2)}, u32[]{:S(2)}) collective-permute-start(bf16[2,3,96,96]{3,2,1,0:T(8,128)(2,1)S(1)} %broadcast_select_fusion), channel_id=1, source_target_pairs={{0,192},{32,224},{64,0},{96,32},{128,64},{160,96},{192,128},{224,1... | collective-permute-start | bytes 331784 | tf_op jit(solution)/shard_map/ppermute | solution.py:161
  15.9 27.8 %collective-permute-start.4 = (bf16[2,3,96,96]{3,2,1,0:T(8,128)(2,1)S(1)}, bf16[2,3,96,96]{3,2,1,0:T(8,128)(2,1)S(1)}, u32[]{:S(2)}, u32[]{:S(2)}) collective-permute-start(bf16[2,3,96,96]{3,2,1,0:T(8,128)(2,1)S(1)} %broadcast_select_fusion), channel_id=1, source_target_pairs={{0,160},{32,192},{64,224},{96,0},{128,32},{160,64},{192,96},{224,1... | collective-permute-start | bytes 331784 | tf_op jit(solution)/shard_map/ppermute | solution.py:161
  19.0 24.7 %collective-permute-start.3 = (bf16[2,3,96,96]{3,2,1,0:T(8,128)(2,1)S(1)}, bf16[2,3,96,96]{3,2,1,0:T(8,128)(2,1)S(1)}, u32[]{:S(2)}, u32[]{:S(2)}) collective-permute-start(bf16[2,3,96,96]{3,2,1,0:T(8,128)(2,1)S(1)} %broadcast_select_fusion), channel_id=1, source_target_pairs={{0,128},{32,160},{64,192},{96,224},{128,0},{160,32},{192,64},{224,... | collective-permute-start | bytes 331784 | tf_op jit(solution)/shard_map/ppermute | solution.py:161
  21.9 6.6 %collective-permute-start = (bf16[2,3,96,96]{3,2,1,0:T(8,128)(2,1)S(1)}, bf16[2,3,96,96]{3,2,1,0:T(8,128)(2,1)S(1)}, u32[]{:S(2)}, u32[]{:S(2)}) collective-permute-start(bf16[2,3,96,96]{3,2,1,0:T(8,128)(2,1)S(1)} %broadcast_select_fusion), channel_id=1, source_target_pairs={{0,32},{32,64},{64,96},{96,128},{128,160},{160,192},{192,224},{224... | collective-permute-start | bytes 331784 | tf_op jit(solution)/shard_map/ppermute | solution.py:161
  28.5 6.4 %collective-permute-start.1 = (bf16[2,3,96,96]{3,2,1,0:T(8,128)(2,1)S(1)}, bf16[2,3,96,96]{3,2,1,0:T(8,128)(2,1)S(1)}, u32[]{:S(2)}, u32[]{:S(2)}) collective-permute-start(bf16[2,3,96,96]{3,2,1,0:T(8,128)(2,1)S(1)} %broadcast_select_fusion), channel_id=1, source_target_pairs={{0,64},{32,96},{64,128},{96,160},{128,192},{160,224},{192,0},{224,... | collective-permute-start | bytes 331784 | tf_op jit(solution)/shard_map/ppermute | solution.py:161
  34.9 8.8 %collective-permute-start.2 = (bf16[2,3,96,96]{3,2,1,0:T(8,128)(2,1)S(1)}, bf16[2,3,96,96]{3,2,1,0:T(8,128)(2,1)S(1)}, u32[]{:S(2)}, u32[]{:S(2)}) collective-permute-start(bf16[2,3,96,96]{3,2,1,0:T(8,128)(2,1)S(1)} %broadcast_select_fusion), channel_id=1, source_target_pairs={{0,96},{32,128},{64,160},{96,192},{128,224},{160,0},{192,32},{224,... | collective-permute-start | bytes 331784 | tf_op jit(solution)/shard_map/ppermute | solution.py:161
  45.6 180.7 %all-to-all-start = ((bf16[32,3,96,96]{3,2,1,0:T(8,128)(2,1)}), bf16[32,3,96,96]{3,2,1,0:T(8,128)(2,1)S(1)}, u32[]{:S(2)}, u32[]{:S(2)}) async-start(bf16[32,3,96,96]{3,2,1,0:T(8,128)(2,1)} %param.9), calls=%async_computation | async-start | bytes 4718592 | tf_op jit(solution)/shard_map/all_to_all | solution.py:174
  55.3 171.0 %copy-start.3 = (bf16[96,96]{1,0:T(8,128)(2,1)}, bf16[96,96]{1,0:T(8,128)(2,1)S(1)}, u32[]{:S(2)}) copy-start(bf16[96,96]{1,0:T(8,128)(2,1)S(1)} %multiply_convert_fusion.table_ref) | copy-start | bytes 55300
  55.9 170.4 %copy-start.2 = (bf16[256,256]{1,0:T(8,128)(2,1)}, bf16[256,256]{1,0:T(8,128)(2,1)S(1)}, u32[]{:S(2)}) copy-start(bf16[256,256]{1,0:T(8,128)(2,1)S(1)} %scatter.9.double_ref) | copy-start | bytes 393220
  226.3 1.4 copy-start.1
Sparse Core Ops, SparseCore 0:
  45.7 171.2 all-gather.2

commit v2 on v1

v2 whole, which is shorter than its diff:
```python
import functools
import itertools
import math

import jax
import jax.numpy as jnp
from jax import lax
from jax.experimental import pallas as pl
from jax.experimental.pallas import tpu as pltpu
from jax.sharding import PartitionSpec as P

F32 = jnp.float32
BF16 = jnp.bfloat16
EXCHANGE_FRACTION = 0.25
LANES = 128
ROWS = 16
VMEM_LIMIT = 60 * 2**20
PITCH = 104
BOTH = ("band", "pw")


def cas_table(length):
    counter = lax.iota(jnp.int32, length)
    product = counter[:, None] * counter[None, :] % length
    angles = product.astype(F32) * (2.0 * math.pi / length)
    return ((jnp.cos(angles) + jnp.sin(angles)) / math.sqrt(length)).astype(BF16)


def double_table(table):
    length = table.shape[0]
    wide = jnp.zeros((2 * LANES, 2 * LANES), table.dtype)
    wide = wide.at[:length, :length].set(table)
    return wide.at[LANES : LANES + length, LANES : LANES + length].set(table)


def dot(a, b):
    return jnp.dot(a, b, preferred_element_type=F32)


def pack_tiles(tiles):
    count, width = tiles.shape[-3], tiles.shape[-1]
    free = LANES - width
    kept = count * width // LANES + 1
    thirds = [tiles[..., kept + k // 3, :, (k % 3) * free : (k % 3 + 1) * free] for k in range(3 * (count - kept))]
    thirds += [jnp.zeros_like(thirds[0])] * (kept - len(thirds))
    return jnp.concatenate([tiles[..., :kept, :, :], jnp.stack(thirds, axis=-3)], axis=-1)


def lookup_kernel(level_ref, values_ref, field_ref):
    parts, planes, length, width = level_ref.shape
    values = jnp.broadcast_to(values_ref[...], (length, LANES))
    blank = jnp.zeros((length, LANES - width), jnp.int32)

    @pl.loop(0, parts // 4)
    def _(step):
        for k in range(4):
            part = step * 4 + k
            for plane in range(planes):
                levels = level_ref[part, plane].astype(F32).astype(jnp.int32)
                levels = jnp.concatenate([levels, blank], axis=1)
                field_ref[part * planes + plane] = jnp.take_along_axis(values, levels, axis=1, mode="promise_in_bounds")


def kernel_field(levels, shell_kernel):
    parts, planes, length, width = levels.shape
    return pl.pallas_call(
        lookup_kernel,
        out_shape=jax.ShapeDtypeStruct((parts * planes, length, LANES), F32),
        compiler_params=pltpu.CompilerParams(vmem_limit_bytes=VMEM_LIMIT),
        name="kernel_field",
    )(levels, shell_kernel.reshape(1, LANES))


def unpack_sources(place_ref, pieces, source):
    planes = 3
    length = source.shape[1]
    parts = length // planes
    width = length
    blank = jnp.zeros((length // 2, LANES - width), BF16)
    lows = [pl.multiple_of(h * (length // 2), ROWS) for h in (place_ref[1], 1 - place_ref[1])]
    unroll = 4

    @pl.loop(0, parts // unroll)
    def _(step):
        for k in range(unroll):
            part = step * unroll + k
            for number, ref in enumerate(pieces):
                tiles = [ref[part, t] for t in range(7)]
                spare = [jnp.concatenate([tiles[3 * i + k][:, width:] for k in range(3)], axis=1) for i in range(2)]
                rows = [t[:, :width] for t in tiles] + spare
                for plane in range(planes):
                    here = jnp.concatenate(rows[3 * plane : 3 * plane + 3], axis=0)
                    here = jnp.concatenate([here, blank], axis=1)
                    source[number // 2, part * planes + plane, pl.ds(lows[number % 2], length // 2), :] = here


def solve_kernel(unpack, last, place_ref, near_ref, far_ref, *refs):
    if unpack:
        pieces, refs = refs[:4], refs[4:]
    else:
        source, refs = refs[0], refs[1:]
    field_hbm, table_ref, double_ref = refs[:3]
    refs = refs[3:]
    if last:
        before_hbm, keep_ref, send_ref = refs[:3]
        refs = refs[3:]
    else:
        total_ref, refs = refs[0], refs[1:]
    if unpack:
        source, refs = refs[0], refs[1:]
    first, second, field = refs[:3]
    refs = refs[3:]
    semaphores = refs[-1]
    chips, planes, length, width = near_ref.shape
    chip_group = 4
    table = table_ref[...]
    halves = (slice(0, LANES), slice(LANES, 2 * LANES))
    blank = jnp.zeros((length, LANES - width), BF16)
    field_copy = pltpu.make_async_copy(field_hbm, field, semaphores.at[0])
    field_copy.start()
    if last:
        before = refs[0]
        before_copy = pltpu.make_async_copy(before_hbm, before, semaphores.at[1])
        before_copy.start()
    if unpack:
        unpack_sources(place_ref, pieces, source)
    core = place_ref[0]

    def sections_of(step):
        for k in range(chip_group):
            chip = step * chip_group + k
            for near in (True, False):
                for plane in range(planes):
                    yield chip, near, plane, (2 * chip + (core if near else 1 - core)) * planes + plane

    @pl.loop(0, chips // chip_group)
    def _(step):
        rows = []
        for chip, near, plane, row in sections_of(step):
            orbital = (near_ref if near else far_ref)[chip, plane]
            orbital = jnp.concatenate([orbital, blank], axis=1).astype(F32)
            pair = [(source[s, row].astype(F32) * orbital).astype(BF16) for s in range(2)]
            rows.append(jnp.concatenate(pair, axis=1))
        along_z = dot(jnp.concatenate(rows, axis=0), double_ref[...]).astype(BF16)
        for k, (chip, near, plane, row) in enumerate(sections_of(step)):
            section = dot(table, along_z[k * length : (k + 1) * length])
            at = pl.multiple_of(row * PITCH, 8)
            for s in range(2):
                first[s, pl.ds(at, length), :] = section[:, halves[s]]

    field_copy.wait()
    group = 24

    @pl.loop(0, length // group)
    def _(step):
        for k in range(group):
            row = step * group + k
            values = [first[s, pl.ds(row, length, stride=PITCH), :].astype(BF16) for s in range(2)]
            section = dot(table, jnp.concatenate(values, axis=1))
            values = [(section[:, halves[s]] * field[row]).astype(BF16) for s in range(2)]
            section = dot(table, jnp.concatenate(values, axis=1))
            at = pl.multiple_of(row * PITCH, 8)
            for s in range(2):
                second[s, pl.ds(at, length), :] = section[:, halves[s]]

    if last:
        before_copy.wait()

    @pl.loop(0, chips // chip_group)
    def _(step):
        sections = []
        for chip, near, plane, row in sections_of(step):
            values = [second[s, pl.ds(row, length, stride=PITCH), :].astype(BF16) for s in range(2)]
            sections.append(dot(table, jnp.concatenate(values, axis=1)).astype(BF16))
        potential = dot(jnp.concatenate(sections, axis=0), double_ref[...])
        for k, (chip, near, plane, row) in enumerate(sections_of(step)):
            here = potential[k * length : (k + 1) * length]
            terms = [source[s, row].astype(F32) * here[:, halves[s]] for s in range(2)]
            result = terms[0] + terms[1]
            if last:
                result = (-EXCHANGE_FRACTION * (result + before[row]))[:, :width]
                if near:
                    keep_ref[chip, plane] = result
                else:
                    send_ref[chip, plane] = result.astype(BF16)
            else:
                total_ref[row] = result


def solve(place, orbital, pieces, source, field, table, before):
    near, far = orbital
    length = near.shape[2]
    whole = (length, length, LANES)
    vmem = pl.BlockSpec(memory_space=pltpu.VMEM)
    hbm = pl.BlockSpec(memory_space=pl.ANY)
    unpack, last = source is None, before is not None
    given = list(pieces) if unpack else [source]
    operands = [place, near, far, *given, field, table, double_table(table)]
    in_specs = [pl.BlockSpec(memory_space=pltpu.SMEM), vmem, vmem] + [vmem] * len(given) + [hbm, vmem, vmem]
    scratch = [pltpu.VMEM((2, length * PITCH, LANES), F32)] * 2 + [pltpu.VMEM(whole, F32)]
    if last:
        operands.append(before)
        in_specs.append(hbm)
        scratch.append(pltpu.VMEM(whole, F32))
        out = [jax.ShapeDtypeStruct(near.shape, F32), jax.ShapeDtypeStruct(near.shape, BF16)]
    else:
        out = [jax.ShapeDtypeStruct(whole, F32)]
    if unpack:
        out.append(jax.ShapeDtypeStruct((2,) + whole, BF16))
    return pl.pallas_call(
        functools.partial(solve_kernel, unpack, last),
        in_specs=in_specs,
        out_specs=[vmem] * len(out),
        out_shape=out,
        scratch_shapes=scratch + [pltpu.SemaphoreType.DMA((2,))],
        compiler_params=pltpu.CompilerParams(vmem_limit_bytes=VMEM_LIMIT),
        cost_estimate=pl.CostEstimate(flops=24 * length**4 * 6, bytes_accessed=8 * length**3, transcendentals=0),
        name="solve",
    )(*operands)


def device(y, x, z, core):
    return ((y * 2 + x // 2) * 2 + x % 2) * 16 + z * 2 + core


def shift(value, dy=0, dx=0, dz=0, core=0):
    places = itertools.product(range(4), range(4), range(8), range(2))
    pairs = [
        (device(y, x, z, c), device((y + dy) % 4, (x + dx) % 4, (z + dz) % 8, c ^ core)) for y, x, z, c in places
    ]
    return lax.ppermute(value, BOTH, pairs)


def chip_groups(bands, parts):
    return [[b * parts + 2 * p + c for p in range(parts // 2)] for b in range(bands) for c in range(2)]


def between_chips(value):
    groups = chip_groups(lax.axis_size("band"), lax.axis_size("pw"))
    return lax.all_to_all(value, BOTH, 0, 0, axis_index_groups=groups, tiled=True)


def own_pieces(orbitals, owners, chosen):
    me = lax.axis_index("band")
    planes, length, width = orbitals.shape[1:]
    own_round = jnp.argmax(owners == me)
    own = jnp.take(orbitals, chosen[own_round], axis=0)
    tiles = own.reshape(2, planes, 2, length // 2 // ROWS, ROWS, width)
    tiles = tiles.transpose(2, 0, 1, 3, 4, 5).reshape(2, 2, planes * length // 2 // ROWS, ROWS, width)
    packed = pack_tiles(tiles)
    received = lax.all_to_all(jnp.concatenate([packed] * 4, axis=0), "band", 0, 0, tiled=True)
    return lax.dynamic_index_in_dim(received, owners[me // 2], 0, keepdims=False)


def on_device(orbitals, owners, chosen, shell_index, shell_kernel):
    band, part = lax.axis_index("band"), lax.axis_index("pw")
    count, planes, length, width = orbitals.shape
    table = cas_table(length)
    place = jnp.stack([part % 2, band % 2])
    levels = lax.all_gather(jnp.swapaxes(shell_index, 0, 1).astype(BF16), "pw")
    by_core = orbitals.reshape(count // 2, 2, planes, length, width)

    pieces = own_pieces(orbitals, owners, chosen)
    copies = jnp.broadcast_to(pieces[None], (count // 2,) + pieces.shape).reshape((count,) + pieces.shape[1:])
    own = lax.all_to_all(copies, "pw", 0, 0, tiled=True)
    across = shift(own, dx=2)
    opposite = shift(own, dy=2)
    both = jnp.stack([own, across])
    beside = [shift(both, dy=dy) for dy in (1, 3)]
    pairs = [[own, across, opposite, shift(opposite, dx=2)]]
    pairs.append([beside[k][h] for k in range(2) for h in range(2)])
    second_half, across, opposite = lax.optimization_barrier((by_core[:, 1], across, opposite))
    halves = [by_core[:, 0], second_half]

    field = kernel_field(levels, shell_kernel)
    unpacked = [None, None]
    applied = []
    for which in range(2):
        near = between_chips(halves[which])
        orbital = (near, shift(near, core=1))
        total, *given = solve(place, orbital, pairs[0], unpacked[0], field, table, None)
        if which == 0:
            unpacked[0] = given[0]
        keep, send, *given = solve(place, orbital, pairs[1], unpacked[1], field, table, total)
        if which == 0:
            unpacked[1] = given[0]
            unpacked[0], send = lax.optimization_barrier((unpacked[0], send))
        result = (keep + shift(send, core=1).astype(F32)).astype(BF16)
        applied.append(between_chips(result))
    return jnp.stack(applied, axis=1).reshape(orbitals.shape)


def solution(mesh):
    return jax.shard_map(
        on_device,
        mesh=mesh,
        in_specs=(P("band", "pw", None, None), P(), P(), P(None, "pw", None), P()),
        out_specs=P("band", "pw", None, None),
        check_vma=False,
    )
```

time: 355 us -> 289 us (0.81)
  waiting for transfers between devices: 179 us -> 91.1 us
  blocking collectives: 65.2 us -> 35.4 us
  starting transfers between devices: 21.6 us -> 41.6 us
  Pallas kernels: 60.4 us -> 77 us
  local copies, waits for them, and re-layouts: 6.77 us -> 14.6 us
  other arithmetic: 4.47 us -> 10.6 us
    all_gather x1, waiting for transfers between devices: 161 us -> 0.01 us  [on_device(): levels = lax.all_gather(jnp.swapaxes(shell_index, 0, 1).astype(BF16), 'pw')]
    all_to_all x1 -> x5, waiting for transfers between devices: 0.01 us -> 49.3 us  [the longest x1 25.9 us: on_device(): own = lax.all_to_all(copies, 'pw', 0, 0, tiled=True)]
    all_to_all x1, blocking collectives: 65.2 us -> 35.4 us  [between_chips(): lax.all_to_all(value, BOTH, 0, 0, axis_index_groups=groups, tiled=True)]
    ppermute x7 -> x9, waiting for transfers between devices: 17.4 us -> 41.7 us  [shift(): return lax.ppermute(value, BOTH, pairs)]
    all_to_all x1 -> x5, starting transfers between devices: 9.5 us -> 33.8 us  [the longest x3 16.7 us: between_chips(): lax.all_to_all(value, BOTH, 0, 0, axis_index_groups=groups, tiled=True)]
    pallas_call x2 -> x5, Pallas kernels: 60.4 us -> 77 us  [the longest x4 69.4 us: solve(): pl.pallas_call(functools.partial(solve_kernel, unpack, last), in_specs=in...]
    squeeze x0 -> x3, local copies, waits for them, and re-layouts: none -> 7.85 us  [the longest x2 6.2 us: on_device(): pairs.append([beside[k][h] for k in range(2) for h in range(2)])]
    convert_element_type x0 -> x3, other arithmetic: none -> 5.39 us  [the longest x2 4.75 us: on_device(): result = (keep + shift(send, core=1).astype(F32)).astype(BF16)]
  transfers between devices with their start and end apart: 9 -> 15, of which waited for: 4 -> 8; matrix products, arithmetic and copies ran while one was open for 1% -> 5% of each run, Pallas kernels for 3% -> 27%
where the time goes in v2:
time: 289 us; the launch traced here: 288 us
  waiting for transfers between devices  91.1 us (32%)
  Pallas kernels  77 us (27%)
  starting transfers between devices  41.6 us (14%)
  blocking collectives  35.4 us (12%)
  between operations  17.5 us (6%)
  local copies, waits for them, and re-layouts  14.6 us (5%)
  other arithmetic  10.6 us (4%)
    pallas_call x4, Pallas kernels, solve(): pl.pallas_call(functools.partial(solve_kernel, unpack, last), in_specs=in...  69.4 us
    ppermute x9, waiting for transfers between devices, shift(): return lax.ppermute(value, BOTH, pairs)  41.7 us
    all_to_all x1, blocking collectives, between_chips(): lax.all_to_all(value, BOTH, 0, 0, axis_index_groups=groups, tiled=True)  35.4 us
    all_to_all x1, waiting for transfers between devices, on_device(): own = lax.all_to_all(copies, 'pw', 0, 0, tiled=True)  25.9 us
    all_to_all x3, waiting for transfers between devices, between_chips(): lax.all_to_all(value, BOTH, 0, 0, axis_index_groups=groups, tiled=True)  17.8 us
    all_to_all x3, starting transfers between devices, between_chips(): lax.all_to_all(value, BOTH, 0, 0, axis_index_groups=groups, tiled=True)  16.7 us
    all_to_all x1, starting transfers between devices, on_device(): own = lax.all_to_all(copies, 'pw', 0, 0, tiled=True)  9.49 us
    ppermute x9, starting transfers between devices, shift(): return lax.ppermute(value, BOTH, pairs)  7.75 us
  transfers between devices with their start and end apart: 15, of which 8 were waited for; matrix products, arithmetic and copies ran while one was open for 5% of the time, Pallas kernels for 27%

profile of v2, /device:TPU:4, one launch (start us, length us, event | category | flops | bytes accessed | tf_op | source)
XLA Modules:
  0.0 287.7 jit_solution(1816833021072019197)
XLA Ops:
  6.5 1.4 compare_reduce_fusion
  9.8 0.2 dynamic-slice_reduce_fusion
  10.0 2.2 gather_fusion
  12.3 0.1 select_bitcast_fusion
  12.4 0.1 slice_dynamic-update-slice_fusion.4
  12.5 0.1 slice_dynamic-update-slice_fusion.3
  12.6 0.1 slice_dynamic-update-slice_fusion.1
  12.7 0.1 slice_dynamic-update-slice_fusion
  12.8 1.0 maximum_maximum_fusion
  13.7 7.6 %all-to-all-start.1 = ((bf16[8,2,7,16,128]{4,3,2,1,0:T(8,128)(2,1)}), bf16[8,2,7,16,128]{4,3,2,1,0:T(8,128)(2,1)S(1)}, u32[]{:S(2)}, u32[]{:S(2)}) async-start(bf16[8,2,7,16,128]{4,3,2,1,0:T(8,128)(2,1)} %maximum_maximum_fusion), calls=%async_computation.1 | async-start | bytes 917504 | tf_op jit(solution)/shard_map/all_to_all | solution.py:251
  21.3 0.6 dynamic_slice.11
  23.9 5.6 %all-to-all-done.1 = bf16[8,2,7,16,128]{4,3,2,1,0:T(8,128)(2,1)S(1)} async-done(((bf16[8,2,7,16,128]{4,3,2,1,0:T(8,128)(2,1)}), bf16[8,2,7,16,128]{4,3,2,1,0:T(8,128)(2,1)S(1)}, u32[]{:S(2)}, u32[]{:S(2)}) %all-to-all-start.1) | async-done | bytes 458784 | tf_op jit(solution)/shard_map/all_to_all | solution.py:251
  29.5 1.1 broadcast_in_dim.23
  30.6 9.5 %all-to-all-start.2 = ((bf16[32,7,16,128]{3,2,1,0:T(8,128)(2,1)}), bf16[32,7,16,128]{3,2,1,0:T(8,128)(2,1)S(1)}, u32[]{:S(2)}, u32[]{:S(2)}) async-start(bf16[32,7,16,128]{3,2,1,0:T(8,128)(2,1)} %bitcast.10), calls=%async_computation.2 | async-start | bytes 1835008 | tf_op jit(solution)/shard_map/all_to_all | solution.py:265
  40.1 0.0 all-gather.3.cloned.1.call-start
  40.1 0.6 convert_bitcast_fusion
  40.8 0.0 all-gather.3.cloned.1.call-update
  40.8 0.0 copy-done.3
  40.8 1.7 slice_bitcast_fusion.1
  42.5 25.9 %all-to-all-done.2.refs_0_ = bf16[32,7,16,128]{3,2,1,0:T(8,128)(2,1)S(1)} async-done(((bf16[32,7,16,128]{3,2,1,0:T(8,128)(2,1)}), bf16[32,7,16,128]{3,2,1,0:T(8,128)(2,1)S(1)}, u32[]{:S(2)}, u32[]{:S(2)}) %all-to-all-start.2) | async-done | bytes 917536 | tf_op jit(solution)/shard_map/all_to_all | solution.py:265
  68.3 4.4 %all-to-all-start = ((bf16[16,3,96,96]{3,2,1,0:T(8,128)(2,1)}), bf16[16,3,96,96]{3,2,1,0:T(8,128)(2,1)}, u32[]{:S(2)}, u32[]{:S(2)}) async-start(bf16[16,3,96,96]{3,2,1,0:T(8,128)(2,1)} %get-tuple-element.99), calls=%async_computation | async-start | bytes 2359296 | tf_op jit(solution)/shard_map/all_to_all | solution.py:240
  72.7 0.1 collective-permute-start.4
  72.8 2.6 collective-permute-start.1
  75.4 19.9 %collective-permute-done.4.refs_2_ = bf16[32,7,16,128]{3,2,1,0:T(8,128)(2,1)} collective-permute-done((bf16[32,7,16,128]{3,2,1,0:T(8,128)(2,1)S(1)}, bf16[32,7,16,128]{3,2,1,0:T(8,128)(2,1)}, u32[]{:S(2)}, u32[]{:S(2)}) %collective-permute-start.4) | collective-permute-done | bytes 917536 | tf_op jit(solution)/shard_map/ppermute | solution.py:231
  95.2 2.6 collective-permute-start.5
  97.8 8.5 %all-to-all-done.near_ref = bf16[16,3,96,96]{3,2,1,0:T(8,128)(2,1)} async-done(((bf16[16,3,96,96]{3,2,1,0:T(8,128)(2,1)}), bf16[16,3,96,96]{3,2,1,0:T(8,128)(2,1)}, u32[]{:S(2)}, u32[]{:S(2)}) %all-to-all-start) | async-done | bytes 884768 | tf_op jit(solution)/shard_map/all_to_all | solution.py:240
  106.3 0.0 collective-permute-start
  106.3 9.3 %collective-permute-done.1.refs_1_ = bf16[32,7,16,128]{3,2,1,0:T(8,128)(2,1)} collective-permute-done((bf16[32,7,16,128]{3,2,1,0:T(8,128)(2,1)S(1)}, bf16[32,7,16,128]{3,2,1,0:T(8,128)(2,1)}, u32[]{:S(2)}, u32[]{:S(2)}) %collective-permute-start.1) | collective-permute-done | bytes 917536 | tf_op jit(solution)/shard_map/ppermute | solution.py:231
  115.6 1.4 pad_maximum_fusion.1
  117.0 0.0 copy-done.2
  117.0 0.4 collective-permute-start.3
  117.4 6.4 %all-to-all-start.4 = ((bf16[16,3,96,96]{3,2,1,0:T(8,128)(2,1)}), bf16[16,3,96,96]{3,2,1,0:T(8,128)(2,1)S(1)}, u32[]{:S(2)}, u32[]{:S(2)}) async-start(bf16[16,3,96,96]{3,2,1,0:T(8,128)(2,1)} %get-tuple-element.94), calls=%async_computation.4 | async-start | bytes 2359296 | tf_op jit(solution)/shard_map/all_to_all | solution.py:240
  123.8 1.2 collective-permute-start.2
  125.0 0.2 multiply_convert_fusion.refs_5_.refs_2_
  125.3 0.5 scatter.9.refs_6_.refs_3_
  125.8 0.7 pad_add_fusion.place_ref
  126.5 7.6 %kernel_field.1.refs_4_.refs_1_ = f32[96,96,128]{2,1,0:T(8,128)} custom-call(bf16[32,3,96,96]{3,2,1,0:T(8,128)(2,1)} %bitcast.44, f32[1,128]{1,0:T(1,128)} %bitcast.53), custom_call_target="tpu_custom_call" | custom-call | tf_op jit(solution)/shard_map/kernel_field/pallas_call | solution.py:66
  134.1 0.0 copy-done.7
  134.1 0.0 collective-permute-done.far_ref
  134.1 9.6 %collective-permute-done.5.refs_3_ = bf16[32,7,16,128]{3,2,1,0:T(8,128)(2,1)} collective-permute-done((bf16[32,7,16,128]{3,2,1,0:T(8,128)(2,1)}, bf16[32,7,16,128]{3,2,1,0:T(8,128)(2,1)}, u32[]{:S(2)}, u32[]{:S(2)}) %collective-permute-start.5) | collective-permute-done | bytes 917536 | tf_op jit(solution)/shard_map/ppermute | solution.py:231
  143.6 18.3 %solve.4 = (f32[96,96,128]{2,1,0:T(8,128)}, bf16[2,96,96,128]{3,2,1,0:T(8,128)(2,1)}) custom-call(s32[2]{0:T(128)} %pad_add_fusion.place_ref, bf16[16,3,96,96]{3,2,1,0:T(8,128)(2,1)} %all-to-all-done.near_ref, bf16[16,3,96,96]{3,2,1,0:T(8,128)(2,1)} %collective-permute-done.far_ref, bf16[32,7,16,128]{3,2,1,0:T(8,128)(2,1)} %copy-done.2, ...), custom_call_target="tpu_custom_call" | custom-call | flops 12230590464 | bytes 7077888 | tf_op jit(solution)/shard_map/solve/pallas_call | solution.py:210
  162.0 0.0 all-to-all-done.4.near_ref
  162.0 0.3 collective-permute-start.7
  162.3 0.0 collective-permute-done.3
  162.3 3.2 %slice_bitcast_fusion.2 = (bf16[32,7,16,128]{3,2,1,0:T(8,128)(2,1)}, bf16[32,7,16,128]{3,2,1,0:T(8,128)(2,1)}) fusion(bf16[2,32,7,16,128]{4,3,2,1,0:T(8,128)(2,1)} %collective-permute-done.3), kind=kLoop, calls=%fused_computation.7 | loop fusion | bytes 3670016 | tf_op jit(solution)/shard_map/squeeze | solution.py:271
  165.5 0.0 collective-permute-done.2
  165.5 3.0 %slice_bitcast_fusion.4 = (bf16[32,7,16,128]{3,2,1,0:T(8,128)(2,1)}, bf16[32,7,16,128]{3,2,1,0:T(8,128)(2,1)}) fusion(bf16[2,32,7,16,128]{4,3,2,1,0:T(8,128)(2,1)} %collective-permute-done.2), kind=kLoop, calls=%fused_computation.9 | loop fusion | bytes 3670016 | tf_op jit(solution)/shard_map/squeeze | solution.py:271
  168.5 18.6 %solve.5 = (f32[16,3,96,96]{3,2,1,0:T(8,128)}, bf16[16,3,96,96]{3,2,1,0:T(8,128)(2,1)}, bf16[2,96,96,128]{3,2,1,0:T(8,128)(2,1)}) custom-call(s32[2]{0:T(128)} %pad_add_fusion.place_ref, bf16[16,3,96,96]{3,2,1,0:T(8,128)(2,1)} %all-to-all-done.near_ref, bf16[16,3,96,96]{3,2,1,0:T(8,128)(2,1)} %collective-permute-done.far_ref, ...), custom_call_target="tpu_custom_call" | custom-call | flops 12230590464 | bytes 7077888 | tf_op jit(solution)/shard_map/solve/pallas_call | solution.py:210
  187.1 0.0 copy-start.4
  187.1 0.4 collective-permute-start.6
  187.5 0.0 collective-permute-done.7.far_ref
  187.5 16.6 %solve.6.refs_4_ = f32[96,96,128]{2,1,0:T(8,128)} custom-call(s32[2]{0:T(128)} %pad_add_fusion.place_ref, bf16[16,3,96,96]{3,2,1,0:T(8,128)(2,1)} %copy-done.5, bf16[16,3,96,96]{3,2,1,0:T(8,128)(2,1)} %collective-permute-done.7.far_ref, bf16[2,96,96,128]{3,2,1,0:T(8,128)(2,1)} %get-tuple-element.96.refs_0_, f32[96,96,128]{2,1,0:T(8,128)} %kernel_field.1.refs_4_.refs_1_, ...), custom_call_target="tpu_custom_call" | custom-call | flops 12230590464 | bytes 7077888 | tf_op jit(solution)/shard_map/solve/pallas_call | solution.py:210
  204.1 0.0 collective-permute-done.6
  204.1 2.7 add_convert_fusion.1
  206.8 6.0 %all-to-all-start.3 = ((bf16[16,3,96,96]{3,2,1,0:T(8,128)(2,1)}), bf16[16,3,96,96]{3,2,1,0:T(8,128)(2,1)S(1)}, u32[]{:S(2)}, u32[]{:S(2)}) async-start(bf16[16,3,96,96]{3,2,1,0:T(8,128)(2,1)} %add_convert_fusion.1), calls=%async_computation.3 | async-start | bytes 2359296 | tf_op jit(solution)/shard_map/all_to_all | solution.py:240
  212.8 15.9 %solve.7 = (f32[16,3,96,96]{3,2,1,0:T(8,128)}, bf16[16,3,96,96]{3,2,1,0:T(8,128)(2,1)}) custom-call(s32[2]{0:T(128)} %pad_add_fusion.place_ref, bf16[16,3,96,96]{3,2,1,0:T(8,128)(2,1)} %copy-done.5, bf16[16,3,96,96]{3,2,1,0:T(8,128)(2,1)} %collective-permute-done.7.far_ref, bf16[2,96,96,128]{3,2,1,0:T(8,128)(2,1)} %get-tuple-element.95.refs_0_, ...), custom_call_target="tpu_custom_call" | custom-call | flops 12230590464 | bytes 7077888 | tf_op jit(solution)/shard_map/solve/pallas_call | solution.py:210
  228.7 0.2 collective-permute-start.8
  228.9 3.0 %collective-permute-done.8 = bf16[16,3,96,96]{3,2,1,0:T(8,128)(2,1)S(1)} collective-permute-done((bf16[16,3,96,96]{3,2,1,0:T(8,128)(2,1)}, bf16[16,3,96,96]{3,2,1,0:T(8,128)(2,1)S(1)}, u32[]{:S(2)}, u32[]{:S(2)}) %collective-permute-start.8) | collective-permute-done | bytes 884768 | tf_op jit(solution)/shard_map/ppermute | solution.py:231
  231.9 2.1 add_convert_fusion
  233.9 9.4 %all-to-all-done.3 = bf16[16,3,96,96]{3,2,1,0:T(8,128)(2,1)S(1)} async-done(((bf16[16,3,96,96]{3,2,1,0:T(8,128)(2,1)}), bf16[16,3,96,96]{3,2,1,0:T(8,128)(2,1)S(1)}, u32[]{:S(2)}, u32[]{:S(2)}) %all-to-all-start.3) | async-done | bytes 884768 | tf_op jit(solution)/shard_map/all_to_all | solution.py:240
  243.3 35.4 %all_to_all.30 = bf16[16,3,96,96]{3,2,1,0:T(8,128)(2,1)S(1)} all-to-all(bf16[16,3,96,96]{3,2,1,0:T(8,128)(2,1)S(1)} %add_convert_fusion), channel_id=1, replica_groups={{0,2,4,6,8,10,12,14,16,18,20,22,24,26,28,30},{1,3,5,7,9,11,13,15,17,19,..., dimensions={0} | all-to-all | bytes 1769472 | tf_op jit(solution)/shard_map/all_to_all | solution.py:240
  278.7 0.5 pad_maximum_fusion
  279.2 1.7 copy.16
  280.9 0.0 copy-done.1
  (26 shorter events, 0.1 us)
Async XLA Ops:
  6.5 3.3 %copy-start = (s32[4,2]{0,1:T(2,128)S(1)}, s32[4,2]{0,1:T(2,128)}, u32[]{:S(2)}) copy-start(s32[4,2]{0,1:T(2,128)} %param.23) | copy-start | bytes 100
  6.5 14.8 %copy-start.9 = (s32[4]{0:T(128)S(1)}, s32[4]{0:T(128)}, u32[]{:S(2)}) copy-start(s32[4]{0:T(128)} %param.22) | copy-start | bytes 52
  13.7 26.4 %copy-start.6 = (s32[96,3,96]{2,0,1:T(8,128)S(1)}, s32[96,3,96]{2,0,1:T(8,128)}, u32[]{:S(2)}) copy-start(s32[96,3,96]{2,0,1:T(8,128)} %param.24) | copy-start | bytes 331780
  13.7 15.8 %all-to-all-start.1 = ((bf16[8,2,7,16,128]{4,3,2,1,0:T(8,128)(2,1)}), bf16[8,2,7,16,128]{4,3,2,1,0:T(8,128)(2,1)S(1)}, u32[]{:S(2)}, u32[]{:S(2)}) async-start(bf16[8,2,7,16,128]{4,3,2,1,0:T(8,128)(2,1)} %maximum_maximum_fusion), calls=%async_computation.1 | async-start | bytes 917504 | tf_op jit(solution)/shard_map/all_to_all | solution.py:251
  21.3 19.5 %copy-start.3 = (bf16[32,3,96,96]{3,2,1,0:T(8,128)(2,1)S(1)}, bf16[32,3,96,96]{3,2,1,0:T(8,128)(2,1)}, u32[]{:S(2)}) copy-start(bf16[32,3,96,96]{3,2,1,0:T(8,128)(2,1)} %param.21) | copy-start | bytes 5308420
  30.6 37.8 %all-to-all-start.2 = ((bf16[32,7,16,128]{3,2,1,0:T(8,128)(2,1)}), bf16[32,7,16,128]{3,2,1,0:T(8,128)(2,1)S(1)}, u32[]{:S(2)}, u32[]{:S(2)}) async-start(bf16[32,7,16,128]{3,2,1,0:T(8,128)(2,1)} %bitcast.10), calls=%async_computation.2 | async-start | bytes 1835008 | tf_op jit(solution)/shard_map/all_to_all | solution.py:265
  40.1 86.4 %all-gather.3.cloned.1.call-start = ((), (), s32[]{:S(2)}) async-start(), calls=%async_computation.6 | async-start | bytes 2433024 | tf_op jit(solution)/shard_map/all_gather | solution.py:260
  68.3 48.6 %copy-start.2 = (bf16[32,7,16,128]{3,2,1,0:T(8,128)(2,1)}, bf16[32,7,16,128]{3,2,1,0:T(8,128)(2,1)S(1)}, u32[]{:S(2)}) copy-start(bf16[32,7,16,128]{3,2,1,0:T(8,128)(2,1)S(1)} %all-to-all-done.2.refs_0_) | copy-start | bytes 2752516
  68.3 37.9 %all-to-all-start = ((bf16[16,3,96,96]{3,2,1,0:T(8,128)(2,1)}), bf16[16,3,96,96]{3,2,1,0:T(8,128)(2,1)}, u32[]{:S(2)}, u32[]{:S(2)}) async-start(bf16[16,3,96,96]{3,2,1,0:T(8,128)(2,1)} %get-tuple-element.99), calls=%async_computation | async-start | bytes 2359296 | tf_op jit(solution)/shard_map/all_to_all | solution.py:240
  72.7 22.5 %collective-permute-start.4 = (bf16[32,7,16,128]{3,2,1,0:T(8,128)(2,1)S(1)}, bf16[32,7,16,128]{3,2,1,0:T(8,128)(2,1)}, u32[]{:S(2)}, u32[]{:S(2)}) collective-permute-start(bf16[32,7,16,128]{3,2,1,0:T(8,128)(2,1)S(1)} %all-to-all-done.2.refs_0_), channel_id=1, source_target_pairs={{0,128},{1,129},{2,130},{3,131},{4,132},{5,133},{6,134},{7,135},{8... | collective-permute-start | bytes 2752520 | tf_op jit(solution)/shard_map/ppermute | solution.py:231
  72.8 42.8 %collective-permute-start.1 = (bf16[32,7,16,128]{3,2,1,0:T(8,128)(2,1)S(1)}, bf16[32,7,16,128]{3,2,1,0:T(8,128)(2,1)}, u32[]{:S(2)}, u32[]{:S(2)}) collective-permute-start(bf16[32,7,16,128]{3,2,1,0:T(8,128)(2,1)S(1)} %all-to-all-done.2.refs_0_), channel_id=1, source_target_pairs={{0,32},{1,33},{2,34},{3,35},{4,36},{5,37},{6,38},{7,39},{8,40},{9,... | collective-permute-start | bytes 2752520 | tf_op jit(solution)/shard_map/ppermute | solution.py:231
  95.2 48.4 %collective-permute-start.5 = (bf16[32,7,16,128]{3,2,1,0:T(8,128)(2,1)}, bf16[32,7,16,128]{3,2,1,0:T(8,128)(2,1)}, u32[]{:S(2)}, u32[]{:S(2)}) collective-permute-start(bf16[32,7,16,128]{3,2,1,0:T(8,128)(2,1)} %collective-permute-done.4.refs_2_), channel_id=1, source_target_pairs={{0,32},{1,33},{2,34},{3,35},{4,36},{5,37},{6,38},{7,39},{8,40},{9,... | collective-permute-start | bytes 2752520 | tf_op jit(solution)/shard_map/ppermute | solution.py:231
  106.3 27.8 %collective-permute-start = (bf16[16,3,96,96]{3,2,1,0:T(8,128)(2,1)}, bf16[16,3,96,96]{3,2,1,0:T(8,128)(2,1)}, u32[]{:S(2)}, u32[]{:S(2)}) collective-permute-start(bf16[16,3,96,96]{3,2,1,0:T(8,128)(2,1)} %all-to-all-done.near_ref), channel_id=1, source_target_pairs={{0,1},{1,0},{2,3},{3,2},{4,5},{5,4},{6,7},{7,6},{8,9},{9,8},{10,11... | collective-permute-start | bytes 2654216 | tf_op jit(solution)/shard_map/ppermute | solution.py:231
  117.0 45.3 %collective-permute-start.3 = (bf16[2,32,7,16,128]{4,3,2,1,0:T(8,128)(2,1)S(1)}, bf16[2,32,7,16,128]{4,3,2,1,0:T(8,128)(2,1)}, u32[]{:S(2)}, u32[]{:S(2)}) collective-permute-start(bf16[2,32,7,16,128]{4,3,2,1,0:T(8,128)(2,1)S(1)} %pad_maximum_fusion.1), channel_id=1, source_target_pairs={{0,192},{1,193},{2,194},{3,195},{4,196},{5,197},{6,198},{7,199},{8... | collective-permute-start | bytes 5505032 | tf_op jit(solution)/shard_map/ppermute | solution.py:231
  117.4 44.6 %all-to-all-start.4 = ((bf16[16,3,96,96]{3,2,1,0:T(8,128)(2,1)}), bf16[16,3,96,96]{3,2,1,0:T(8,128)(2,1)S(1)}, u32[]{:S(2)}, u32[]{:S(2)}) async-start(bf16[16,3,96,96]{3,2,1,0:T(8,128)(2,1)} %get-tuple-element.94), calls=%async_computation.4 | async-start | bytes 2359296 | tf_op jit(solution)/shard_map/all_to_all | solution.py:240
  123.8 41.7 %collective-permute-start.2 = (bf16[2,32,7,16,128]{4,3,2,1,0:T(8,128)(2,1)S(1)}, bf16[2,32,7,16,128]{4,3,2,1,0:T(8,128)(2,1)}, u32[]{:S(2)}, u32[]{:S(2)}) collective-permute-start(bf16[2,32,7,16,128]{4,3,2,1,0:T(8,128)(2,1)S(1)} %pad_maximum_fusion.1), channel_id=1, source_target_pairs={{0,64},{1,65},{2,66},{3,67},{4,68},{5,69},{6,70},{7,71},{8,72},{9,... | collective-permute-start | bytes 5505032 | tf_op jit(solution)/shard_map/ppermute | solution.py:231
  125.2 8.8 %copy-start.8 = (bf16[96,96]{1,0:T(8,128)(2,1)}, bf16[96,96]{1,0:T(8,128)(2,1)S(1)}, u32[]{:S(2)}) copy-start(bf16[96,96]{1,0:T(8,128)(2,1)S(1)} %multiply_convert_fusion.refs_5_.refs_2_) | copy-start | bytes 55300
  125.8 8.2 %copy-start.7 = (bf16[256,256]{1,0:T(8,128)(2,1)}, bf16[256,256]{1,0:T(8,128)(2,1)S(1)}, u32[]{:S(2)}) copy-start(bf16[256,256]{1,0:T(8,128)(2,1)S(1)} %scatter.9.refs_6_.refs_3_) | copy-start | bytes 393220
  162.0 3.5 %copy-start.5 = (bf16[16,3,96,96]{3,2,1,0:T(8,128)(2,1)}, bf16[16,3,96,96]{3,2,1,0:T(8,128)(2,1)S(1)}, u32[]{:S(2)}) copy-start(bf16[16,3,96,96]{3,2,1,0:T(8,128)(2,1)S(1)} %all-to-all-done.4.near_ref) | copy-start | bytes 2654212
  162.0 25.5 %collective-permute-start.7 = (bf16[16,3,96,96]{3,2,1,0:T(8,128)(2,1)S(1)}, bf16[16,3,96,96]{3,2,1,0:T(8,128)(2,1)}, u32[]{:S(2)}, u32[]{:S(2)}) collective-permute-start(bf16[16,3,96,96]{3,2,1,0:T(8,128)(2,1)S(1)} %all-to-all-done.4.near_ref), channel_id=1, source_target_pairs={{0,1},{1,0},{2,3},{3,2},{4,5},{5,4},{6,7},{7,6},{8,9},{9,8},{10,11... | collective-permute-start | bytes 2654216 | tf_op jit(solution)/shard_map/ppermute | solution.py:231
  187.1 17.1 %copy-start.4 = (f32[16,3,96,96]{3,2,1,0:T(8,128)S(1)}, f32[16,3,96,96]{3,2,1,0:T(8,128)}, u32[]{:S(2)}) copy-start(f32[16,3,96,96]{3,2,1,0:T(8,128)} %get-tuple-element.90) | copy-start | bytes 5308420
  187.1 17.1 %collective-permute-start.6 = (bf16[16,3,96,96]{3,2,1,0:T(8,128)(2,1)}, bf16[16,3,96,96]{3,2,1,0:T(8,128)(2,1)}, u32[]{:S(2)}, u32[]{:S(2)}) collective-permute-start(bf16[16,3,96,96]{3,2,1,0:T(8,128)(2,1)} %get-tuple-element.93), channel_id=1, source_target_pairs={{0,1},{1,0},{2,3},{3,2},{4,5},{5,4},{6,7},{7,6},{8,9},{9,8},{10,11... | collective-permute-start | bytes 2654216 | tf_op jit(solution)/shard_map/ppermute | solution.py:231
  206.8 36.4 %all-to-all-start.3 = ((bf16[16,3,96,96]{3,2,1,0:T(8,128)(2,1)}), bf16[16,3,96,96]{3,2,1,0:T(8,128)(2,1)S(1)}, u32[]{:S(2)}, u32[]{:S(2)}) async-start(bf16[16,3,96,96]{3,2,1,0:T(8,128)(2,1)} %add_convert_fusion.1), calls=%async_computation.3 | async-start | bytes 2359296 | tf_op jit(solution)/shard_map/all_to_all | solution.py:240
  228.7 3.1 %collective-permute-start.8 = (bf16[16,3,96,96]{3,2,1,0:T(8,128)(2,1)}, bf16[16,3,96,96]{3,2,1,0:T(8,128)(2,1)S(1)}, u32[]{:S(2)}, u32[]{:S(2)}) collective-permute-start(bf16[16,3,96,96]{3,2,1,0:T(8,128)(2,1)} %get-tuple-element.98), channel_id=1, source_target_pairs={{0,1},{1,0},{2,3},{3,2},{4,5},{5,4},{6,7},{7,6},{8,9},{9,8},{10,11... | collective-permute-start | bytes 2654216 | tf_op jit(solution)/shard_map/ppermute | solution.py:231
  278.7 2.2 copy-start.1
Sparse Core Ops, SparseCore 0:
  42.8 76.8 all-gather.2

commit v3 on v0

v3 whole, which is shorter than its diff:
```python
import functools
import itertools
import math

import jax
import jax.numpy as jnp
import ml_dtypes
import numpy as np
from jax import lax
from jax.experimental import pallas as pl
from jax.experimental.pallas import tpu as pltpu
from jax.sharding import PartitionSpec as P

F32 = jnp.float32
BF16 = jnp.bfloat16
EXCHANGE_FRACTION = 0.25
LANES = 128
ROWS = 16
SLAB = 14
PIECE = 7
VMEM_LIMIT = 60 * 2**20
PITCH = 104
CHIP_GROUP = 8
BOTH = ("band", "pw")
HALVES = (slice(0, LANES), slice(LANES, 2 * LANES))


def cas_table(length):
    counter = np.arange(length)
    angles = counter[:, None] * counter[None, :] % length * (2.0 * math.pi / length)
    return ((np.cos(angles) + np.sin(angles)) / math.sqrt(length)).astype(ml_dtypes.bfloat16)


def double_table(table):
    length = table.shape[0]
    wide = np.zeros((2 * LANES, 2 * LANES), table.dtype)
    for low in (0, LANES):
        wide[low : low + length, low : low + length] = table
    return wide


def dot(a, b):
    return jnp.dot(a, b, preferred_element_type=F32)


def pack_tiles(tiles, kept):
    count, width = tiles.shape[-3], tiles.shape[-1]
    free = LANES - width
    thirds = [tiles[..., kept + k // 3, :, (k % 3) * free : (k % 3 + 1) * free] for k in range(3 * (count - kept))]
    thirds += [jnp.zeros_like(thirds[0])] * (kept - len(thirds))
    return jnp.concatenate([tiles[..., :kept, :, :], jnp.stack(thirds, axis=-3)], axis=-1)


def packed_rows(rows):
    width = rows[0].shape[1]
    free = LANES - width
    last = len(rows) - SLAB
    thirds = [rows[SLAB + k // 3][:, (k % 3) * free : (k % 3 + 1) * free] for k in range(3 * last)]
    thirds += [jnp.zeros_like(thirds[0])] * (SLAB - len(thirds))
    return [jnp.concatenate([rows[t], thirds[t]], axis=1) for t in range(SLAB)]


def unpacked_rows(tiles, count, width):
    extra = count - len(tiles)
    spare = [jnp.concatenate([tiles[3 * j + k][:, width:] for k in range(3)], axis=1) for j in range(extra)]
    return [t[:, :width] for t in tiles] + spare


def slab_planes(ref, chip, low, planes, length):
    per_plane = length // ROWS
    rows = unpacked_rows([ref[chip, low + t] for t in range(SLAB)], planes * per_plane, length)
    return [jnp.concatenate(rows[p * per_plane : (p + 1) * per_plane], axis=0) for p in range(planes)]


def slab_tiles(planes):
    return [plane[t * ROWS : (t + 1) * ROWS] for plane in planes for t in range(plane.shape[0] // ROWS)]


def pack_kernel(orbital_ref, index_ref, values_ref, even_ref, odd_ref):
    planes, length, width = index_ref.shape
    values = jnp.broadcast_to(values_ref[...], (length, LANES))
    blank = jnp.zeros((length, LANES - width), jnp.int32)
    field = []
    for plane in range(planes):
        levels = jnp.concatenate([index_ref[plane], blank], axis=1)
        here = jnp.take_along_axis(values, levels, axis=1, mode="promise_in_bounds")
        field.append(here[:, :width].astype(BF16))
    field = packed_rows(slab_tiles(field))
    chips = even_ref.shape[0]
    unroll = 4

    @pl.loop(0, chips // unroll)
    def _(step):
        for k in range(unroll):
            chip = step * unroll + k
            for which, ref in enumerate((even_ref, odd_ref)):
                slab = [orbital_ref[2 * chip + which, p] for p in range(planes)]
                for t, tile in enumerate(packed_rows(slab_tiles(slab))):
                    ref[chip, t] = tile
            for t in range(SLAB):
                even_ref[chip, SLAB + t] = field[t]


def pack_slabs(orbitals, shell_index, shell_kernel):
    chips = orbitals.shape[0] // 2
    vmem = pl.BlockSpec(memory_space=pltpu.VMEM)
    return pl.pallas_call(
        pack_kernel,
        in_specs=[vmem] * 3,
        out_specs=[vmem] * 2,
        out_shape=[jax.ShapeDtypeStruct((chips, n * SLAB, ROWS, LANES), BF16) for n in (2, 1)],
        compiler_params=pltpu.CompilerParams(vmem_limit_bytes=VMEM_LIMIT),
        name="pack",
    )(orbitals, shell_index, shell_kernel.reshape(1, LANES))


def unpack_sources(place_ref, pieces, planes, source):
    length = source.shape[1]
    per_plane = length // 2 // ROWS
    blank = jnp.zeros((length // 2, LANES - length), BF16)
    lows = [pl.multiple_of(h * (length // 2), ROWS) for h in (place_ref[1], 1 - place_ref[1])]
    unroll = 8

    @pl.loop(0, length // planes // unroll)
    def _(step):
        for k in range(unroll):
            part = step * unroll + k
            for number, ref in enumerate(pieces):
                rows = unpacked_rows([ref[part, t] for t in range(PIECE)], planes * per_plane, length)
                for plane in range(planes):
                    here = jnp.concatenate(rows[per_plane * plane : per_plane * (plane + 1)], axis=0)
                    here = jnp.concatenate([here, blank], axis=1)
                    source[number // 2, part * planes + plane, pl.ds(lows[number % 2], length // 2), :] = here


def solve_pair(core, planes, orbital, source, fields, tables, scratch, finish):
    near_ref, far_ref = orbital
    table_ref, double_ref = tables
    first, second = scratch
    chips = near_ref.shape[0]
    length = table_ref.shape[0]
    table = table_ref[...]
    blank = jnp.zeros((length, LANES - length), BF16)

    def slabs_of(step):
        for k in range(CHIP_GROUP):
            for near in (True, False):
                chip = step * CHIP_GROUP + k
                yield chip, near, (2 * chip + (core if near else 1 - core)) * planes

    @pl.loop(0, chips // CHIP_GROUP)
    def _(step):
        rows = []
        for chip, near, base in slabs_of(step):
            for p, plane in enumerate(slab_planes(near_ref if near else far_ref, chip, 0, planes, length)):
                plane = jnp.concatenate([plane, blank], axis=1).astype(F32)
                pair = [(source[s, base + p].astype(F32) * plane).astype(BF16) for s in range(2)]
                rows.append(jnp.concatenate(pair, axis=1))
        along_z = dot(jnp.concatenate(rows, axis=0), double_ref[...]).astype(BF16)
        for k, (chip, near, base) in enumerate(slabs_of(step)):
            for p in range(planes):
                low = (k * planes + p) * length
                section = dot(table, along_z[low : low + length])
                at = pl.multiple_of((base + p) * PITCH, 8)
                for s in range(2):
                    first[s, pl.ds(at, length), :] = section[:, HALVES[s]]

    @pl.loop(0, chips // CHIP_GROUP)
    def _(step):
        for chip, near, base in slabs_of(step):
            for p, field in enumerate(slab_planes(fields[0] if near else fields[1], chip, SLAB, planes, length)):
                field = jnp.concatenate([field, blank], axis=1).astype(F32)
                row = base + p
                values = [first[s, pl.ds(row, length, stride=PITCH), :].astype(BF16) for s in range(2)]
                section = dot(table, jnp.concatenate(values, axis=1))
                values = [(section[:, HALVES[s]] * field).astype(BF16) for s in range(2)]
                section = dot(table, jnp.concatenate(values, axis=1))
                at = pl.multiple_of(row * PITCH, 8)
                for s in range(2):
                    second[s, pl.ds(at, length), :] = section[:, HALVES[s]]

    @pl.loop(0, chips // CHIP_GROUP)
    def _(step):
        sections = []
        for chip, near, base in slabs_of(step):
            for p in range(planes):
                values = [second[s, pl.ds(base + p, length, stride=PITCH), :].astype(BF16) for s in range(2)]
                sections.append(dot(table, jnp.concatenate(values, axis=1)).astype(BF16))
        potential = dot(jnp.concatenate(sections, axis=0), double_ref[...])
        for k, (chip, near, base) in enumerate(slabs_of(step)):
            terms = []
            for p in range(planes):
                low = (k * planes + p) * length
                here = potential[low : low + length]
                both = [source[s, base + p].astype(F32) * here[:, HALVES[s]] for s in range(2)]
                terms.append(both[0] + both[1])
            finish(chip, near, base, terms)


def store_scaled(chip, near, sums, keep_ref, send_ref):
    length = sums[0].shape[0]
    rows = slab_tiles([(-EXCHANGE_FRACTION * value)[:, :length] for value in sums])
    for t, tile in enumerate(packed_rows(rows)):
        if near:
            keep_ref[chip, t] = tile
        else:
            send_ref[chip, t] = tile.astype(BF16)


def first_kernel(last, planes, place_ref, near_ref, far_ref, *refs):
    pieces, refs = refs[:4], refs[4:]
    table_ref, double_ref = refs[:2]
    refs = refs[2:]
    if last:
        before_hbm, keep_ref, send_ref, source, first, second, before, semaphore = refs
        before_copy = pltpu.make_async_copy(before_hbm, before, semaphore)
        before_copy.start()
    else:
        total_ref, source, first, second = refs
    unpack_sources(place_ref, pieces, planes, source)
    if last:
        before_copy.wait()

    def finish(chip, near, base, terms):
        if last:
            sums = [before[base + p] + terms[p] for p in range(planes)]
            store_scaled(chip, near, sums, keep_ref, send_ref)
        else:
            for p in range(planes):
                total_ref[base + p] = terms[p]

    orbital = (near_ref, far_ref)
    solve_pair(place_ref[0], planes, orbital, source, orbital, (table_ref, double_ref), (first, second), finish)


def second_kernel(planes, place_ref, near_ref, far_ref, near_field, far_field, one_hbm, two_hbm, table_ref, double_ref,
                  keep_ref, send_ref, sources, first, second, total, semaphores):
    copies = [
        pltpu.make_async_copy(ref, sources.at[k], semaphores.at[k]) for k, ref in enumerate((one_hbm, two_hbm))
    ]
    for copy in copies:
        copy.start()
    copies[0].wait()

    def keep_total(chip, near, base, terms):
        for p in range(planes):
            total[base + p] = terms[p]

    def finish(chip, near, base, terms):
        store_scaled(chip, near, [total[base + p] + terms[p] for p in range(planes)], keep_ref, send_ref)

    orbital, fields = (near_ref, far_ref), (near_field, far_field)
    tables, scratch = (table_ref, double_ref), (first, second)
    core = place_ref[0]
    solve_pair(core, planes, orbital, sources.at[0], fields, tables, scratch, keep_total)
    copies[1].wait()
    solve_pair(core, planes, orbital, sources.at[1], fields, tables, scratch, finish)


def solve_call(kernel, operands, in_hbm, outs, scratch, length, pairs):
    vmem = pl.BlockSpec(memory_space=pltpu.VMEM)
    specs = [pl.BlockSpec(memory_space=pl.ANY) if k in in_hbm else vmem for k in range(len(operands))]
    specs[0] = pl.BlockSpec(memory_space=pltpu.SMEM)
    return pl.pallas_call(
        kernel,
        in_specs=specs,
        out_specs=[vmem] * len(outs),
        out_shape=outs,
        scratch_shapes=scratch,
        compiler_params=pltpu.CompilerParams(vmem_limit_bytes=VMEM_LIMIT),
        cost_estimate=pl.CostEstimate(
            flops=144 * length**4 * pairs, bytes_accessed=8 * length**3, transcendentals=0
        ),
        name="solve",
    )(*operands)


def solve_first(place, orbital, pieces, table, before, planes):
    near, far = orbital
    length = table.shape[0]
    whole = (length, length, LANES)
    last = before is not None
    operands = [place, near, far, *pieces, table, double_table(table)]
    in_hbm = []
    section = pltpu.VMEM((2, (length + 1) * PITCH, LANES), F32)
    scratch = [section, section]
    if last:
        in_hbm.append(len(operands))
        operands.append(before)
        scratch += [pltpu.VMEM(whole, F32), pltpu.SemaphoreType.DMA]
        slab = (near.shape[0], SLAB) + near.shape[2:]
        outs = [jax.ShapeDtypeStruct(slab, F32), jax.ShapeDtypeStruct(slab, BF16)]
    else:
        outs = [jax.ShapeDtypeStruct(whole, F32)]
    outs.append(jax.ShapeDtypeStruct((2,) + whole, BF16))
    return solve_call(functools.partial(first_kernel, last, planes), operands, in_hbm, outs, scratch, length, 1)


def solve_second(place, orbital, field, sources, table, planes):
    near, far = orbital
    length = table.shape[0]
    whole = (length, length, LANES)
    section = pltpu.VMEM((2, (length + 1) * PITCH, LANES), F32)
    outs = [jax.ShapeDtypeStruct(near.shape, F32), jax.ShapeDtypeStruct(near.shape, BF16)]
    scratch = [pltpu.VMEM((2, 2) + whole, BF16), section, section, pltpu.VMEM(whole, F32)]
    scratch.append(pltpu.SemaphoreType.DMA((2,)))
    operands = [place, near, far, *field, *sources, table, double_table(table)]
    return solve_call(functools.partial(second_kernel, planes), operands, (5, 6), outs, scratch, length, 2)


def unpack_kernel(slab_ref, *refs):
    out_ref = refs[-1]
    planes, length = out_ref.shape[2:4]
    for chip in range(slab_ref.shape[0]):
        for p, plane in enumerate(slab_planes(slab_ref, chip, 0, planes, length)):
            out_ref[chip, 0, p] = plane


def unpack_slabs(slabs, which, before, planes, length):
    chips = slabs.shape[0]
    steps = 2
    block = pl.BlockSpec((chips // steps,) + slabs.shape[1:], lambda i: (i, 0, 0, 0))
    given = [] if before is None else [before]
    return pl.pallas_call(
        unpack_kernel,
        grid=(steps,),
        in_specs=[block] + [pl.BlockSpec(memory_space=pl.ANY)] * len(given),
        out_specs=pl.BlockSpec((chips // steps, 1, planes, length, length), lambda i: (i, which, 0, 0, 0)),
        out_shape=jax.ShapeDtypeStruct((chips, 2, planes, length, length), BF16),
        input_output_aliases={1: 0} if given else {},
        compiler_params=pltpu.CompilerParams(vmem_limit_bytes=VMEM_LIMIT),
        name="unpack",
    )(slabs, *given)


def device(y, x, z, core):
    return ((y * 2 + x // 2) * 2 + x % 2) * 16 + z * 2 + core


def moved(value, dy=0, mirror=False, core=0):
    places = itertools.product(range(4), range(4), range(8), range(2))
    pairs = [(device(y, x, z, c), device((y + dy) % 4, 3 - x if mirror else x, z, c ^ core)) for y, x, z, c in places]
    return lax.ppermute(value, BOTH, pairs)


def between_chips(value):
    bands, parts = lax.axis_size("band"), lax.axis_size("pw")
    groups = [[b * parts + 2 * p + c for p in range(parts // 2)] for b in range(bands) for c in range(2)]
    return lax.all_to_all(value, BOTH, 0, 0, axis_index_groups=groups, tiled=True)


def own_pieces(orbitals, owners, chosen):
    me = lax.axis_index("band")
    planes, length, width = orbitals.shape[1:]
    rows = jnp.sum(jnp.where((owners == me)[:, None], chosen, 0), axis=0)
    own = jnp.concatenate([lax.dynamic_slice_in_dim(orbitals, rows[s], 1) for s in range(2)], axis=0)
    tiles = own.reshape(2, planes, 2, length // 2 // ROWS, ROWS, width)
    tiles = tiles.transpose(2, 0, 1, 3, 4, 5).reshape(2, 2, planes * length // 2 // ROWS, ROWS, width)
    packed = pack_tiles(tiles, PIECE)
    received = lax.all_to_all(jnp.concatenate([packed] * 4, axis=0), "band", 0, 0, tiled=True)
    return lax.dynamic_index_in_dim(received, owners[me // 2], 0, keepdims=False)


def on_device(orbitals, owners, chosen, shell_index, shell_kernel):
    band, part = lax.axis_index("band"), lax.axis_index("pw")
    count, planes, length, width = orbitals.shape
    table = cas_table(length)
    place = jnp.stack([part % 2, band % 2])

    pieces = own_pieces(orbitals, owners, chosen)
    copies = jnp.broadcast_to(pieces[None], (count // 2,) + pieces.shape).reshape((count,) + pieces.shape[1:])
    own = lax.all_to_all(copies, "pw", 0, 0, tiled=True)
    across = moved(own, mirror=True)
    opposite = moved(own, dy=2)
    opposite_across = moved(opposite, mirror=True)
    later_own, _ = lax.optimization_barrier((own, opposite))
    beside = [moved(later_own, dy=dy) for dy in (1, 3)]

    slabs = list(pack_slabs(orbitals, jnp.swapaxes(shell_index, 0, 1), shell_kernel))
    even = between_chips(slabs[0])
    even, across, opposite_across, *beside = lax.optimization_barrier((even, across, opposite_across, *beside))
    beside_across = [moved(across, dy=dy) for dy in (1, 3)]
    even = (even, moved(even, core=1))
    slabs[1], _ = lax.optimization_barrier((slabs[1], across))
    odd = between_chips(slabs[1])
    odd = (odd, moved(odd, core=1))

    def finished(keep, send):
        return between_chips((keep + moved(send, core=1).astype(F32)).astype(BF16))

    pieces = [own, across, opposite, opposite_across]
    total, one = solve_first(place, even, pieces, table, None, planes)
    pieces = [beside[0], beside_across[0], beside[1], beside_across[1]]
    keep, send, two = solve_first(place, even, pieces, table, total, planes)
    result = unpack_slabs(finished(keep, send), 0, None, planes, length)
    keep, send = solve_second(place, odd, even, (one, two), table, planes)
    result = unpack_slabs(finished(keep, send), 1, result, planes, length)
    return result.reshape(orbitals.shape)


def solution(mesh):
    return jax.shard_map(
        on_device,
        mesh=mesh,
        in_specs=(P("band", "pw", None, None), P(), P(), P(None, "pw", None), P()),
        out_specs=P("band", "pw", None, None),
        check_vma=False,
    )
```

time: 1120 us -> 242 us (0.22)
  waiting for transfers between devices: 670 us -> 93.7 us
  local copies, waits for them, and re-layouts: 168 us -> 5.55 us
  matrix products: 151 us -> 0 us
  Pallas kernels: 0 us -> 70.8 us
  other arithmetic: 42 us -> 8.5 us
    all_to_all x8 -> x6, waiting for transfers between devices: 583 us -> 66 us  [the longest x4 38.7 us: between_chips(): lax.all_to_all(value, BOTH, 0, 0, axis_index_groups=groups, tiled=True)]
    dot_general x20 -> x0, matrix products: 151 us -> none  [apply_axis(): jnp.einsum(form, values, transform, preferred_element_type=jnp.float32)]
    psum x1 -> x0, waiting for transfers between devices: 87.2 us -> none  [from_root(): return lax.psum(jnp.where(mine, value, jnp.zeros_like(value)), axis)]
    pallas_call x0 -> x6, Pallas kernels: none -> 70.8 us  [the longest x3 62 us: solve_call(): pl.pallas_call(kernel, in_specs=specs, out_specs=[vmem] * len(outs), out_...]
    dynamic_slice x192 -> x2, local copies, waits for them, and re-layouts: 69.6 us -> 1.59 us  [the longest x1 0.94 us: own_pieces(): lax.dynamic_slice_in_dim(orbitals, rows[s], 1)]
    convert_element_type x8 -> x0, local copies, waits for them, and re-layouts: 51.8 us -> none  [the longest x4 26.3 us: middle_sections(): return apply_axis(section, transform, FORM_FIRST).astype(jnp.bfloat16)]
    ppermute x0 -> x11, waiting for transfers between devices: none -> 27.7 us  [moved(): return lax.ppermute(value, BOTH, pairs)]
    reduce_sum x96 -> x1, other arithmetic: 21.3 us -> 0.79 us  [own_pieces(): rows = jnp.sum(jnp.where((owners == me)[:, None], chosen, 0), axis=0)]
  transfers between devices with their start and end apart: 9 -> 17, of which waited for: 8 -> 9; matrix products, arithmetic and copies ran while one was open for 26% -> 3% of each run, Pallas kernels for 0% -> 29%
where the time goes in v3:
time: 242 us; the launch traced here: 240 us
  waiting for transfers between devices  93.7 us (39%)
  Pallas kernels  70.8 us (29%)
  starting transfers between devices  55.7 us (23%)
  other arithmetic  8.5 us (4%)
  between operations  5.96 us (2%)
  local copies, waits for them, and re-layouts  5.55 us (2%)
    pallas_call x3, Pallas kernels, solve_call(): pl.pallas_call(kernel, in_specs=specs, out_specs=[vmem] * len(outs), out_...  62 us
    all_to_all x4, waiting for transfers between devices, between_chips(): lax.all_to_all(value, BOTH, 0, 0, axis_index_groups=groups, tiled=True)  38.7 us
    all_to_all x4, starting transfers between devices, between_chips(): lax.all_to_all(value, BOTH, 0, 0, axis_index_groups=groups, tiled=True)  28.6 us
    ppermute x11, waiting for transfers between devices, moved(): return lax.ppermute(value, BOTH, pairs)  27.7 us
    all_to_all x1, waiting for transfers between devices, on_device(): own = lax.all_to_all(copies, 'pw', 0, 0, tiled=True)  21.7 us
    ppermute x11, starting transfers between devices, moved(): return lax.ppermute(value, BOTH, pairs)  10.2 us
    all_to_all x1, starting transfers between devices, on_device(): own = lax.all_to_all(copies, 'pw', 0, 0, tiled=True)  9.49 us
    all_to_all x1, starting transfers between devices, own_pieces(): lax.all_to_all(jnp.concatenate([packed] * 4, axis=0), 'band', 0, 0, tiled...  7.43 us
  transfers between devices with their start and end apart: 17, of which 9 were waited for; matrix products, arithmetic and copies ran while one was open for 3% of the time, Pallas kernels for 29%

profile of v3, /device:TPU:4, one launch (start us, length us, event | category | flops | bytes accessed | tf_op | source)
XLA Modules:
  0.0 240.2 jit_solution(7680632064483549762)
XLA Ops:
  0.0 0.0 copy-start.6
  0.0 0.7 broadcast_compare_fusion
  0.7 0.8 select_reduce_fusion
  1.5 0.7 fusion
  6.0 0.9 constant_dynamic-slice_fusion.1
  7.1 0.1 slice_dynamic-update-slice_fusion.4
  7.1 0.1 slice_dynamic-update-slice_fusion.3
  7.2 0.1 slice_dynamic-update-slice_fusion.1
  7.3 0.1 slice_dynamic-update-slice_fusion
  7.4 1.0 maximum_maximum_fusion
  8.4 7.4 %all-to-all-start.1 = ((bf16[8,2,7,16,128]{4,3,2,1,0:T(8,128)(2,1)}), bf16[8,2,7,16,128]{4,3,2,1,0:T(8,128)(2,1)S(1)}, u32[]{:S(2)}, u32[]{:S(2)}) async-start(bf16[8,2,7,16,128]{4,3,2,1,0:T(8,128)(2,1)} %maximum_maximum_fusion), calls=%async_computation.1 | async-start | bytes 917504 | tf_op jit(solution)/shard_map/all_to_all | solution.py:360
  15.8 0.0 copy-done.6
  15.8 0.7 dynamic_slice.15
  18.4 5.6 %all-to-all-done.1 = bf16[8,2,7,16,128]{4,3,2,1,0:T(8,128)(2,1)S(1)} async-done(((bf16[8,2,7,16,128]{4,3,2,1,0:T(8,128)(2,1)}), bf16[8,2,7,16,128]{4,3,2,1,0:T(8,128)(2,1)S(1)}, u32[]{:S(2)}, u32[]{:S(2)}) %all-to-all-start.1) | async-done | bytes 458784 | tf_op jit(solution)/shard_map/all_to_all | solution.py:360
  24.0 1.1 broadcast_in_dim.24
  25.1 9.5 %all-to-all-start.2 = ((bf16[32,7,16,128]{3,2,1,0:T(8,128)(2,1)}), bf16[32,7,16,128]{3,2,1,0:T(8,128)(2,1)S(1)}, u32[]{:S(2)}, u32[]{:S(2)}) async-start(bf16[32,7,16,128]{3,2,1,0:T(8,128)(2,1)} %bitcast.11), calls=%async_computation.2 | async-start | bytes 1835008 | tf_op jit(solution)/shard_map/all_to_all | solution.py:372
  34.6 4.2 %pack.1 = (bf16[16,28,16,128]{3,2,1,0:T(8,128)(2,1)}, bf16[16,14,16,128]{3,2,1,0:T(8,128)(2,1)}) custom-call(bf16[32,3,96,96]{3,2,1,0:T(8,128)(2,1)} %orbital_ref.1, s32[3,96,96]{2,1,0:T(8,128)} %bitcast.23, f32[1,128]{1,0:T(1,128)} %bitcast.24), custom_call_target="tpu_custom_call" | custom-call | tf_op jit(solution)/shard_map/pack/pallas_call | solution.py:107
  38.8 21.7 %all-to-all-done.2.refs_0_ = bf16[32,7,16,128]{3,2,1,0:T(8,128)(2,1)S(1)} async-done(((bf16[32,7,16,128]{3,2,1,0:T(8,128)(2,1)}), bf16[32,7,16,128]{3,2,1,0:T(8,128)(2,1)S(1)}, u32[]{:S(2)}, u32[]{:S(2)}) %all-to-all-start.2) | async-done | bytes 917536 | tf_op jit(solution)/shard_map/all_to_all | solution.py:372
  60.5 3.7 %all-to-all-start = ((bf16[16,28,16,128]{3,2,1,0:T(8,128)(2,1)}), bf16[16,28,16,128]{3,2,1,0:T(8,128)(2,1)S(1)}, u32[]{:S(2)}, u32[]{:S(2)}) async-start(bf16[16,28,16,128]{3,2,1,0:T(8,128)(2,1)} %get-tuple-element.22), calls=%async_computation | async-start | bytes 3670016 | tf_op jit(solution)/shard_map/all_to_all | solution.py:349
  64.2 0.7 collective-permute-start.1
  65.0 2.6 %collective-permute-start = (bf16[32,7,16,128]{3,2,1,0:T(8,128)(2,1)S(1)}, bf16[32,7,16,128]{3,2,1,0:T(8,128)(2,1)}, u32[]{:S(2)}, u32[]{:S(2)}) collective-permute-start(bf16[32,7,16,128]{3,2,1,0:T(8,128)(2,1)S(1)} %all-to-all-done.2.refs_0_), channel_id=1, source_target_pairs={{0,48},{1,49},{2,50},{3,51},{4,52},{5,53},{6,54},{7,55},{8,56},{9,... | collective-permute-start | bytes 2752520 | tf_op jit(solution)/shard_map/ppermute | solution.py:343
  67.5 20.1 %collective-permute-done.1.refs_2_ = bf16[32,7,16,128]{3,2,1,0:T(8,128)(2,1)} collective-permute-done((bf16[32,7,16,128]{3,2,1,0:T(8,128)(2,1)S(1)}, bf16[32,7,16,128]{3,2,1,0:T(8,128)(2,1)}, u32[]{:S(2)}, u32[]{:S(2)}) %collective-permute-start.1) | collective-permute-done | bytes 917536 | tf_op jit(solution)/shard_map/ppermute | solution.py:343
  87.7 1.2 collective-permute-start.4
  88.9 0.0 copy-done.3
  88.9 0.9 collective-permute-start.3
  89.7 2.2 collective-permute-start.2
  91.9 0.0 collective-permute-done.refs_1_
  91.9 16.3 %all-to-all-done.near_ref.near_field = bf16[16,28,16,128]{3,2,1,0:T(8,128)(2,1)S(1)} async-done(((bf16[16,28,16,128]{3,2,1,0:T(8,128)(2,1)}), bf16[16,28,16,128]{3,2,1,0:T(8,128)(2,1)S(1)}, u32[]{:S(2)}, u32[]{:S(2)}) %all-to-all-start) | async-done | bytes 1835040 | tf_op jit(solution)/shard_map/all_to_all | solution.py:349
  108.2 0.5 collective-permute-done.4.refs_2_
  108.6 2.1 collective-permute-done.3.refs_0_
  110.7 0.0 collective-permute-done.2.refs_3_
  110.7 0.0 collective-permute-start.6
  110.7 0.7 pad_add_fusion.place_ref
  111.4 2.0 collective-permute-start.8
  113.4 0.1 collective-permute-start.7
  113.4 8.7 %all-to-all-start.3 = ((bf16[16,14,16,128]{3,2,1,0:T(8,128)(2,1)}), bf16[16,14,16,128]{3,2,1,0:T(8,128)(2,1)S(1)}, u32[]{:S(2)}, u32[]{:S(2)}) async-start(bf16[16,14,16,128]{3,2,1,0:T(8,128)(2,1)} %get-tuple-element.25), calls=%async_computation.3 | async-start | bytes 1835008 | tf_op jit(solution)/shard_map/all_to_all | solution.py:349
  122.1 0.0 collective-permute-done.6.far_ref.far_field
  122.1 0.0 copy-done.2
  122.1 16.7 %solve.3 = (f32[96,96,128]{2,1,0:T(8,128)}, bf16[2,96,96,128]{3,2,1,0:T(8,128)(2,1)}) custom-call(s32[2]{0:T(128)} %pad_add_fusion.place_ref, bf16[16,28,16,128]{3,2,1,0:T(8,128)(2,1)} %copy-done.2, bf16[16,28,16,128]{3,2,1,0:T(8,128)(2,1)} %collective-permute-done.6.far_ref.far_field, bf16[32,7,16,128]{3,2,1,0:T(8,128)(2,1)} %copy-done.3, ...), custom_call_target="tpu_custom_call" | custom-call | flops 12230590464 | bytes 7077888 | tf_op jit(solution)/shard_map/solve/pallas_call | solution.py:264
  138.8 0.0 collective-permute-done.8.refs_3_
  138.8 0.0 collective-permute-done.7.refs_1_
  138.8 18.7 %solve.4 = (f32[16,14,16,128]{3,2,1,0:T(8,128)}, bf16[16,14,16,128]{3,2,1,0:T(8,128)(2,1)}, bf16[2,96,96,128]{3,2,1,0:T(8,128)(2,1)}) custom-call(s32[2]{0:T(128)} %pad_add_fusion.place_ref, bf16[16,28,16,128]{3,2,1,0:T(8,128)(2,1)} %copy-done.2, bf16[16,28,16,128]{3,2,1,0:T(8,128)(2,1)} %collective-permute-done.6.far_ref.far_field, ...), custom_call_target="tpu_custom_call" | custom-call | flops 12230590464 | bytes 7077888 | tf_op jit(solution)/shard_map/solve/pallas_call | solution.py:264
  157.6 0.1 collective-permute-start.10
  157.7 0.0 all-to-all-done.3.near_ref
  157.7 0.0 copy-start.4
  157.7 0.5 collective-permute-start.5
  158.2 2.3 collective-permute-done.10
  160.5 2.7 %add_convert_fusion = bf16[16,14,16,128]{3,2,1,0:T(8,128)(2,1)} fusion(f32[16,14,16,128]{3,2,1,0:T(8,128)} %get-tuple-element.35, bf16[16,14,16,128]{3,2,1,0:T(8,128)(2,1)S(1)} %collective-permute-done.10), kind=kLoop, calls=%fused_computation | loop fusion | flops 1376256 | bytes 3670016 | tf_op jit(solution)/shard_map/convert_element_type | solution.py:389
  163.1 0.0 copy-done.4
  163.1 8.1 %all-to-all-start.5 = ((bf16[16,14,16,128]{3,2,1,0:T(8,128)(2,1)}), bf16[16,14,16,128]{3,2,1,0:T(8,128)(2,1)S(1)}, u32[]{:S(2)}, u32[]{:S(2)}) async-start(bf16[16,14,16,128]{3,2,1,0:T(8,128)(2,1)} %add_convert_fusion), calls=%async_computation.5 | async-start | bytes 1835008 | tf_op jit(solution)/shard_map/all_to_all | solution.py:349
  171.2 0.0 collective-permute-done.5.far_ref
  171.2 0.0 copy-start.5
  171.2 0.9 copy-done.5
  172.2 26.5 %solve.5 = (f32[16,14,16,128]{3,2,1,0:T(8,128)}, bf16[16,14,16,128]{3,2,1,0:T(8,128)(2,1)}) custom-call(s32[2]{0:T(128)} %pad_add_fusion.place_ref, bf16[16,14,16,128]{3,2,1,0:T(8,128)(2,1)} %copy-done.4, bf16[16,14,16,128]{3,2,1,0:T(8,128)(2,1)} %copy-done.5, bf16[16,28,16,128]{3,2,1,0:T(8,128)(2,1)} %copy-done.2, ...), custom_call_target="tpu_custom_call" | custom-call | flops 24461180928 | bytes 7077888 | tf_op jit(solution)/shard_map/solve/pallas_call | solution.py:264
  198.7 0.1 collective-permute-start.9
  198.8 2.7 %collective-permute-done.9 = bf16[16,14,16,128]{3,2,1,0:T(8,128)(2,1)S(1)} collective-permute-done((bf16[16,14,16,128]{3,2,1,0:T(8,128)(2,1)}, bf16[16,14,16,128]{3,2,1,0:T(8,128)(2,1)S(1)}, u32[]{:S(2)}, u32[]{:S(2)}) %collective-permute-start.9) | collective-permute-done | bytes 917536 | tf_op jit(solution)/shard_map/ppermute | solution.py:343
  201.5 2.7 %add_convert_fusion.1 = bf16[16,14,16,128]{3,2,1,0:T(8,128)(2,1)} fusion(f32[16,14,16,128]{3,2,1,0:T(8,128)} %get-tuple-element.33, bf16[16,14,16,128]{3,2,1,0:T(8,128)(2,1)S(1)} %collective-permute-done.9), kind=kLoop, calls=%fused_computation.1 | loop fusion | flops 1376256 | bytes 3670016 | tf_op jit(solution)/shard_map/convert_element_type | solution.py:389
  204.1 0.0 all-to-all-done.5.slab_ref
  204.1 8.1 %all-to-all-start.4 = ((bf16[16,14,16,128]{3,2,1,0:T(8,128)(2,1)}), bf16[16,14,16,128]{3,2,1,0:T(8,128)(2,1)S(1)}, u32[]{:S(2)}, u32[]{:S(2)}) async-start(bf16[16,14,16,128]{3,2,1,0:T(8,128)(2,1)} %add_convert_fusion.1), calls=%async_computation.4 | async-start | bytes 1835008 | tf_op jit(solution)/shard_map/all_to_all | solution.py:349
  212.3 0.0 copy-done
  212.3 2.3 unpack.2.refs_0_
  214.6 22.4 %all-to-all-done.4.slab_ref = bf16[16,14,16,128]{3,2,1,0:T(8,128)(2,1)S(1)} async-done(((bf16[16,14,16,128]{3,2,1,0:T(8,128)(2,1)}), bf16[16,14,16,128]{3,2,1,0:T(8,128)(2,1)S(1)}, u32[]{:S(2)}, u32[]{:S(2)}) %all-to-all-start.4) | async-done | bytes 917536 | tf_op jit(solution)/shard_map/all_to_all | solution.py:349
  237.0 0.9 copy-done.1
  237.9 2.3 unpack.3
  (11 shorter events, 0.1 us)
Async XLA Ops:
  0.0 15.8 %copy-start.6 = (s32[4]{0:T(128)S(1)}, s32[4]{0:T(128)}, u32[]{:S(2)}) copy-start(s32[4]{0:T(128)} %param.10) | copy-start | bytes 52
  8.4 15.6 %all-to-all-start.1 = ((bf16[8,2,7,16,128]{4,3,2,1,0:T(8,128)(2,1)}), bf16[8,2,7,16,128]{4,3,2,1,0:T(8,128)(2,1)S(1)}, u32[]{:S(2)}, u32[]{:S(2)}) async-start(bf16[8,2,7,16,128]{4,3,2,1,0:T(8,128)(2,1)} %maximum_maximum_fusion), calls=%async_computation.1 | async-start | bytes 917504 | tf_op jit(solution)/shard_map/all_to_all | solution.py:360
  25.1 35.4 %all-to-all-start.2 = ((bf16[32,7,16,128]{3,2,1,0:T(8,128)(2,1)}), bf16[32,7,16,128]{3,2,1,0:T(8,128)(2,1)S(1)}, u32[]{:S(2)}, u32[]{:S(2)}) async-start(bf16[32,7,16,128]{3,2,1,0:T(8,128)(2,1)} %bitcast.11), calls=%async_computation.2 | async-start | bytes 1835008 | tf_op jit(solution)/shard_map/all_to_all | solution.py:372
  60.5 28.4 %copy-start.3 = (bf16[32,7,16,128]{3,2,1,0:T(8,128)(2,1)}, bf16[32,7,16,128]{3,2,1,0:T(8,128)(2,1)S(1)}, u32[]{:S(2)}) copy-start(bf16[32,7,16,128]{3,2,1,0:T(8,128)(2,1)S(1)} %all-to-all-done.2.refs_0_) | copy-start | bytes 2752516
  60.5 47.7 %all-to-all-start = ((bf16[16,28,16,128]{3,2,1,0:T(8,128)(2,1)}), bf16[16,28,16,128]{3,2,1,0:T(8,128)(2,1)S(1)}, u32[]{:S(2)}, u32[]{:S(2)}) async-start(bf16[16,28,16,128]{3,2,1,0:T(8,128)(2,1)} %get-tuple-element.22), calls=%async_computation | async-start | bytes 3670016 | tf_op jit(solution)/shard_map/all_to_all | solution.py:349
  64.2 23.5 %collective-permute-start.1 = (bf16[32,7,16,128]{3,2,1,0:T(8,128)(2,1)S(1)}, bf16[32,7,16,128]{3,2,1,0:T(8,128)(2,1)}, u32[]{:S(2)}, u32[]{:S(2)}) collective-permute-start(bf16[32,7,16,128]{3,2,1,0:T(8,128)(2,1)S(1)} %all-to-all-done.2.refs_0_), channel_id=1, source_target_pairs={{0,128},{1,129},{2,130},{3,131},{4,132},{5,133},{6,134},{7,135},{8... | collective-permute-start | bytes 2752520 | tf_op jit(solution)/shard_map/ppermute | solution.py:343
  65.0 26.9 %collective-permute-start = (bf16[32,7,16,128]{3,2,1,0:T(8,128)(2,1)S(1)}, bf16[32,7,16,128]{3,2,1,0:T(8,128)(2,1)}, u32[]{:S(2)}, u32[]{:S(2)}) collective-permute-start(bf16[32,7,16,128]{3,2,1,0:T(8,128)(2,1)S(1)} %all-to-all-done.2.refs_0_), channel_id=1, source_target_pairs={{0,48},{1,49},{2,50},{3,51},{4,52},{5,53},{6,54},{7,55},{8,56},{9,... | collective-permute-start | bytes 2752520 | tf_op jit(solution)/shard_map/ppermute | solution.py:343
  87.7 21.0 %collective-permute-start.4 = (bf16[32,7,16,128]{3,2,1,0:T(8,128)(2,1)S(1)}, bf16[32,7,16,128]{3,2,1,0:T(8,128)(2,1)}, u32[]{:S(2)}, u32[]{:S(2)}) collective-permute-start(bf16[32,7,16,128]{3,2,1,0:T(8,128)(2,1)S(1)} %all-to-all-done.2.refs_0_), channel_id=1, source_target_pairs={{0,192},{1,193},{2,194},{3,195},{4,196},{5,197},{6,198},{7,199},{8... | collective-permute-start | bytes 2752520 | tf_op jit(solution)/shard_map/ppermute | solution.py:343
  88.9 21.9 %collective-permute-start.3 = (bf16[32,7,16,128]{3,2,1,0:T(8,128)(2,1)S(1)}, bf16[32,7,16,128]{3,2,1,0:T(8,128)(2,1)}, u32[]{:S(2)}, u32[]{:S(2)}) collective-permute-start(bf16[32,7,16,128]{3,2,1,0:T(8,128)(2,1)S(1)} %all-to-all-done.2.refs_0_), channel_id=1, source_target_pairs={{0,64},{1,65},{2,66},{3,67},{4,68},{5,69},{6,70},{7,71},{8,72},{9,... | collective-permute-start | bytes 2752520 | tf_op jit(solution)/shard_map/ppermute | solution.py:343
  89.7 21.0 %collective-permute-start.2 = (bf16[32,7,16,128]{3,2,1,0:T(8,128)(2,1)}, bf16[32,7,16,128]{3,2,1,0:T(8,128)(2,1)}, u32[]{:S(2)}, u32[]{:S(2)}) collective-permute-start(bf16[32,7,16,128]{3,2,1,0:T(8,128)(2,1)} %collective-permute-done.1.refs_2_), channel_id=1, source_target_pairs={{0,48},{1,49},{2,50},{3,51},{4,52},{5,53},{6,54},{7,55},{8,56},{9,... | collective-permute-start | bytes 2752520 | tf_op jit(solution)/shard_map/ppermute | solution.py:343
  108.2 14.0 %copy-start.2 = (bf16[16,28,16,128]{3,2,1,0:T(8,128)(2,1)}, bf16[16,28,16,128]{3,2,1,0:T(8,128)(2,1)S(1)}, u32[]{:S(2)}) copy-start(bf16[16,28,16,128]{3,2,1,0:T(8,128)(2,1)S(1)} %all-to-all-done.near_ref.near_field) | copy-start | bytes 5505028
  110.7 11.4 %collective-permute-start.6 = (bf16[16,28,16,128]{3,2,1,0:T(8,128)(2,1)S(1)}, bf16[16,28,16,128]{3,2,1,0:T(8,128)(2,1)}, u32[]{:S(2)}, u32[]{:S(2)}) collective-permute-start(bf16[16,28,16,128]{3,2,1,0:T(8,128)(2,1)S(1)} %all-to-all-done.near_ref.near_field), channel_id=1, source_target_pairs={{0,1},{1,0},{2,3},{3,2},{4,5},{5,4},{6,7},{7,6},{8,9},{9,8},{10,11... | collective-permute-start | bytes 5505032 | tf_op jit(solution)/shard_map/ppermute | solution.py:343
  111.4 27.4 %collective-permute-start.8 = (bf16[32,7,16,128]{3,2,1,0:T(8,128)(2,1)}, bf16[32,7,16,128]{3,2,1,0:T(8,128)(2,1)}, u32[]{:S(2)}, u32[]{:S(2)}) collective-permute-start(bf16[32,7,16,128]{3,2,1,0:T(8,128)(2,1)} %collective-permute-done.refs_1_), channel_id=1, source_target_pairs={{0,192},{1,193},{2,194},{3,195},{4,196},{5,197},{6,198},{7,199},{8... | collective-permute-start | bytes 2752520 | tf_op jit(solution)/shard_map/ppermute | solution.py:343
  113.4 25.5 %collective-permute-start.7 = (bf16[32,7,16,128]{3,2,1,0:T(8,128)(2,1)}, bf16[32,7,16,128]{3,2,1,0:T(8,128)(2,1)}, u32[]{:S(2)}, u32[]{:S(2)}) collective-permute-start(bf16[32,7,16,128]{3,2,1,0:T(8,128)(2,1)} %collective-permute-done.refs_1_), channel_id=1, source_target_pairs={{0,64},{1,65},{2,66},{3,67},{4,68},{5,69},{6,70},{7,71},{8,72},{9,... | collective-permute-start | bytes 2752520 | tf_op jit(solution)/shard_map/ppermute | solution.py:343
  113.4 44.2 %all-to-all-start.3 = ((bf16[16,14,16,128]{3,2,1,0:T(8,128)(2,1)}), bf16[16,14,16,128]{3,2,1,0:T(8,128)(2,1)S(1)}, u32[]{:S(2)}, u32[]{:S(2)}) async-start(bf16[16,14,16,128]{3,2,1,0:T(8,128)(2,1)} %get-tuple-element.25), calls=%async_computation.3 | async-start | bytes 1835008 | tf_op jit(solution)/shard_map/all_to_all | solution.py:349
  157.6 2.9 %collective-permute-start.10 = (bf16[16,14,16,128]{3,2,1,0:T(8,128)(2,1)}, bf16[16,14,16,128]{3,2,1,0:T(8,128)(2,1)S(1)}, u32[]{:S(2)}, u32[]{:S(2)}) collective-permute-start(bf16[16,14,16,128]{3,2,1,0:T(8,128)(2,1)} %get-tuple-element.36), channel_id=1, source_target_pairs={{0,1},{1,0},{2,3},{3,2},{4,5},{5,4},{6,7},{7,6},{8,9},{9,8},{10,11... | collective-permute-start | bytes 2752520 | tf_op jit(solution)/shard_map/ppermute | solution.py:343
  157.7 5.4 %copy-start.4 = (bf16[16,14,16,128]{3,2,1,0:T(8,128)(2,1)}, bf16[16,14,16,128]{3,2,1,0:T(8,128)(2,1)S(1)}, u32[]{:S(2)}) copy-start(bf16[16,14,16,128]{3,2,1,0:T(8,128)(2,1)S(1)} %all-to-all-done.3.near_ref) | copy-start | bytes 2752516
  157.7 13.5 %collective-permute-start.5 = (bf16[16,14,16,128]{3,2,1,0:T(8,128)(2,1)S(1)}, bf16[16,14,16,128]{3,2,1,0:T(8,128)(2,1)S(1)}, u32[]{:S(2)}, u32[]{:S(2)}) collective-permute-start(bf16[16,14,16,128]{3,2,1,0:T(8,128)(2,1)S(1)} %all-to-all-done.3.near_ref), channel_id=1, source_target_pairs={{0,1},{1,0},{2,3},{3,2},{4,5},{5,4},{6,7},{7,6},{8,9},{9,8},{10,11... | collective-permute-start | bytes 2752520 | tf_op jit(solution)/shard_map/ppermute | solution.py:343
  163.1 41.0 %all-to-all-start.5 = ((bf16[16,14,16,128]{3,2,1,0:T(8,128)(2,1)}), bf16[16,14,16,128]{3,2,1,0:T(8,128)(2,1)S(1)}, u32[]{:S(2)}, u32[]{:S(2)}) async-start(bf16[16,14,16,128]{3,2,1,0:T(8,128)(2,1)} %add_convert_fusion), calls=%async_computation.5 | async-start | bytes 1835008 | tf_op jit(solution)/shard_map/all_to_all | solution.py:349
  171.2 0.9 copy-start.5
  198.7 2.8 %collective-permute-start.9 = (bf16[16,14,16,128]{3,2,1,0:T(8,128)(2,1)}, bf16[16,14,16,128]{3,2,1,0:T(8,128)(2,1)S(1)}, u32[]{:S(2)}, u32[]{:S(2)}) collective-permute-start(bf16[16,14,16,128]{3,2,1,0:T(8,128)(2,1)} %get-tuple-element.34), channel_id=1, source_target_pairs={{0,1},{1,0},{2,3},{3,2},{4,5},{5,4},{6,7},{7,6},{8,9},{9,8},{10,11... | collective-permute-start | bytes 2752520 | tf_op jit(solution)/shard_map/ppermute | solution.py:343
  204.1 8.1 %copy-start = (bf16[16,14,16,128]{3,2,1,0:T(8,128)(2,1)}, bf16[16,14,16,128]{3,2,1,0:T(8,128)(2,1)S(1)}, u32[]{:S(2)}) copy-start(bf16[16,14,16,128]{3,2,1,0:T(8,128)(2,1)S(1)} %all-to-all-done.5.slab_ref) | copy-start | bytes 2752516
  204.1 32.8 %all-to-all-start.4 = ((bf16[16,14,16,128]{3,2,1,0:T(8,128)(2,1)}), bf16[16,14,16,128]{3,2,1,0:T(8,128)(2,1)S(1)}, u32[]{:S(2)}, u32[]{:S(2)}) async-start(bf16[16,14,16,128]{3,2,1,0:T(8,128)(2,1)} %add_convert_fusion.1), calls=%async_computation.4 | async-start | bytes 1835008 | tf_op jit(solution)/shard_map/all_to_all | solution.py:349
  236.9 0.9 copy-start.1

commit v4 on v3

--- a/solution.py
+++ b/solution.py
@@ -43,21 +43,12 @@
     return jnp.dot(a, b, preferred_element_type=F32)
 
 
-def pack_tiles(tiles, kept):
-    count, width = tiles.shape[-3], tiles.shape[-1]
-    free = LANES - width
-    thirds = [tiles[..., kept + k // 3, :, (k % 3) * free : (k % 3 + 1) * free] for k in range(3 * (count - kept))]
-    thirds += [jnp.zeros_like(thirds[0])] * (kept - len(thirds))
-    return jnp.concatenate([tiles[..., :kept, :, :], jnp.stack(thirds, axis=-3)], axis=-1)
-
-
-def packed_rows(rows):
+def packed_rows(rows, kept):
     width = rows[0].shape[1]
     free = LANES - width
-    last = len(rows) - SLAB
-    thirds = [rows[SLAB + k // 3][:, (k % 3) * free : (k % 3 + 1) * free] for k in range(3 * last)]
-    thirds += [jnp.zeros_like(thirds[0])] * (SLAB - len(thirds))
-    return [jnp.concatenate([rows[t], thirds[t]], axis=1) for t in range(SLAB)]
+    thirds = [rows[kept + k // 3][:, (k % 3) * free : (k % 3 + 1) * free] for k in range(3 * (len(rows) - kept))]
+    thirds += [jnp.zeros_like(thirds[0])] * (kept - len(thirds))
+    return [jnp.concatenate([rows[t], thirds[t]], axis=1) for t in range(kept)]
 
 
 def unpacked_rows(tiles, count, width):
@@ -66,9 +57,9 @@
     return [t[:, :width] for t in tiles] + spare
 
 
-def slab_planes(ref, chip, low, planes, length):
+def slab_planes(ref, chip, planes, length):
     per_plane = length // ROWS
-    rows = unpacked_rows([ref[chip, low + t] for t in range(SLAB)], planes * per_plane, length)
+    rows = unpacked_rows([ref[chip, t] for t in range(SLAB)], planes * per_plane, length)
     return [jnp.concatenate(rows[p * per_plane : (p + 1) * per_plane], axis=0) for p in range(planes)]
 
 
@@ -85,7 +76,7 @@
         levels = jnp.concatenate([index_ref[plane], blank], axis=1)
         here = jnp.take_along_axis(values, levels, axis=1, mode="promise_in_bounds")
         field.append(here[:, :width].astype(BF16))
-    field = packed_rows(slab_tiles(field))
+    field = packed_rows(slab_tiles(field), SLAB)
     chips = even_ref.shape[0]
     unroll = 4
 
@@ -95,7 +86,7 @@
             chip = step * unroll + k
             for which, ref in enumerate((even_ref, odd_ref)):
                 slab = [orbital_ref[2 * chip + which, p] for p in range(planes)]
-                for t, tile in enumerate(packed_rows(slab_tiles(slab))):
+                for t, tile in enumerate(packed_rows(slab_tiles(slab), SLAB)):
                     ref[chip, t] = tile
             for t in range(SLAB):
                 even_ref[chip, SLAB + t] = field[t]
@@ -133,7 +124,7 @@
                     source[number // 2, part * planes + plane, pl.ds(lows[number % 2], length // 2), :] = here
 
 
-def solve_pair(core, planes, orbital, source, fields, tables, scratch, finish):
+def solve_pair(core, planes, orbital, source, fields, tables, scratch, wait_fields, finish, step_done):
     near_ref, far_ref = orbital
     table_ref, double_ref = tables
     first, second = scratch
@@ -152,7 +143,7 @@
     def _(step):
         rows = []
         for chip, near, base in slabs_of(step):
-            for p, plane in enumerate(slab_planes(near_ref if near else far_ref, chip, 0, planes, length)):
+            for p, plane in enumerate(slab_planes(near_ref if near else far_ref, chip, planes, length)):
                 plane = jnp.concatenate([plane, blank], axis=1).astype(F32)
                 pair = [(source[s, base + p].astype(F32) * plane).astype(BF16) for s in range(2)]
                 rows.append(jnp.concatenate(pair, axis=1))
@@ -165,10 +156,12 @@
                 for s in range(2):
                     first[s, pl.ds(at, length), :] = section[:, HALVES[s]]
 
+    wait_fields()
+
     @pl.loop(0, chips // CHIP_GROUP)
     def _(step):
         for chip, near, base in slabs_of(step):
-            for p, field in enumerate(slab_planes(fields[0] if near else fields[1], chip, SLAB, planes, length)):
+            for p, field in enumerate(slab_planes(fields[0] if near else fields[1], chip, planes, length)):
                 field = jnp.concatenate([field, blank], axis=1).astype(F32)
                 row = base + p
                 values = [first[s, pl.ds(row, length, stride=PITCH), :].astype(BF16) for s in range(2)]
@@ -195,52 +188,92 @@
                 both = [source[s, base + p].astype(F32) * here[:, HALVES[s]] for s in range(2)]
                 terms.append(both[0] + both[1])
             finish(chip, near, base, terms)
+        step_done(step)
 
 
 def store_scaled(chip, near, sums, keep_ref, send_ref):
     length = sums[0].shape[0]
     rows = slab_tiles([(-EXCHANGE_FRACTION * value)[:, :length] for value in sums])
-    for t, tile in enumerate(packed_rows(rows)):
+    for t, tile in enumerate(packed_rows(rows, SLAB)):
         if near:
             keep_ref[chip, t] = tile
         else:
             send_ref[chip, t] = tile.astype(BF16)
 
 
-def first_kernel(last, planes, place_ref, near_ref, far_ref, *refs):
-    pieces, refs = refs[:4], refs[4:]
-    table_ref, double_ref = refs[:2]
-    refs = refs[2:]
+def started(pairs, semaphores, low):
+    copies = [pltpu.make_async_copy(*pair, semaphores.at[low + k]) for k, pair in enumerate(pairs)]
+    for copy in copies:
+        copy.start()
+    return copies
+
+
+def wait_for(copies):
+    for copy in copies:
+        copy.wait()
+
+
+def nothing(*_):
+    pass
+
+
+def first_kernel(last, planes, place_ref, *refs):
+    slabs_hbm, pieces_hbm, (table_ref, double_ref), refs = refs[:2], refs[2:6], refs[6:8], refs[8:]
     if last:
-        before_hbm, keep_ref, send_ref, source, first, second, before, semaphore = refs
-        before_copy = pltpu.make_async_copy(before_hbm, before, semaphore)
-        before_copy.start()
+        before_hbm, keep_ref, send_ref, *refs = refs
     else:
-        total_ref, source, first, second = refs
-    unpack_sources(place_ref, pieces, planes, source)
+        total_hbm, *refs = refs
+    slabs, pieces, source, first, second, total, semaphores = refs
+    piece_copies = started([(ref, pieces.at[k]) for k, ref in enumerate(pieces_hbm)], semaphores, 0)
+    slab_copies = started([(ref, slabs.at[k]) for k, ref in enumerate(slabs_hbm)], semaphores, 4)
     if last:
-        before_copy.wait()
+        total_copies = started([(before_hbm, total)], semaphores, 6)
+    wait_for(piece_copies)
+    unpack_sources(place_ref, [pieces.at[k] for k in range(4)], planes, source)
+    wait_for(slab_copies)
+    chunk = CHIP_GROUP * 2 * planes
+
+    def rows_out(step):
+        rows = pl.ds(pl.multiple_of(step * chunk, chunk), chunk)
+        return pltpu.make_async_copy(total.at[rows], total_hbm.at[rows], semaphores.at[6 + step])
+
+    def wait_fields():
+        if last:
+            wait_for(total_copies)
 
     def finish(chip, near, base, terms):
         if last:
-            sums = [before[base + p] + terms[p] for p in range(planes)]
+            sums = [total[base + p] + terms[p] for p in range(planes)]
             store_scaled(chip, near, sums, keep_ref, send_ref)
         else:
             for p in range(planes):
-                total_ref[base + p] = terms[p]
-
-    orbital = (near_ref, far_ref)
-    solve_pair(place_ref[0], planes, orbital, source, orbital, (table_ref, double_ref), (first, second), finish)
-
-
-def second_kernel(planes, place_ref, near_ref, far_ref, near_field, far_field, one_hbm, two_hbm, table_ref, double_ref,
-                  keep_ref, send_ref, sources, first, second, total, semaphores):
-    copies = [
-        pltpu.make_async_copy(ref, sources.at[k], semaphores.at[k]) for k, ref in enumerate((one_hbm, two_hbm))
-    ]
-    for copy in copies:
-        copy.start()
-    copies[0].wait()
+                total[base + p] = terms[p]
+
+    def step_done(step):
+        if not last:
+            rows_out(step).start()
+
+    orbital = [slabs.at[k, :, 0:SLAB] for k in range(2)]
+    fields = [slabs.at[k, :, SLAB : 2 * SLAB] for k in range(2)]
+    tables, scratch = (table_ref, double_ref), (first, second)
+    solve_pair(place_ref[0], planes, orbital, source, fields, tables, scratch, wait_fields, finish, step_done)
+    if not last:
+        for step in range(total.shape[0] // chunk):
+            rows_out(step).wait()
+
+
+def second_kernel(planes, place_ref, *refs):
+    slabs_hbm, other_hbm, pieces_hbm, (table_ref, double_ref), refs = refs[:2], refs[2:4], refs[4:12], refs[12:14], refs[14:]
+    keep_ref, send_ref, slabs, fields, pieces, source, first, second, total, semaphores = refs
+    piece_pairs = [(ref, pieces.at[k]) for k, ref in enumerate(pieces_hbm)]
+    first_pieces = started(piece_pairs[:4], semaphores, 0)
+    slab_copies = started([(ref, slabs.at[k]) for k, ref in enumerate(slabs_hbm)], semaphores, 4)
+    field_pairs = [(ref.at[:, SLAB : 2 * SLAB], fields.at[k]) for k, ref in enumerate(other_hbm)]
+    field_copies = started(field_pairs, semaphores, 6)
+    second_pieces = started(piece_pairs[4:], semaphores, 8)
+    wait_for(first_pieces)
+    unpack_sources(place_ref, [pieces.at[k] for k in range(4)], planes, source)
+    wait_for(slab_copies)
 
     def keep_total(chip, near, base, terms):
         for p in range(planes):
@@ -249,22 +282,27 @@
     def finish(chip, near, base, terms):
         store_scaled(chip, near, [total[base + p] + terms[p] for p in range(planes)], keep_ref, send_ref)
 
-    orbital, fields = (near_ref, far_ref), (near_field, far_field)
-    tables, scratch = (table_ref, double_ref), (first, second)
-    core = place_ref[0]
-    solve_pair(core, planes, orbital, sources.at[0], fields, tables, scratch, keep_total)
-    copies[1].wait()
-    solve_pair(core, planes, orbital, sources.at[1], fields, tables, scratch, finish)
-
-
-def solve_call(kernel, operands, in_hbm, outs, scratch, length, pairs):
-    vmem = pl.BlockSpec(memory_space=pltpu.VMEM)
-    specs = [pl.BlockSpec(memory_space=pl.ANY) if k in in_hbm else vmem for k in range(len(operands))]
-    specs[0] = pl.BlockSpec(memory_space=pltpu.SMEM)
+    given = [slabs.at[k] for k in range(2)], source, [fields.at[k] for k in range(2)]
+    given += (table_ref, double_ref), (first, second)
+    solve_pair(place_ref[0], planes, *given, lambda: wait_for(field_copies), keep_total, nothing)
+    wait_for(second_pieces)
+    unpack_sources(place_ref, [pieces.at[k] for k in range(4, 8)], planes, source)
+    solve_pair(place_ref[0], planes, *given, nothing, finish, nothing)
+
+
+def solve_call(kernel, place, in_hbm, table, outs, out_spec, slabs, pairs):
+    length = table.shape[0]
+    whole = (length, length, LANES)
+    hbm, vmem = pl.BlockSpec(memory_space=pl.ANY), pl.BlockSpec(memory_space=pltpu.VMEM)
+    before, after = in_hbm
+    section = pltpu.VMEM((2, (length + 1) * PITCH, LANES), F32)
+    piece = (pairs * 4, length // 3, PIECE, ROWS, LANES)
+    scratch = [pltpu.VMEM(shape, BF16) for shape in (*slabs, piece, (2,) + whole)]
+    scratch += [section, section, pltpu.VMEM(whole, F32), pltpu.SemaphoreType.DMA((12,))]
     return pl.pallas_call(
         kernel,
-        in_specs=specs,
-        out_specs=[vmem] * len(outs),
+        in_specs=[pl.BlockSpec(memory_space=pltpu.SMEM)] + [hbm] * len(before) + [vmem] * 2 + [hbm] * len(after),
+        out_specs=[out_spec] * len(outs),
         out_shape=outs,
         scratch_shapes=scratch,
         compiler_params=pltpu.CompilerParams(vmem_limit_bytes=VMEM_LIMIT),
@@ -272,47 +310,37 @@
             flops=144 * length**4 * pairs, bytes_accessed=8 * length**3, transcendentals=0
         ),
         name="solve",
-    )(*operands)
+    )(place, *before, table, double_table(table), *after)
 
 
 def solve_first(place, orbital, pieces, table, before, planes):
-    near, far = orbital
+    chips = orbital[0].shape[0]
     length = table.shape[0]
-    whole = (length, length, LANES)
     last = before is not None
-    operands = [place, near, far, *pieces, table, double_table(table)]
-    in_hbm = []
-    section = pltpu.VMEM((2, (length + 1) * PITCH, LANES), F32)
-    scratch = [section, section]
+    out_spec = pl.BlockSpec(memory_space=pltpu.VMEM if last else pl.ANY)
     if last:
-        in_hbm.append(len(operands))
-        operands.append(before)
-        scratch += [pltpu.VMEM(whole, F32), pltpu.SemaphoreType.DMA]
-        slab = (near.shape[0], SLAB) + near.shape[2:]
-        outs = [jax.ShapeDtypeStruct(slab, F32), jax.ShapeDtypeStruct(slab, BF16)]
+        outs = [jax.ShapeDtypeStruct((chips, SLAB, ROWS, LANES), kind) for kind in (F32, BF16)]
     else:
-        outs = [jax.ShapeDtypeStruct(whole, F32)]
-    outs.append(jax.ShapeDtypeStruct((2,) + whole, BF16))
-    return solve_call(functools.partial(first_kernel, last, planes), operands, in_hbm, outs, scratch, length, 1)
-
-
-def solve_second(place, orbital, field, sources, table, planes):
-    near, far = orbital
-    length = table.shape[0]
-    whole = (length, length, LANES)
-    section = pltpu.VMEM((2, (length + 1) * PITCH, LANES), F32)
-    outs = [jax.ShapeDtypeStruct(near.shape, F32), jax.ShapeDtypeStruct(near.shape, BF16)]
-    scratch = [pltpu.VMEM((2, 2) + whole, BF16), section, section, pltpu.VMEM(whole, F32)]
-    scratch.append(pltpu.SemaphoreType.DMA((2,)))
-    operands = [place, near, far, *field, *sources, table, double_table(table)]
-    return solve_call(functools.partial(second_kernel, planes), operands, (5, 6), outs, scratch, length, 2)
+        outs = [jax.ShapeDtypeStruct((length, length, LANES), F32)]
+    kernel = functools.partial(first_kernel, last, planes)
+    in_hbm = ([*orbital, *pieces], [before] if last else [])
+    return solve_call(kernel, place, in_hbm, table, outs, out_spec, [(2,) + orbital[0].shape], 1)
+
+
+def solve_second(place, orbital, other, pieces, table, planes):
+    shape = orbital[0].shape
+    outs = [jax.ShapeDtypeStruct(shape, kind) for kind in (F32, BF16)]
+    out_spec = pl.BlockSpec(memory_space=pltpu.VMEM)
+    in_hbm = ([*orbital, *other, *pieces], [])
+    kernel = functools.partial(second_kernel, planes)
+    return solve_call(kernel, place, in_hbm, table, outs, out_spec, [(2,) + shape] * 2, 2)
 
 
 def unpack_kernel(slab_ref, *refs):
     out_ref = refs[-1]
     planes, length = out_ref.shape[2:4]
     for chip in range(slab_ref.shape[0]):
-        for p, plane in enumerate(slab_planes(slab_ref, chip, 0, planes, length)):
+        for p, plane in enumerate(slab_planes(slab_ref, chip, planes, length)):
             out_ref[chip, 0, p] = plane
 
 
@@ -349,15 +377,38 @@
     return lax.all_to_all(value, BOTH, 0, 0, axis_index_groups=groups, tiled=True)
 
 
+def own_kernel(me_ref, owners_ref, chosen_ref, orbitals_hbm, out_ref, slabs, semaphores):
+    planes, length, width = slabs.shape[1:]
+    copies = []
+    for s in range(2):
+        row = jnp.int32(0)
+        for r in range(owners_ref.shape[0]):
+            row = jnp.where(owners_ref[r] == me_ref[0], chosen_ref[r, s], row)
+        copies.append(pltpu.make_async_copy(orbitals_hbm.at[row], slabs.at[s], semaphores.at[s]))
+        copies[s].start()
+    half = length // 2
+    for s in range(2):
+        copies[s].wait()
+        for h in range(2):
+            rows = slab_tiles([slabs[s, p, h * half : (h + 1) * half] for p in range(planes)])
+            for t, tile in enumerate(packed_rows(rows, PIECE)):
+                for band in range(h, out_ref.shape[0], 2):
+                    out_ref[band, s, t] = tile
+
+
 def own_pieces(orbitals, owners, chosen):
     me = lax.axis_index("band")
-    planes, length, width = orbitals.shape[1:]
-    rows = jnp.sum(jnp.where((owners == me)[:, None], chosen, 0), axis=0)
-    own = jnp.concatenate([lax.dynamic_slice_in_dim(orbitals, rows[s], 1) for s in range(2)], axis=0)
-    tiles = own.reshape(2, planes, 2, length // 2 // ROWS, ROWS, width)
-    tiles = tiles.transpose(2, 0, 1, 3, 4, 5).reshape(2, 2, planes * length // 2 // ROWS, ROWS, width)
-    packed = pack_tiles(tiles, PIECE)
-    received = lax.all_to_all(jnp.concatenate([packed] * 4, axis=0), "band", 0, 0, tiled=True)
+    bands = lax.axis_size("band")
+    smem = pl.BlockSpec(memory_space=pltpu.SMEM)
+    packed = pl.pallas_call(
+        own_kernel,
+        in_specs=[smem, smem, smem, pl.BlockSpec(memory_space=pl.ANY)],
+        out_specs=pl.BlockSpec(memory_space=pltpu.VMEM),
+        out_shape=jax.ShapeDtypeStruct((bands, 2, PIECE, ROWS, LANES), BF16),
+        scratch_shapes=[pltpu.VMEM((2,) + orbitals.shape[1:], BF16), pltpu.SemaphoreType.DMA((2,))],
+        name="own_pieces",
+    )(me.reshape(1), owners, chosen, orbitals)
+    received = lax.all_to_all(packed, "band", 0, 0, tiled=True)
     return lax.dynamic_index_in_dim(received, owners[me // 2], 0, keepdims=False)
 
 
@@ -388,12 +439,13 @@
     def finished(keep, send):
         return between_chips((keep + moved(send, core=1).astype(F32)).astype(BF16))
 
-    pieces = [own, across, opposite, opposite_across]
-    total, one = solve_first(place, even, pieces, table, None, planes)
-    pieces = [beside[0], beside_across[0], beside[1], beside_across[1]]
-    keep, send, two = solve_first(place, even, pieces, table, total, planes)
+    pairs = [[own, across, opposite, opposite_across]]
+    pairs.append([beside[0], beside_across[0], beside[1], beside_across[1]])
+    (total,) = solve_first(place, even, pairs[0], table, None, planes)
+    keep, send = solve_first(place, even, pairs[1], table, total, planes)
     result = unpack_slabs(finished(keep, send), 0, None, planes, length)
-    keep, send = solve_second(place, odd, even, (one, two), table, planes)
+    later, _ = lax.optimization_barrier((pairs[0] + pairs[1], send))
+    keep, send = solve_second(place, odd, even, later, table, planes)
     result = unpack_slabs(finished(keep, send), 1, result, planes, length)
     return result.reshape(orbitals.shape)
 

time: 242 us -> 235 us (0.971)
  between operations: 5.96 us -> 1.89 us
  other arithmetic: 8.5 us -> 5.92 us
    ppermute x11, starting transfers between devices: 10.2 us -> 12.6 us  [moved(): return lax.ppermute(value, BOTH, pairs)]
    pallas_call x3 -> x4, Pallas kernels: 62 us -> 60.9 us  [the longest x3 58.2 us: solve_call(): pl.pallas_call(kernel, in_specs=[pl.BlockSpec(memory_space=pltpu.SMEM)] +...]
  transfers between devices with their start and end apart: 17 -> 17, of which waited for: 9 -> 9; matrix products, arithmetic and copies ran while one was open for 3% -> 3% of each run, Pallas kernels for 29% -> 28%
where the time goes in v4:
time: 235 us; the launch traced here: 234 us
  waiting for transfers between devices  93.7 us (40%)
  Pallas kernels  69.7 us (30%)
  starting transfers between devices  58 us (25%)
  other arithmetic  5.92 us (3%)
  local copies, waits for them, and re-layouts  4.85 us (2%)
    pallas_call x3, Pallas kernels, solve_call(): pl.pallas_call(kernel, in_specs=[pl.BlockSpec(memory_space=pltpu.SMEM)] +...  58.2 us
    all_to_all x4, waiting for transfers between devices, between_chips(): lax.all_to_all(value, BOTH, 0, 0, axis_index_groups=groups, tiled=True)  37.5 us
    ppermute x11, waiting for transfers between devices, moved(): return lax.ppermute(value, BOTH, pairs)  28.7 us
    all_to_all x4, starting transfers between devices, between_chips(): lax.all_to_all(value, BOTH, 0, 0, axis_index_groups=groups, tiled=True)  28.4 us
    all_to_all x1, waiting for transfers between devices, on_device(): own = lax.all_to_all(copies, 'pw', 0, 0, tiled=True)  21.7 us
    ppermute x11, starting transfers between devices, moved(): return lax.ppermute(value, BOTH, pairs)  12.6 us
    all_to_all x1, starting transfers between devices, on_device(): own = lax.all_to_all(copies, 'pw', 0, 0, tiled=True)  9.49 us
    all_to_all x1, starting transfers between devices, own_pieces(): received = lax.all_to_all(packed, 'band', 0, 0, tiled=True)  7.44 us
  transfers between devices with their start and end apart: 17, of which 9 were waited for; matrix products, arithmetic and copies ran while one was open for 3% of the time, Pallas kernels for 28%

profile of v4, /device:TPU:4, one launch (start us, length us, event | category | flops | bytes accessed | tf_op | source)
XLA Modules:
  0.0 234.1 jit_solution(9297885165213078199)
XLA Ops:
  0.0 1.3 copy.11.chosen_ref
  1.3 0.0 copy-start.5
  1.3 2.7 %own_pieces.1 = bf16[8,2,7,16,128]{4,3,2,1,0:T(8,128)(2,1)} custom-call(s32[1]{0:T(128)} %bitcast.4.me_ref, s32[4]{0:T(128)} %owners_ref.1, s32[4,2]{1,0:T(4,128)} %copy.11.chosen_ref, bf16[32,3,96,96]{3,2,1,0:T(8,128)(2,1)} %orbitals_hbm.1), custom_call_target="tpu_custom_call" | custom-call | tf_op jit(solution)/shard_map/own_pieces/pallas_call | solution.py:403
  4.0 7.4 %all-to-all-start.1 = ((bf16[8,2,7,16,128]{4,3,2,1,0:T(8,128)(2,1)}), bf16[8,2,7,16,128]{4,3,2,1,0:T(8,128)(2,1)S(1)}, u32[]{:S(2)}, u32[]{:S(2)}) async-start(bf16[8,2,7,16,128]{4,3,2,1,0:T(8,128)(2,1)} %own_pieces.1), calls=%async_computation.1 | async-start | bytes 917504 | tf_op jit(solution)/shard_map/all_to_all | solution.py:411
  11.5 0.0 copy-done.5
  11.5 0.6 dynamic_slice.7
  13.8 5.9 %all-to-all-done.1 = bf16[8,2,7,16,128]{4,3,2,1,0:T(8,128)(2,1)S(1)} async-done(((bf16[8,2,7,16,128]{4,3,2,1,0:T(8,128)(2,1)}), bf16[8,2,7,16,128]{4,3,2,1,0:T(8,128)(2,1)S(1)}, u32[]{:S(2)}, u32[]{:S(2)}) %all-to-all-start.1) | async-done | bytes 458784 | tf_op jit(solution)/shard_map/all_to_all | solution.py:411
  19.7 1.1 broadcast_in_dim.9
  20.8 9.5 %all-to-all-start.2 = ((bf16[32,7,16,128]{3,2,1,0:T(8,128)(2,1)}), bf16[32,7,16,128]{3,2,1,0:T(8,128)(2,1)S(1)}, u32[]{:S(2)}, u32[]{:S(2)}) async-start(bf16[32,7,16,128]{3,2,1,0:T(8,128)(2,1)} %bitcast.7), calls=%async_computation.2 | async-start | bytes 1835008 | tf_op jit(solution)/shard_map/all_to_all | solution.py:423
  30.3 4.2 %pack.1 = (bf16[16,28,16,128]{3,2,1,0:T(8,128)(2,1)}, bf16[16,14,16,128]{3,2,1,0:T(8,128)(2,1)}) custom-call(bf16[32,3,96,96]{3,2,1,0:T(8,128)(2,1)} %orbitals_hbm.1, s32[3,96,96]{2,1,0:T(8,128)} %bitcast.10, f32[1,128]{1,0:T(1,128)} %bitcast.11), custom_call_target="tpu_custom_call" | custom-call | tf_op jit(solution)/shard_map/pack/pallas_call | solution.py:98
  34.5 21.7 %all-to-all-done.2.refs_2_.refs_4_ = bf16[32,7,16,128]{3,2,1,0:T(8,128)(2,1)S(1)} async-done(((bf16[32,7,16,128]{3,2,1,0:T(8,128)(2,1)}), bf16[32,7,16,128]{3,2,1,0:T(8,128)(2,1)S(1)}, u32[]{:S(2)}, u32[]{:S(2)}) %all-to-all-start.2) | async-done | bytes 917536 | tf_op jit(solution)/shard_map/all_to_all | solution.py:423
  56.2 0.0 copy-start.3
  56.2 3.7 %all-to-all-start = ((bf16[16,28,16,128]{3,2,1,0:T(8,128)(2,1)}), bf16[16,28,16,128]{3,2,1,0:T(8,128)(2,1)S(1)}, u32[]{:S(2)}, u32[]{:S(2)}) async-start(bf16[16,28,16,128]{3,2,1,0:T(8,128)(2,1)} %get-tuple-element.27), calls=%async_computation | async-start | bytes 3670016 | tf_op jit(solution)/shard_map/all_to_all | solution.py:377
  59.9 0.7 collective-permute-start.1
  60.6 2.6 %collective-permute-start = (bf16[32,7,16,128]{3,2,1,0:T(8,128)(2,1)S(1)}, bf16[32,7,16,128]{3,2,1,0:T(8,128)(2,1)}, u32[]{:S(2)}, u32[]{:S(2)}) collective-permute-start(bf16[32,7,16,128]{3,2,1,0:T(8,128)(2,1)S(1)} %all-to-all-done.2.refs_2_.refs_4_), channel_id=1, source_target_pairs={{0,48},{1,49},{2,50},{3,51},{4,52},{5,53},{6,54},{7,55},{8,56},{9,... | collective-permute-start | bytes 2752520 | tf_op jit(solution)/shard_map/ppermute | solution.py:371
  63.2 20.1 %collective-permute-done.1.refs_4_.refs_6_ = bf16[32,7,16,128]{3,2,1,0:T(8,128)(2,1)} collective-permute-done((bf16[32,7,16,128]{3,2,1,0:T(8,128)(2,1)S(1)}, bf16[32,7,16,128]{3,2,1,0:T(8,128)(2,1)}, u32[]{:S(2)}, u32[]{:S(2)}) %collective-permute-start.1) | collective-permute-done | bytes 917536 | tf_op jit(solution)/shard_map/ppermute | solution.py:371
  83.4 0.6 collective-permute-start.3
  83.9 0.0 copy-done.3
  83.9 2.7 %collective-permute-start.4 = (bf16[32,7,16,128]{3,2,1,0:T(8,128)(2,1)S(1)}, bf16[32,7,16,128]{3,2,1,0:T(8,128)(2,1)}, u32[]{:S(2)}, u32[]{:S(2)}) collective-permute-start(bf16[32,7,16,128]{3,2,1,0:T(8,128)(2,1)S(1)} %all-to-all-done.2.refs_2_.refs_4_), channel_id=1, source_target_pairs={{0,192},{1,193},{2,194},{3,195},{4,196},{5,197},{6,198},{7,199},{8... | collective-permute-start | bytes 2752520 | tf_op jit(solution)/shard_map/ppermute | solution.py:371
  86.6 2.2 collective-permute-start.2
  88.8 0.0 collective-permute-done.refs_3_.refs_5_
  88.8 15.1 %all-to-all-done.refs_0_.refs_2_ = bf16[16,28,16,128]{3,2,1,0:T(8,128)(2,1)S(1)} async-done(((bf16[16,28,16,128]{3,2,1,0:T(8,128)(2,1)}), bf16[16,28,16,128]{3,2,1,0:T(8,128)(2,1)S(1)}, u32[]{:S(2)}, u32[]{:S(2)}) %all-to-all-start) | async-done | bytes 1835040 | tf_op jit(solution)/shard_map/all_to_all | solution.py:377
  103.8 0.0 copy-start.2
  103.8 1.7 collective-permute-done.3.refs_2_.refs_8_
  105.5 0.0 collective-permute-done.4.refs_4_.refs_10_
  105.5 1.9 collective-permute-done.2.refs_5_.refs_7_
  107.4 0.0 collective-permute-start.6
  107.4 0.6 pad_add_fusion.place_ref
  108.1 0.0 collective-permute-start.7
  108.1 3.2 %collective-permute-start.8 = (bf16[32,7,16,128]{3,2,1,0:T(8,128)(2,1)}, bf16[32,7,16,128]{3,2,1,0:T(8,128)(2,1)}, u32[]{:S(2)}, u32[]{:S(2)}) collective-permute-start(bf16[32,7,16,128]{3,2,1,0:T(8,128)(2,1)} %collective-permute-done.refs_3_.refs_5_), channel_id=1, source_target_pairs={{0,192},{1,193},{2,194},{3,195},{4,196},{5,197},{6,198},{7,199},{8... | collective-permute-start | bytes 2752520 | tf_op jit(solution)/shard_map/ppermute | solution.py:371
  111.3 8.5 %all-to-all-start.3 = ((bf16[16,14,16,128]{3,2,1,0:T(8,128)(2,1)}), bf16[16,14,16,128]{3,2,1,0:T(8,128)(2,1)S(1)}, u32[]{:S(2)}, u32[]{:S(2)}) async-start(bf16[16,14,16,128]{3,2,1,0:T(8,128)(2,1)} %get-tuple-element.30), calls=%async_computation.3 | async-start | bytes 1835008 | tf_op jit(solution)/shard_map/all_to_all | solution.py:377
  119.8 0.0 collective-permute-done.6.refs_1_.refs_3_
  119.8 0.0 copy-done.2
  119.8 15.4 %solve.3.refs_8_ = f32[96,96,128]{2,1,0:T(8,128)} custom-call(s32[2]{0:T(128)} %pad_add_fusion.place_ref, bf16[16,28,16,128]{3,2,1,0:T(8,128)(2,1)} %copy-done.2, bf16[16,28,16,128]{3,2,1,0:T(8,128)(2,1)} %collective-permute-done.6.refs_1_.refs_3_, bf16[32,7,16,128]{3,2,1,0:T(8,128)(2,1)} %copy-done.3, ...), custom_call_target="tpu_custom_call" | custom-call | flops 12230590464 | bytes 7077888 | tf_op jit(solution)/shard_map/solve/pallas_call | solution.py:302
  135.2 0.0 collective-permute-done.7.refs_3_.refs_9_
  135.2 0.0 collective-permute-done.8.refs_5_.refs_11_
  135.3 16.0 %solve.4 = (f32[16,14,16,128]{3,2,1,0:T(8,128)}, bf16[16,14,16,128]{3,2,1,0:T(8,128)(2,1)}) custom-call(s32[2]{0:T(128)} %pad_add_fusion.place_ref, bf16[16,28,16,128]{3,2,1,0:T(8,128)(2,1)} %copy-done.2, bf16[16,28,16,128]{3,2,1,0:T(8,128)(2,1)} %collective-permute-done.6.refs_1_.refs_3_, bf16[32,7,16,128]{3,2,1,0:T(8,128)(2,1)} %collective-permute-done.3.refs_2_.refs_8_, ...), custom_call_target="tpu_custom_call" | custom-call | flops 12230590464 | bytes 7077888 | tf_op jit(solution)/shard_map/solve/pallas_call | solution.py:302
  151.3 0.1 collective-permute-start.10
  151.4 0.0 all-to-all-done.3.refs_0_
  151.4 0.0 copy-start.4
  151.4 0.5 collective-permute-start.5
  151.9 2.3 collective-permute-done.10
  154.2 2.6 %add_convert_fusion = bf16[16,14,16,128]{3,2,1,0:T(8,128)(2,1)} fusion(f32[16,14,16,128]{3,2,1,0:T(8,128)} %get-tuple-element.46, bf16[16,14,16,128]{3,2,1,0:T(8,128)(2,1)S(1)} %collective-permute-done.10), kind=kLoop, calls=%fused_computation | loop fusion | flops 1376256 | bytes 3670016 | tf_op jit(solution)/shard_map/convert_element_type | solution.py:440
  156.8 0.0 copy-done.4
  156.8 8.1 %all-to-all-start.5 = ((bf16[16,14,16,128]{3,2,1,0:T(8,128)(2,1)}), bf16[16,14,16,128]{3,2,1,0:T(8,128)(2,1)S(1)}, u32[]{:S(2)}, u32[]{:S(2)}) async-start(bf16[16,14,16,128]{3,2,1,0:T(8,128)(2,1)} %add_convert_fusion), calls=%async_computation.5 | async-start | bytes 1835008 | tf_op jit(solution)/shard_map/all_to_all | solution.py:377
  164.9 0.0 collective-permute-done.5.refs_1_
  164.9 0.0 copy-start.6
  164.9 0.9 copy-done.6
  165.9 26.8 %solve.5 = (f32[16,14,16,128]{3,2,1,0:T(8,128)}, bf16[16,14,16,128]{3,2,1,0:T(8,128)(2,1)}) custom-call(s32[2]{0:T(128)} %pad_add_fusion.place_ref, bf16[16,14,16,128]{3,2,1,0:T(8,128)(2,1)} %copy-done.4, bf16[16,14,16,128]{3,2,1,0:T(8,128)(2,1)} %copy-done.6, bf16[16,28,16,128]{3,2,1,0:T(8,128)(2,1)} %copy-done.2, ...), custom_call_target="tpu_custom_call" | custom-call | flops 24461180928 | bytes 7077888 | tf_op jit(solution)/shard_map/solve/pallas_call | solution.py:302
  192.7 0.1 collective-permute-start.9
  192.8 2.7 %collective-permute-done.9 = bf16[16,14,16,128]{3,2,1,0:T(8,128)(2,1)S(1)} collective-permute-done((bf16[16,14,16,128]{3,2,1,0:T(8,128)(2,1)}, bf16[16,14,16,128]{3,2,1,0:T(8,128)(2,1)S(1)}, u32[]{:S(2)}, u32[]{:S(2)}) %collective-permute-start.9) | collective-permute-done | bytes 917536 | tf_op jit(solution)/shard_map/ppermute | solution.py:371
  195.4 2.7 %add_convert_fusion.1 = bf16[16,14,16,128]{3,2,1,0:T(8,128)(2,1)} fusion(f32[16,14,16,128]{3,2,1,0:T(8,128)} %get-tuple-element.44, bf16[16,14,16,128]{3,2,1,0:T(8,128)(2,1)S(1)} %collective-permute-done.9), kind=kLoop, calls=%fused_computation.1 | loop fusion | flops 1376256 | bytes 3670016 | tf_op jit(solution)/shard_map/convert_element_type | solution.py:440
  198.1 0.0 all-to-all-done.5.slab_ref
  198.1 0.0 copy-start
  198.1 8.1 %all-to-all-start.4 = ((bf16[16,14,16,128]{3,2,1,0:T(8,128)(2,1)}), bf16[16,14,16,128]{3,2,1,0:T(8,128)(2,1)S(1)}, u32[]{:S(2)}, u32[]{:S(2)}) async-start(bf16[16,14,16,128]{3,2,1,0:T(8,128)(2,1)} %add_convert_fusion.1), calls=%async_computation.4 | async-start | bytes 1835008 | tf_op jit(solution)/shard_map/all_to_all | solution.py:377
  206.2 0.0 copy-done
  206.2 2.3 unpack.2.refs_0_
  208.5 22.4 %all-to-all-done.4.slab_ref = bf16[16,14,16,128]{3,2,1,0:T(8,128)(2,1)S(1)} async-done(((bf16[16,14,16,128]{3,2,1,0:T(8,128)(2,1)}), bf16[16,14,16,128]{3,2,1,0:T(8,128)(2,1)S(1)}, u32[]{:S(2)}, u32[]{:S(2)}) %all-to-all-start.4) | async-done | bytes 917536 | tf_op jit(solution)/shard_map/all_to_all | solution.py:377
  230.9 0.0 copy-start.1
  230.9 0.9 copy-done.1
  231.8 2.3 unpack.3
  (1 shorter events, 0.0 us)
Async XLA Ops:
  1.3 10.2 %copy-start.5 = (s32[4]{0:T(128)S(1)}, s32[4]{0:T(128)}, u32[]{:S(2)}) copy-start(s32[4]{0:T(128)} %owners_ref.1) | copy-start | bytes 52
  4.0 15.7 %all-to-all-start.1 = ((bf16[8,2,7,16,128]{4,3,2,1,0:T(8,128)(2,1)}), bf16[8,2,7,16,128]{4,3,2,1,0:T(8,128)(2,1)S(1)}, u32[]{:S(2)}, u32[]{:S(2)}) async-start(bf16[8,2,7,16,128]{4,3,2,1,0:T(8,128)(2,1)} %own_pieces.1), calls=%async_computation.1 | async-start | bytes 917504 | tf_op jit(solution)/shard_map/all_to_all | solution.py:411
  20.8 35.4 %all-to-all-start.2 = ((bf16[32,7,16,128]{3,2,1,0:T(8,128)(2,1)}), bf16[32,7,16,128]{3,2,1,0:T(8,128)(2,1)S(1)}, u32[]{:S(2)}, u32[]{:S(2)}) async-start(bf16[32,7,16,128]{3,2,1,0:T(8,128)(2,1)} %bitcast.7), calls=%async_computation.2 | async-start | bytes 1835008 | tf_op jit(solution)/shard_map/all_to_all | solution.py:423
  56.2 27.8 %copy-start.3 = (bf16[32,7,16,128]{3,2,1,0:T(8,128)(2,1)}, bf16[32,7,16,128]{3,2,1,0:T(8,128)(2,1)S(1)}, u32[]{:S(2)}) copy-start(bf16[32,7,16,128]{3,2,1,0:T(8,128)(2,1)S(1)} %all-to-all-done.2.refs_2_.refs_4_) | copy-start | bytes 2752516
  56.2 47.7 %all-to-all-start = ((bf16[16,28,16,128]{3,2,1,0:T(8,128)(2,1)}), bf16[16,28,16,128]{3,2,1,0:T(8,128)(2,1)S(1)}, u32[]{:S(2)}, u32[]{:S(2)}) async-start(bf16[16,28,16,128]{3,2,1,0:T(8,128)(2,1)} %get-tuple-element.27), calls=%async_computation | async-start | bytes 3670016 | tf_op jit(solution)/shard_map/all_to_all | solution.py:377
  59.9 23.5 %collective-permute-start.1 = (bf16[32,7,16,128]{3,2,1,0:T(8,128)(2,1)S(1)}, bf16[32,7,16,128]{3,2,1,0:T(8,128)(2,1)}, u32[]{:S(2)}, u32[]{:S(2)}) collective-permute-start(bf16[32,7,16,128]{3,2,1,0:T(8,128)(2,1)S(1)} %all-to-all-done.2.refs_2_.refs_4_), channel_id=1, source_target_pairs={{0,128},{1,129},{2,130},{3,131},{4,132},{5,133},{6,134},{7,135},{8... | collective-permute-start | bytes 2752520 | tf_op jit(solution)/shard_map/ppermute | solution.py:371
  60.6 28.1 %collective-permute-start = (bf16[32,7,16,128]{3,2,1,0:T(8,128)(2,1)S(1)}, bf16[32,7,16,128]{3,2,1,0:T(8,128)(2,1)}, u32[]{:S(2)}, u32[]{:S(2)}) collective-permute-start(bf16[32,7,16,128]{3,2,1,0:T(8,128)(2,1)S(1)} %all-to-all-done.2.refs_2_.refs_4_), channel_id=1, source_target_pairs={{0,48},{1,49},{2,50},{3,51},{4,52},{5,53},{6,54},{7,55},{8,56},{9,... | collective-permute-start | bytes 2752520 | tf_op jit(solution)/shard_map/ppermute | solution.py:371
  83.4 22.2 %collective-permute-start.3 = (bf16[32,7,16,128]{3,2,1,0:T(8,128)(2,1)S(1)}, bf16[32,7,16,128]{3,2,1,0:T(8,128)(2,1)}, u32[]{:S(2)}, u32[]{:S(2)}) collective-permute-start(bf16[32,7,16,128]{3,2,1,0:T(8,128)(2,1)S(1)} %all-to-all-done.2.refs_2_.refs_4_), channel_id=1, source_target_pairs={{0,64},{1,65},{2,66},{3,67},{4,68},{5,69},{6,70},{7,71},{8,72},{9,... | collective-permute-start | bytes 2752520 | tf_op jit(solution)/shard_map/ppermute | solution.py:371
  83.9 21.6 %collective-permute-start.4 = (bf16[32,7,16,128]{3,2,1,0:T(8,128)(2,1)S(1)}, bf16[32,7,16,128]{3,2,1,0:T(8,128)(2,1)}, u32[]{:S(2)}, u32[]{:S(2)}) collective-permute-start(bf16[32,7,16,128]{3,2,1,0:T(8,128)(2,1)S(1)} %all-to-all-done.2.refs_2_.refs_4_), channel_id=1, source_target_pairs={{0,192},{1,193},{2,194},{3,195},{4,196},{5,197},{6,198},{7,199},{8... | collective-permute-start | bytes 2752520 | tf_op jit(solution)/shard_map/ppermute | solution.py:371
  86.6 20.8 %collective-permute-start.2 = (bf16[32,7,16,128]{3,2,1,0:T(8,128)(2,1)}, bf16[32,7,16,128]{3,2,1,0:T(8,128)(2,1)}, u32[]{:S(2)}, u32[]{:S(2)}) collective-permute-start(bf16[32,7,16,128]{3,2,1,0:T(8,128)(2,1)} %collective-permute-done.1.refs_4_.refs_6_), channel_id=1, source_target_pairs={{0,48},{1,49},{2,50},{3,51},{4,52},{5,53},{6,54},{7,55},{8,56},{9,... | collective-permute-start | bytes 2752520 | tf_op jit(solution)/shard_map/ppermute | solution.py:371
  103.8 16.0 %copy-start.2 = (bf16[16,28,16,128]{3,2,1,0:T(8,128)(2,1)}, bf16[16,28,16,128]{3,2,1,0:T(8,128)(2,1)S(1)}, u32[]{:S(2)}) copy-start(bf16[16,28,16,128]{3,2,1,0:T(8,128)(2,1)S(1)} %all-to-all-done.refs_0_.refs_2_) | copy-start | bytes 5505028
  107.4 12.4 %collective-permute-start.6 = (bf16[16,28,16,128]{3,2,1,0:T(8,128)(2,1)S(1)}, bf16[16,28,16,128]{3,2,1,0:T(8,128)(2,1)}, u32[]{:S(2)}, u32[]{:S(2)}) collective-permute-start(bf16[16,28,16,128]{3,2,1,0:T(8,128)(2,1)S(1)} %all-to-all-done.refs_0_.refs_2_), channel_id=1, source_target_pairs={{0,1},{1,0},{2,3},{3,2},{4,5},{5,4},{6,7},{7,6},{8,9},{9,8},{10,11... | collective-permute-start | bytes 5505032 | tf_op jit(solution)/shard_map/ppermute | solution.py:371
  108.1 27.2 %collective-permute-start.7 = (bf16[32,7,16,128]{3,2,1,0:T(8,128)(2,1)}, bf16[32,7,16,128]{3,2,1,0:T(8,128)(2,1)}, u32[]{:S(2)}, u32[]{:S(2)}) collective-permute-start(bf16[32,7,16,128]{3,2,1,0:T(8,128)(2,1)} %collective-permute-done.refs_3_.refs_5_), channel_id=1, source_target_pairs={{0,64},{1,65},{2,66},{3,67},{4,68},{5,69},{6,70},{7,71},{8,72},{9,... | collective-permute-start | bytes 2752520 | tf_op jit(solution)/shard_map/ppermute | solution.py:371
  108.1 27.2 %collective-permute-start.8 = (bf16[32,7,16,128]{3,2,1,0:T(8,128)(2,1)}, bf16[32,7,16,128]{3,2,1,0:T(8,128)(2,1)}, u32[]{:S(2)}, u32[]{:S(2)}) collective-permute-start(bf16[32,7,16,128]{3,2,1,0:T(8,128)(2,1)} %collective-permute-done.refs_3_.refs_5_), channel_id=1, source_target_pairs={{0,192},{1,193},{2,194},{3,195},{4,196},{5,197},{6,198},{7,199},{8... | collective-permute-start | bytes 2752520 | tf_op jit(solution)/shard_map/ppermute | solution.py:371
  111.3 40.1 %all-to-all-start.3 = ((bf16[16,14,16,128]{3,2,1,0:T(8,128)(2,1)}), bf16[16,14,16,128]{3,2,1,0:T(8,128)(2,1)S(1)}, u32[]{:S(2)}, u32[]{:S(2)}) async-start(bf16[16,14,16,128]{3,2,1,0:T(8,128)(2,1)} %get-tuple-element.30), calls=%async_computation.3 | async-start | bytes 1835008 | tf_op jit(solution)/shard_map/all_to_all | solution.py:377
  151.3 2.9 %collective-permute-start.10 = (bf16[16,14,16,128]{3,2,1,0:T(8,128)(2,1)}, bf16[16,14,16,128]{3,2,1,0:T(8,128)(2,1)S(1)}, u32[]{:S(2)}, u32[]{:S(2)}) collective-permute-start(bf16[16,14,16,128]{3,2,1,0:T(8,128)(2,1)} %get-tuple-element.35), channel_id=1, source_target_pairs={{0,1},{1,0},{2,3},{3,2},{4,5},{5,4},{6,7},{7,6},{8,9},{9,8},{10,11... | collective-permute-start | bytes 2752520 | tf_op jit(solution)/shard_map/ppermute | solution.py:371
  151.4 5.4 %copy-start.4 = (bf16[16,14,16,128]{3,2,1,0:T(8,128)(2,1)}, bf16[16,14,16,128]{3,2,1,0:T(8,128)(2,1)S(1)}, u32[]{:S(2)}) copy-start(bf16[16,14,16,128]{3,2,1,0:T(8,128)(2,1)S(1)} %all-to-all-done.3.refs_0_) | copy-start | bytes 2752516
  151.4 13.5 %collective-permute-start.5 = (bf16[16,14,16,128]{3,2,1,0:T(8,128)(2,1)S(1)}, bf16[16,14,16,128]{3,2,1,0:T(8,128)(2,1)S(1)}, u32[]{:S(2)}, u32[]{:S(2)}) collective-permute-start(bf16[16,14,16,128]{3,2,1,0:T(8,128)(2,1)S(1)} %all-to-all-done.3.refs_0_), channel_id=1, source_target_pairs={{0,1},{1,0},{2,3},{3,2},{4,5},{5,4},{6,7},{7,6},{8,9},{9,8},{10,11... | collective-permute-start | bytes 2752520 | tf_op jit(solution)/shard_map/ppermute | solution.py:371
  156.8 41.3 %all-to-all-start.5 = ((bf16[16,14,16,128]{3,2,1,0:T(8,128)(2,1)}), bf16[16,14,16,128]{3,2,1,0:T(8,128)(2,1)S(1)}, u32[]{:S(2)}, u32[]{:S(2)}) async-start(bf16[16,14,16,128]{3,2,1,0:T(8,128)(2,1)} %add_convert_fusion), calls=%async_computation.5 | async-start | bytes 1835008 | tf_op jit(solution)/shard_map/all_to_all | solution.py:377
  164.9 0.9 copy-start.6
  192.7 2.8 %collective-permute-start.9 = (bf16[16,14,16,128]{3,2,1,0:T(8,128)(2,1)}, bf16[16,14,16,128]{3,2,1,0:T(8,128)(2,1)S(1)}, u32[]{:S(2)}, u32[]{:S(2)}) collective-permute-start(bf16[16,14,16,128]{3,2,1,0:T(8,128)(2,1)} %get-tuple-element.45), channel_id=1, source_target_pairs={{0,1},{1,0},{2,3},{3,2},{4,5},{5,4},{6,7},{7,6},{8,9},{9,8},{10,11... | collective-permute-start | bytes 2752520 | tf_op jit(solution)/shard_map/ppermute | solution.py:371
  198.1 8.1 %copy-start = (bf16[16,14,16,128]{3,2,1,0:T(8,128)(2,1)}, bf16[16,14,16,128]{3,2,1,0:T(8,128)(2,1)S(1)}, u32[]{:S(2)}) copy-start(bf16[16,14,16,128]{3,2,1,0:T(8,128)(2,1)S(1)} %all-to-all-done.5.slab_ref) | copy-start | bytes 2752516
  198.1 32.8 %all-to-all-start.4 = ((bf16[16,14,16,128]{3,2,1,0:T(8,128)(2,1)}), bf16[16,14,16,128]{3,2,1,0:T(8,128)(2,1)S(1)}, u32[]{:S(2)}, u32[]{:S(2)}) async-start(bf16[16,14,16,128]{3,2,1,0:T(8,128)(2,1)} %add_convert_fusion.1), calls=%async_computation.4 | async-start | bytes 1835008 | tf_op jit(solution)/shard_map/all_to_all | solution.py:377
  230.9 0.9 copy-start.1

commit v5 on v4

--- a/solution.py
+++ b/solution.py
@@ -18,7 +18,8 @@
 ROWS = 16
 SLAB = 14
 PIECE = 7
-VMEM_LIMIT = 60 * 2**20
+VMEM_LIMIT = 49 * 2**20
+SMALL_LIMIT = 16 * 2**20
 PITCH = 104
 CHIP_GROUP = 8
 BOTH = ("band", "pw")
@@ -100,7 +101,7 @@
         in_specs=[vmem] * 3,
         out_specs=[vmem] * 2,
         out_shape=[jax.ShapeDtypeStruct((chips, n * SLAB, ROWS, LANES), BF16) for n in (2, 1)],
-        compiler_params=pltpu.CompilerParams(vmem_limit_bytes=VMEM_LIMIT),
+        compiler_params=pltpu.CompilerParams(vmem_limit_bytes=SMALL_LIMIT),
         name="pack",
     )(orbitals, shell_index, shell_kernel.reshape(1, LANES))
 
@@ -301,7 +302,7 @@
     scratch += [section, section, pltpu.VMEM(whole, F32), pltpu.SemaphoreType.DMA((12,))]
     return pl.pallas_call(
         kernel,
-        in_specs=[pl.BlockSpec(memory_space=pltpu.SMEM)] + [hbm] * len(before) + [vmem] * 2 + [hbm] * len(after),
+        in_specs=[pl.BlockSpec(memory_space=pltpu.SMEM), *[hbm] * len(before), vmem, vmem] + [hbm] * len(after),
         out_specs=[out_spec] * len(outs),
         out_shape=outs,
         scratch_shapes=scratch,
@@ -336,27 +337,32 @@
     return solve_call(kernel, place, in_hbm, table, outs, out_spec, [(2,) + shape] * 2, 2)
 
 
-def unpack_kernel(slab_ref, *refs):
+def unpack_kernel(steps, slabs_ref, *refs):
     out_ref = refs[-1]
     planes, length = out_ref.shape[2:4]
-    for chip in range(slab_ref.shape[0]):
-        for p, plane in enumerate(slab_planes(slab_ref, chip, planes, length)):
-            out_ref[chip, 0, p] = plane
+    chips = slabs_ref.shape[0] // steps
+    step = pl.program_id(0)
+    for k in range(steps):
+
+        @pl.when(step == k)
+        def _():
+            for chip in range(chips):
+                for p, plane in enumerate(slab_planes(slabs_ref, k * chips + chip, planes, length)):
+                    out_ref[chip, 0, p] = plane
 
 
 def unpack_slabs(slabs, which, before, planes, length):
     chips = slabs.shape[0]
     steps = 2
-    block = pl.BlockSpec((chips // steps,) + slabs.shape[1:], lambda i: (i, 0, 0, 0))
     given = [] if before is None else [before]
     return pl.pallas_call(
-        unpack_kernel,
+        functools.partial(unpack_kernel, steps),
         grid=(steps,),
-        in_specs=[block] + [pl.BlockSpec(memory_space=pl.ANY)] * len(given),
+        in_specs=[pl.BlockSpec(memory_space=pltpu.VMEM)] + [pl.BlockSpec(memory_space=pl.ANY)] * len(given),
         out_specs=pl.BlockSpec((chips // steps, 1, planes, length, length), lambda i: (i, which, 0, 0, 0)),
         out_shape=jax.ShapeDtypeStruct((chips, 2, planes, length, length), BF16),
         input_output_aliases={1: 0} if given else {},
-        compiler_params=pltpu.CompilerParams(vmem_limit_bytes=VMEM_LIMIT),
+        compiler_params=pltpu.CompilerParams(vmem_limit_bytes=SMALL_LIMIT),
         name="unpack",
     )(slabs, *given)
 
@@ -377,13 +383,13 @@
     return lax.all_to_all(value, BOTH, 0, 0, axis_index_groups=groups, tiled=True)
 
 
-def own_kernel(me_ref, owners_ref, chosen_ref, orbitals_hbm, out_ref, slabs, semaphores):
+def own_kernel(place_ref, owners_ref, chosen_ref, orbitals_hbm, out_ref, slabs, semaphores):
     planes, length, width = slabs.shape[1:]
     copies = []
     for s in range(2):
         row = jnp.int32(0)
         for r in range(owners_ref.shape[0]):
-            row = jnp.where(owners_ref[r] == me_ref[0], chosen_ref[r, s], row)
+            row = jnp.where(owners_ref[r] == place_ref[2], chosen_ref[r, s], row)
         copies.append(pltpu.make_async_copy(orbitals_hbm.at[row], slabs.at[s], semaphores.at[s]))
         copies[s].start()
     half = length // 2
@@ -396,7 +402,7 @@
                     out_ref[band, s, t] = tile
 
 
-def own_pieces(orbitals, owners, chosen):
+def own_pieces(place, orbitals, owners, chosen):
     me = lax.axis_index("band")
     bands = lax.axis_size("band")
     smem = pl.BlockSpec(memory_space=pltpu.SMEM)
@@ -407,7 +413,7 @@
         out_shape=jax.ShapeDtypeStruct((bands, 2, PIECE, ROWS, LANES), BF16),
         scratch_shapes=[pltpu.VMEM((2,) + orbitals.shape[1:], BF16), pltpu.SemaphoreType.DMA((2,))],
         name="own_pieces",
-    )(me.reshape(1), owners, chosen, orbitals)
+    )(place, owners, chosen, orbitals)
     received = lax.all_to_all(packed, "band", 0, 0, tiled=True)
     return lax.dynamic_index_in_dim(received, owners[me // 2], 0, keepdims=False)
 
@@ -416,9 +422,9 @@
     band, part = lax.axis_index("band"), lax.axis_index("pw")
     count, planes, length, width = orbitals.shape
     table = cas_table(length)
-    place = jnp.stack([part % 2, band % 2])
-
-    pieces = own_pieces(orbitals, owners, chosen)
+    place = jnp.stack([part % 2, band % 2, band])
+
+    pieces = own_pieces(place, orbitals, owners, chosen)
     copies = jnp.broadcast_to(pieces[None], (count // 2,) + pieces.shape).reshape((count,) + pieces.shape[1:])
     own = lax.all_to_all(copies, "pw", 0, 0, tiled=True)
     across = moved(own, mirror=True)

time: 235 us -> 229 us (0.974)
  Pallas kernels: 69.7 us -> 63.2 us
    pallas_call x5, Pallas kernels: 62.8 us -> 58.6 us  [the longest x3 56 us: solve_call(): pl.pallas_call(kernel, in_specs=[pl.BlockSpec(memory_space=pltpu.SMEM), *...]
  transfers between devices with their start and end apart: 17 -> 17, of which waited for: 9 -> 9; matrix products, arithmetic and copies ran while one was open for 3% -> 3% of each run, Pallas kernels for 28% -> 26%
where the time goes in v5:
time: 229 us; the launch traced here: 228 us
  waiting for transfers between devices  92.6 us (40%)
  Pallas kernels  63.2 us (28%)
  starting transfers between devices  58.9 us (26%)
  other arithmetic  6.09 us (3%)
  local copies, waits for them, and re-layouts  5.27 us (2%)
  between operations  2.29 us (1%)
    pallas_call x3, Pallas kernels, solve_call(): pl.pallas_call(kernel, in_specs=[pl.BlockSpec(memory_space=pltpu.SMEM), *...  56 us
    all_to_all x4, waiting for transfers between devices, between_chips(): lax.all_to_all(value, BOTH, 0, 0, axis_index_groups=groups, tiled=True)  38 us
    all_to_all x4, starting transfers between devices, between_chips(): lax.all_to_all(value, BOTH, 0, 0, axis_index_groups=groups, tiled=True)  29.2 us
    ppermute x11, waiting for transfers between devices, moved(): return lax.ppermute(value, BOTH, pairs)  26.3 us
    all_to_all x1, waiting for transfers between devices, on_device(): own = lax.all_to_all(copies, 'pw', 0, 0, tiled=True)  22.8 us
    ppermute x11, starting transfers between devices, moved(): return lax.ppermute(value, BOTH, pairs)  12.7 us
    all_to_all x1, starting transfers between devices, on_device(): own = lax.all_to_all(copies, 'pw', 0, 0, tiled=True)  9.49 us
    all_to_all x1, starting transfers between devices, own_pieces(): received = lax.all_to_all(packed, 'band', 0, 0, tiled=True)  7.58 us
  transfers between devices with their start and end apart: 17, of which 9 were waited for; matrix products, arithmetic and copies ran while one was open for 3% of the time, Pallas kernels for 26%

profile of v5, /device:TPU:4, one launch (start us, length us, event | category | flops | bytes accessed | tf_op | source)
XLA Modules:
  0.0 228.3 jit_solution(13207722615315712581)
XLA Ops:
  0.0 1.3 copy.11.chosen_ref
  1.3 0.6 pad_add_fusion.place_ref
  2.0 2.7 %own_pieces.1 = bf16[8,2,7,16,128]{4,3,2,1,0:T(8,128)(2,1)} custom-call(s32[3]{0:T(128)} %pad_add_fusion.place_ref, s32[4]{0:T(128)} %owners_ref.1, s32[4,2]{1,0:T(4,128)} %copy.11.chosen_ref, bf16[32,3,96,96]{3,2,1,0:T(8,128)(2,1)} %orbitals_hbm.1), custom_call_target="tpu_custom_call" | custom-call | tf_op jit(solution)/shard_map/own_pieces/pallas_call | solution.py:409
  4.7 0.0 copy-start
  4.7 0.0 copy-start.2
  4.7 0.0 copy-start.4
  4.7 7.6 %all-to-all-start.1 = ((bf16[8,2,7,16,128]{4,3,2,1,0:T(8,128)(2,1)}), bf16[8,2,7,16,128]{4,3,2,1,0:T(8,128)(2,1)S(1)}, u32[]{:S(2)}, u32[]{:S(2)}) async-start(bf16[8,2,7,16,128]{4,3,2,1,0:T(8,128)(2,1)} %own_pieces.1), calls=%async_computation.1 | async-start | bytes 917504 | tf_op jit(solution)/shard_map/all_to_all | solution.py:417
  12.3 0.0 copy-done.10
  12.3 0.6 dynamic_slice.7
  15.0 5.5 %all-to-all-done.1 = bf16[8,2,7,16,128]{4,3,2,1,0:T(8,128)(2,1)S(1)} async-done(((bf16[8,2,7,16,128]{4,3,2,1,0:T(8,128)(2,1)}), bf16[8,2,7,16,128]{4,3,2,1,0:T(8,128)(2,1)S(1)}, u32[]{:S(2)}, u32[]{:S(2)}) %all-to-all-start.1) | async-done | bytes 458784 | tf_op jit(solution)/shard_map/all_to_all | solution.py:417
  20.5 1.1 broadcast_in_dim.9
  21.6 9.5 %all-to-all-start.2 = ((bf16[32,7,16,128]{3,2,1,0:T(8,128)(2,1)}), bf16[32,7,16,128]{3,2,1,0:T(8,128)(2,1)S(1)}, u32[]{:S(2)}, u32[]{:S(2)}) async-start(bf16[32,7,16,128]{3,2,1,0:T(8,128)(2,1)} %bitcast.12), calls=%async_computation.2 | async-start | bytes 1835008 | tf_op jit(solution)/shard_map/all_to_all | solution.py:429
  31.1 0.0 copy-done
  31.1 0.0 copy-done.2
  31.1 0.0 copy-done.4
  31.1 1.9 pack.1
  33.0 1.2 copy-done.1
  34.2 22.8 %all-to-all-done.2.refs_2_.refs_4_ = bf16[32,7,16,128]{3,2,1,0:T(8,128)(2,1)S(1)} async-done(((bf16[32,7,16,128]{3,2,1,0:T(8,128)(2,1)}), bf16[32,7,16,128]{3,2,1,0:T(8,128)(2,1)S(1)}, u32[]{:S(2)}, u32[]{:S(2)}) %all-to-all-start.2) | async-done | bytes 917536 | tf_op jit(solution)/shard_map/all_to_all | solution.py:429
  57.0 4.4 %all-to-all-start = ((bf16[16,28,16,128]{3,2,1,0:T(8,128)(2,1)}), bf16[16,28,16,128]{3,2,1,0:T(8,128)(2,1)}, u32[]{:S(2)}, u32[]{:S(2)}) async-start(bf16[16,28,16,128]{3,2,1,0:T(8,128)(2,1)} %copy-done.1), calls=%async_computation | async-start | bytes 3670016 | tf_op jit(solution)/shard_map/all_to_all | solution.py:383
  61.4 0.0 copy-start.3
  61.4 0.0 copy-start.8
  61.4 0.0 copy-start.9
  61.4 0.7 collective-permute-start.1
  62.2 2.6 %collective-permute-start = (bf16[32,7,16,128]{3,2,1,0:T(8,128)(2,1)S(1)}, bf16[32,7,16,128]{3,2,1,0:T(8,128)(2,1)}, u32[]{:S(2)}, u32[]{:S(2)}) collective-permute-start(bf16[32,7,16,128]{3,2,1,0:T(8,128)(2,1)S(1)} %all-to-all-done.2.refs_2_.refs_4_), channel_id=1, source_target_pairs={{0,48},{1,49},{2,50},{3,51},{4,52},{5,53},{6,54},{7,55},{8,56},{9,... | collective-permute-start | bytes 2752520 | tf_op jit(solution)/shard_map/ppermute | solution.py:377
  64.8 19.4 %collective-permute-done.1.refs_4_.refs_6_ = bf16[32,7,16,128]{3,2,1,0:T(8,128)(2,1)S(1)} collective-permute-done((bf16[32,7,16,128]{3,2,1,0:T(8,128)(2,1)S(1)}, bf16[32,7,16,128]{3,2,1,0:T(8,128)(2,1)S(1)}, u32[]{:S(2)}, u32[]{:S(2)}) %collective-permute-start.1) | collective-permute-done | bytes 917536 | tf_op jit(solution)/shard_map/ppermute | solution.py:377
  84.1 0.6 collective-permute-start.3
  84.7 2.7 %collective-permute-start.4 = (bf16[32,7,16,128]{3,2,1,0:T(8,128)(2,1)S(1)}, bf16[32,7,16,128]{3,2,1,0:T(8,128)(2,1)}, u32[]{:S(2)}, u32[]{:S(2)}) collective-permute-start(bf16[32,7,16,128]{3,2,1,0:T(8,128)(2,1)S(1)} %all-to-all-done.2.refs_2_.refs_4_), channel_id=1, source_target_pairs={{0,192},{1,193},{2,194},{3,195},{4,196},{5,197},{6,198},{7,199},{8... | collective-permute-start | bytes 2752520 | tf_op jit(solution)/shard_map/ppermute | solution.py:377
  87.4 2.2 collective-permute-start.2
  89.6 0.0 collective-permute-done.refs_3_.refs_5_
  89.6 14.6 %all-to-all-done.refs_0_.refs_2_ = bf16[16,28,16,128]{3,2,1,0:T(8,128)(2,1)} async-done(((bf16[16,28,16,128]{3,2,1,0:T(8,128)(2,1)}), bf16[16,28,16,128]{3,2,1,0:T(8,128)(2,1)}, u32[]{:S(2)}, u32[]{:S(2)}) %all-to-all-start) | async-done | bytes 1835040 | tf_op jit(solution)/shard_map/all_to_all | solution.py:383
  104.1 1.5 collective-permute-done.3.refs_2_.refs_8_
  105.7 0.9 copy-done.6
  106.6 0.0 collective-permute-done.4.refs_4_.refs_10_
  106.6 0.9 collective-permute-done.2.refs_5_.refs_7_
  107.5 0.0 collective-permute-start.6
  107.5 0.0 collective-permute-start.7
  107.5 3.2 %collective-permute-start.8 = (bf16[32,7,16,128]{3,2,1,0:T(8,128)(2,1)}, bf16[32,7,16,128]{3,2,1,0:T(8,128)(2,1)}, u32[]{:S(2)}, u32[]{:S(2)}) collective-permute-start(bf16[32,7,16,128]{3,2,1,0:T(8,128)(2,1)} %collective-permute-done.refs_3_.refs_5_), channel_id=1, source_target_pairs={{0,192},{1,193},{2,194},{3,195},{4,196},{5,197},{6,198},{7,199},{8... | collective-permute-start | bytes 2752520 | tf_op jit(solution)/shard_map/ppermute | solution.py:377
  110.7 8.5 %all-to-all-start.3 = ((bf16[16,14,16,128]{3,2,1,0:T(8,128)(2,1)}), bf16[16,14,16,128]{3,2,1,0:T(8,128)(2,1)S(1)}, u32[]{:S(2)}, u32[]{:S(2)}) async-start(bf16[16,14,16,128]{3,2,1,0:T(8,128)(2,1)} %get-tuple-element.30), calls=%async_computation.3 | async-start | bytes 1835008 | tf_op jit(solution)/shard_map/all_to_all | solution.py:383
  119.3 0.0 copy-start.7
  119.3 0.0 collective-permute-done.6.refs_1_.refs_3_
  119.3 0.0 copy-done.3
  119.3 0.0 copy-done.8
  119.3 0.0 copy-done.9
  119.3 14.7 %solve.3.refs_8_ = f32[96,96,128]{2,1,0:T(8,128)} custom-call(s32[3]{0:T(128)S(1)} %copy-done.3, bf16[16,28,16,128]{3,2,1,0:T(8,128)(2,1)} %all-to-all-done.refs_0_.refs_2_, bf16[16,28,16,128]{3,2,1,0:T(8,128)(2,1)} %collective-permute-done.6.refs_1_.refs_3_, bf16[32,7,16,128]{3,2,1,0:T(8,128)(2,1)S(1)} %all-to-all-done.2.refs_2_.refs_4_, ...), custom_call_target="tpu_custom_call" | custom-call | flops 12230590464 | bytes 7077888 | tf_op jit(solution)/shard_map/solve/pallas_call | solution.py:303
  134.0 0.0 copy-done.5
  134.0 0.0 collective-permute-done.7.refs_3_.refs_9_
  134.0 0.0 collective-permute-done.8.refs_5_.refs_11_
  134.0 15.3 %solve.4 = (f32[16,14,16,128]{3,2,1,0:T(8,128)}, bf16[16,14,16,128]{3,2,1,0:T(8,128)(2,1)S(1)}) custom-call(s32[3]{0:T(128)S(1)} %copy-done.3, bf16[16,28,16,128]{3,2,1,0:T(8,128)(2,1)} %all-to-all-done.refs_0_.refs_2_, bf16[16,28,16,128]{3,2,1,0:T(8,128)(2,1)} %collective-permute-done.6.refs_1_.refs_3_, bf16[32,7,16,128]{3,2,1,0:T(8,128)(2,1)S(1)} %copy-done.7, ...), custom_call_target="tpu_custom_call" | custom-call | flops 12230590464 | bytes 7077888 | tf_op jit(solution)/shard_map/solve/pallas_call | solution.py:303
  149.3 0.1 collective-permute-start.10
  149.4 0.0 all-to-all-done.3.refs_0_
  149.5 0.5 collective-permute-start.5
  149.9 2.1 collective-permute-done.10
  152.0 2.9 %add_convert_fusion = bf16[16,14,16,128]{3,2,1,0:T(8,128)(2,1)} fusion(f32[16,14,16,128]{3,2,1,0:T(8,128)} %get-tuple-element.46, bf16[16,14,16,128]{3,2,1,0:T(8,128)(2,1)} %collective-permute-done.10), kind=kLoop, calls=%fused_computation | loop fusion | flops 1376256 | bytes 3670016 | tf_op jit(solution)/shard_map/convert_element_type | solution.py:446
  154.9 8.1 %all-to-all-start.5 = ((bf16[16,14,16,128]{3,2,1,0:T(8,128)(2,1)}), bf16[16,14,16,128]{3,2,1,0:T(8,128)(2,1)S(1)}, u32[]{:S(2)}, u32[]{:S(2)}) async-start(bf16[16,14,16,128]{3,2,1,0:T(8,128)(2,1)} %add_convert_fusion), calls=%async_computation.5 | async-start | bytes 1835008 | tf_op jit(solution)/shard_map/all_to_all | solution.py:383
  163.0 0.0 collective-permute-done.5.refs_1_
  163.0 26.0 %solve.5 = (f32[16,14,16,128]{3,2,1,0:T(8,128)}, bf16[16,14,16,128]{3,2,1,0:T(8,128)(2,1)S(1)}) custom-call(s32[3]{0:T(128)S(1)} %copy-done.3, bf16[16,14,16,128]{3,2,1,0:T(8,128)(2,1)S(1)} %all-to-all-done.3.refs_0_, bf16[16,14,16,128]{3,2,1,0:T(8,128)(2,1)} %collective-permute-done.5.refs_1_, bf16[16,28,16,128]{3,2,1,0:T(8,128)(2,1)} %all-to-all-done.refs_0_.refs_2_, ...), custom_call_target="tpu_custom_call" | custom-call | flops 24461180928 | bytes 7077888 | tf_op jit(solution)/shard_map/solve/pallas_call | solution.py:303
  189.1 0.1 collective-permute-start.9
  189.2 2.5 %collective-permute-done.9 = bf16[16,14,16,128]{3,2,1,0:T(8,128)(2,1)S(1)} collective-permute-done((bf16[16,14,16,128]{3,2,1,0:T(8,128)(2,1)S(1)}, bf16[16,14,16,128]{3,2,1,0:T(8,128)(2,1)S(1)}, u32[]{:S(2)}, u32[]{:S(2)}) %collective-permute-start.9) | collective-permute-done | bytes 917536 | tf_op jit(solution)/shard_map/ppermute | solution.py:377
  191.6 2.6 %add_convert_fusion.1 = bf16[16,14,16,128]{3,2,1,0:T(8,128)(2,1)} fusion(f32[16,14,16,128]{3,2,1,0:T(8,128)} %get-tuple-element.44, bf16[16,14,16,128]{3,2,1,0:T(8,128)(2,1)S(1)} %collective-permute-done.9), kind=kLoop, calls=%fused_computation.1 | loop fusion | flops 1376256 | bytes 3670016 | tf_op jit(solution)/shard_map/convert_element_type | solution.py:446
  194.3 0.0 all-to-all-done.5.slabs_ref
  194.3 8.1 %all-to-all-start.4 = ((bf16[16,14,16,128]{3,2,1,0:T(8,128)(2,1)}), bf16[16,14,16,128]{3,2,1,0:T(8,128)(2,1)S(1)}, u32[]{:S(2)}, u32[]{:S(2)}) async-start(bf16[16,14,16,128]{3,2,1,0:T(8,128)(2,1)} %add_convert_fusion.1), calls=%async_computation.4 | async-start | bytes 1835008 | tf_op jit(solution)/shard_map/all_to_all | solution.py:383
  202.4 1.3 unpack.2.refs_0_
  203.7 23.4 %all-to-all-done.4.slabs_ref = bf16[16,14,16,128]{3,2,1,0:T(8,128)(2,1)S(1)} async-done(((bf16[16,14,16,128]{3,2,1,0:T(8,128)(2,1)}), bf16[16,14,16,128]{3,2,1,0:T(8,128)(2,1)S(1)}, u32[]{:S(2)}, u32[]{:S(2)}) %all-to-all-start.4) | async-done | bytes 917536 | tf_op jit(solution)/shard_map/all_to_all | solution.py:383
  227.1 1.3 unpack.3
  (6 shorter events, 0.0 us)
Async XLA Ops:
  2.0 10.3 %copy-start.10 = (s32[4]{0:T(128)S(1)}, s32[4]{0:T(128)}, u32[]{:S(2)}) copy-start(s32[4]{0:T(128)} %owners_ref.1) | copy-start | bytes 52
  4.7 26.4 %copy-start = (bf16[32,3,96,96]{3,2,1,0:T(8,128)(2,1)S(1)}, bf16[32,3,96,96]{3,2,1,0:T(8,128)(2,1)}, u32[]{:S(2)}) copy-start(bf16[32,3,96,96]{3,2,1,0:T(8,128)(2,1)} %orbitals_hbm.1) | copy-start | bytes 5308420
  4.7 26.4 %copy-start.2 = (s32[96,3,96]{2,0,1:T(8,128)S(1)}, s32[96,3,96]{2,0,1:T(8,128)}, u32[]{:S(2)}) copy-start(s32[96,3,96]{2,0,1:T(8,128)} %param.12) | copy-start | bytes 331780
  4.7 26.4 %copy-start.4 = (f32[128]{0:T(128)S(1)}, f32[128]{0:T(128)}, u32[]{:S(2)}) copy-start(f32[128]{0:T(128)} %param.13) | copy-start | bytes 1540
  4.7 15.8 %all-to-all-start.1 = ((bf16[8,2,7,16,128]{4,3,2,1,0:T(8,128)(2,1)}), bf16[8,2,7,16,128]{4,3,2,1,0:T(8,128)(2,1)S(1)}, u32[]{:S(2)}, u32[]{:S(2)}) async-start(bf16[8,2,7,16,128]{4,3,2,1,0:T(8,128)(2,1)} %own_pieces.1), calls=%async_computation.1 | async-start | bytes 917504 | tf_op jit(solution)/shard_map/all_to_all | solution.py:417
  21.6 35.4 %all-to-all-start.2 = ((bf16[32,7,16,128]{3,2,1,0:T(8,128)(2,1)}), bf16[32,7,16,128]{3,2,1,0:T(8,128)(2,1)S(1)}, u32[]{:S(2)}, u32[]{:S(2)}) async-start(bf16[32,7,16,128]{3,2,1,0:T(8,128)(2,1)} %bitcast.12), calls=%async_computation.2 | async-start | bytes 1835008 | tf_op jit(solution)/shard_map/all_to_all | solution.py:429
  33.0 1.2 copy-start.1
  57.0 47.2 %all-to-all-start = ((bf16[16,28,16,128]{3,2,1,0:T(8,128)(2,1)}), bf16[16,28,16,128]{3,2,1,0:T(8,128)(2,1)}, u32[]{:S(2)}, u32[]{:S(2)}) async-start(bf16[16,28,16,128]{3,2,1,0:T(8,128)(2,1)} %copy-done.1), calls=%async_computation | async-start | bytes 3670016 | tf_op jit(solution)/shard_map/all_to_all | solution.py:383
  61.4 57.9 %copy-start.3 = (s32[3]{0:T(128)S(1)}, s32[3]{0:T(128)}, u32[]{:S(2)}) copy-start(s32[3]{0:T(128)} %pad_add_fusion.place_ref) | copy-start | bytes 40
  61.4 57.9 %copy-start.8 = (bf16[256,256]{1,0:T(8,128)(2,1)S(1)}, bf16[256,256]{1,0:T(8,128)(2,1)}, u32[]{:S(2)}) copy-start(bf16[256,256]{1,0:T(8,128)(2,1)} %constant.50.clone.refs_7_.refs_13_) | copy-start | bytes 393220
  61.4 57.9 %copy-start.9 = (bf16[96,96]{1,0:T(8,128)(2,1)S(1)}, bf16[96,96]{1,0:T(8,128)(2,1)}, u32[]{:S(2)}) copy-start(bf16[96,96]{1,0:T(8,128)(2,1)} %constant.49.clone.refs_6_.refs_12_) | copy-start | bytes 55300
  61.4 22.7 %collective-permute-start.1 = (bf16[32,7,16,128]{3,2,1,0:T(8,128)(2,1)S(1)}, bf16[32,7,16,128]{3,2,1,0:T(8,128)(2,1)S(1)}, u32[]{:S(2)}, u32[]{:S(2)}) collective-permute-start(bf16[32,7,16,128]{3,2,1,0:T(8,128)(2,1)S(1)} %all-to-all-done.2.refs_2_.refs_4_), channel_id=1, source_target_pairs={{0,128},{1,129},{2,130},{3,131},{4,132},{5,133},{6,134},{7,135},{8... | collective-permute-start | bytes 2752520 | tf_op jit(solution)/shard_map/ppermute | solution.py:377
  62.2 27.4 %collective-permute-start = (bf16[32,7,16,128]{3,2,1,0:T(8,128)(2,1)S(1)}, bf16[32,7,16,128]{3,2,1,0:T(8,128)(2,1)}, u32[]{:S(2)}, u32[]{:S(2)}) collective-permute-start(bf16[32,7,16,128]{3,2,1,0:T(8,128)(2,1)S(1)} %all-to-all-done.2.refs_2_.refs_4_), channel_id=1, source_target_pairs={{0,48},{1,49},{2,50},{3,51},{4,52},{5,53},{6,54},{7,55},{8,56},{9,... | collective-permute-start | bytes 2752520 | tf_op jit(solution)/shard_map/ppermute | solution.py:377
  84.1 49.9 %copy-start.5 = (bf16[32,7,16,128]{3,2,1,0:T(8,128)(2,1)}, bf16[32,7,16,128]{3,2,1,0:T(8,128)(2,1)S(1)}, u32[]{:S(2)}) copy-start(bf16[32,7,16,128]{3,2,1,0:T(8,128)(2,1)S(1)} %collective-permute-done.1.refs_4_.refs_6_) | copy-start | bytes 2752516
  84.1 21.5 %collective-permute-start.3 = (bf16[32,7,16,128]{3,2,1,0:T(8,128)(2,1)S(1)}, bf16[32,7,16,128]{3,2,1,0:T(8,128)(2,1)S(1)}, u32[]{:S(2)}, u32[]{:S(2)}) collective-permute-start(bf16[32,7,16,128]{3,2,1,0:T(8,128)(2,1)S(1)} %all-to-all-done.2.refs_2_.refs_4_), channel_id=1, source_target_pairs={{0,64},{1,65},{2,66},{3,67},{4,68},{5,69},{6,70},{7,71},{8,72},{9,... | collective-permute-start | bytes 2752520 | tf_op jit(solution)/shard_map/ppermute | solution.py:377
  84.7 21.9 %collective-permute-start.4 = (bf16[32,7,16,128]{3,2,1,0:T(8,128)(2,1)S(1)}, bf16[32,7,16,128]{3,2,1,0:T(8,128)(2,1)}, u32[]{:S(2)}, u32[]{:S(2)}) collective-permute-start(bf16[32,7,16,128]{3,2,1,0:T(8,128)(2,1)S(1)} %all-to-all-done.2.refs_2_.refs_4_), channel_id=1, source_target_pairs={{0,192},{1,193},{2,194},{3,195},{4,196},{5,197},{6,198},{7,199},{8... | collective-permute-start | bytes 2752520 | tf_op jit(solution)/shard_map/ppermute | solution.py:377
  87.4 20.1 %collective-permute-start.2 = (bf16[32,7,16,128]{3,2,1,0:T(8,128)(2,1)S(1)}, bf16[32,7,16,128]{3,2,1,0:T(8,128)(2,1)}, u32[]{:S(2)}, u32[]{:S(2)}) collective-permute-start(bf16[32,7,16,128]{3,2,1,0:T(8,128)(2,1)S(1)} %collective-permute-done.1.refs_4_.refs_6_), channel_id=1, source_target_pairs={{0,48},{1,49},{2,50},{3,51},{4,52},{5,53},{6,54},{7,55},{8,56},{9,... | collective-permute-start | bytes 2752520 | tf_op jit(solution)/shard_map/ppermute | solution.py:377
  105.6 0.9 copy-start.6
  107.5 11.8 %collective-permute-start.6 = (bf16[16,28,16,128]{3,2,1,0:T(8,128)(2,1)}, bf16[16,28,16,128]{3,2,1,0:T(8,128)(2,1)}, u32[]{:S(2)}, u32[]{:S(2)}) collective-permute-start(bf16[16,28,16,128]{3,2,1,0:T(8,128)(2,1)} %all-to-all-done.refs_0_.refs_2_), channel_id=1, source_target_pairs={{0,1},{1,0},{2,3},{3,2},{4,5},{5,4},{6,7},{7,6},{8,9},{9,8},{10,11... | collective-permute-start | bytes 5505032 | tf_op jit(solution)/shard_map/ppermute | solution.py:377
  107.5 26.5 %collective-permute-start.7 = (bf16[32,7,16,128]{3,2,1,0:T(8,128)(2,1)}, bf16[32,7,16,128]{3,2,1,0:T(8,128)(2,1)}, u32[]{:S(2)}, u32[]{:S(2)}) collective-permute-start(bf16[32,7,16,128]{3,2,1,0:T(8,128)(2,1)} %collective-permute-done.refs_3_.refs_5_), channel_id=1, source_target_pairs={{0,64},{1,65},{2,66},{3,67},{4,68},{5,69},{6,70},{7,71},{8,72},{9,... | collective-permute-start | bytes 2752520 | tf_op jit(solution)/shard_map/ppermute | solution.py:377
  107.5 26.5 %collective-permute-start.8 = (bf16[32,7,16,128]{3,2,1,0:T(8,128)(2,1)}, bf16[32,7,16,128]{3,2,1,0:T(8,128)(2,1)}, u32[]{:S(2)}, u32[]{:S(2)}) collective-permute-start(bf16[32,7,16,128]{3,2,1,0:T(8,128)(2,1)} %collective-permute-done.refs_3_.refs_5_), channel_id=1, source_target_pairs={{0,192},{1,193},{2,194},{3,195},{4,196},{5,197},{6,198},{7,199},{8... | collective-permute-start | bytes 2752520 | tf_op jit(solution)/shard_map/ppermute | solution.py:377
  110.7 38.7 %all-to-all-start.3 = ((bf16[16,14,16,128]{3,2,1,0:T(8,128)(2,1)}), bf16[16,14,16,128]{3,2,1,0:T(8,128)(2,1)S(1)}, u32[]{:S(2)}, u32[]{:S(2)}) async-start(bf16[16,14,16,128]{3,2,1,0:T(8,128)(2,1)} %get-tuple-element.30), calls=%async_computation.3 | async-start | bytes 1835008 | tf_op jit(solution)/shard_map/all_to_all | solution.py:383
  119.3 14.8 %copy-start.7 = (bf16[32,7,16,128]{3,2,1,0:T(8,128)(2,1)S(1)}, bf16[32,7,16,128]{3,2,1,0:T(8,128)(2,1)}, u32[]{:S(2)}) copy-start(bf16[32,7,16,128]{3,2,1,0:T(8,128)(2,1)} %copy-done.6) | copy-start | bytes 2752516
  149.3 2.7 %collective-permute-start.10 = (bf16[16,14,16,128]{3,2,1,0:T(8,128)(2,1)S(1)}, bf16[16,14,16,128]{3,2,1,0:T(8,128)(2,1)}, u32[]{:S(2)}, u32[]{:S(2)}) collective-permute-start(bf16[16,14,16,128]{3,2,1,0:T(8,128)(2,1)S(1)} %get-tuple-element.35), channel_id=1, source_target_pairs={{0,1},{1,0},{2,3},{3,2},{4,5},{5,4},{6,7},{7,6},{8,9},{9,8},{10,11... | collective-permute-start | bytes 2752520 | tf_op jit(solution)/shard_map/ppermute | solution.py:377
  149.5 13.6 %collective-permute-start.5 = (bf16[16,14,16,128]{3,2,1,0:T(8,128)(2,1)S(1)}, bf16[16,14,16,128]{3,2,1,0:T(8,128)(2,1)}, u32[]{:S(2)}, u32[]{:S(2)}) collective-permute-start(bf16[16,14,16,128]{3,2,1,0:T(8,128)(2,1)S(1)} %all-to-all-done.3.refs_0_), channel_id=1, source_target_pairs={{0,1},{1,0},{2,3},{3,2},{4,5},{5,4},{6,7},{7,6},{8,9},{9,8},{10,11... | collective-permute-start | bytes 2752520 | tf_op jit(solution)/shard_map/ppermute | solution.py:377
  154.9 39.4 %all-to-all-start.5 = ((bf16[16,14,16,128]{3,2,1,0:T(8,128)(2,1)}), bf16[16,14,16,128]{3,2,1,0:T(8,128)(2,1)S(1)}, u32[]{:S(2)}, u32[]{:S(2)}) async-start(bf16[16,14,16,128]{3,2,1,0:T(8,128)(2,1)} %add_convert_fusion), calls=%async_computation.5 | async-start | bytes 1835008 | tf_op jit(solution)/shard_map/all_to_all | solution.py:383
  189.1 2.6 %collective-permute-start.9 = (bf16[16,14,16,128]{3,2,1,0:T(8,128)(2,1)S(1)}, bf16[16,14,16,128]{3,2,1,0:T(8,128)(2,1)S(1)}, u32[]{:S(2)}, u32[]{:S(2)}) collective-permute-start(bf16[16,14,16,128]{3,2,1,0:T(8,128)(2,1)S(1)} %get-tuple-element.45), channel_id=1, source_target_pairs={{0,1},{1,0},{2,3},{3,2},{4,5},{5,4},{6,7},{7,6},{8,9},{9,8},{10,11... | collective-permute-start | bytes 2752520 | tf_op jit(solution)/shard_map/ppermute | solution.py:377
  194.3 32.8 %all-to-all-start.4 = ((bf16[16,14,16,128]{3,2,1,0:T(8,128)(2,1)}), bf16[16,14,16,128]{3,2,1,0:T(8,128)(2,1)S(1)}, u32[]{:S(2)}, u32[]{:S(2)}) async-start(bf16[16,14,16,128]{3,2,1,0:T(8,128)(2,1)} %add_convert_fusion.1), calls=%async_computation.4 | async-start | bytes 1835008 | tf_op jit(solution)/shard_map/all_to_all | solution.py:383
